TPU v7x, 32 devices: a whole 2x2x4 slice. The times are simulated.
32 devices in a mesh: groups: 2 (over y), terms: 4 (over z), sector: 2 (over x), rep: 2 (over core).
Axes of the slice: x: 2, y: 2, z: 4, core: 2. Of those that a mesh axis runs over, the one named last changes fastest.
Arguments:
- psi_start: float32 [4, 256, 256], P(('groups', 'sector')), parts along dimension 0, may hold values from -6 to 6
- diagonal: float32 [4, 256, 256], P(('groups', 'sector')), parts along dimension 0, may hold values from 0.5 to 3
- sector_sizes: int32 [4, 2], P('groups'), parts along dimension 0, may hold values from 64 to 256, as said below
- conn: int32 [64, 2], P(('groups', 'terms', 'rep'), 'sector'), parts along dimension 0, may hold values from 0 to 1
- left_ops: float32 [64, 2, 256, 256], P(('groups', 'terms', 'rep'), 'sector'), parts along dimension 0, may hold values from -0.375 to 0.375
- right_ops: float32 [64, 2, 256, 256], P(('groups', 'terms', 'rep'), 'sector'), parts along dimension 0, may hold values from -0.0625 to 0.0625
Outputs:
- eigvector: float32 [4, 256, 256], P(('groups', 'sector')), parts along dimension 0
- energy: float32 [2], P('groups'), parts along dimension 0
There are 2 independent parts, one for each index of `groups`. A program takes and returns all parts, laid end to end along the dimension named above; each array names one. Nothing has to cross between parts.
Inputs may be any that keep to these rules, and one draw needn't show every extreme that they name: `sector_sizes`: both sizes of every sector lie in 64 to 256; some sector has both sizes equal to 256.
All inputs are finite; a program needn't handle non-finite values.
Results may differ from a plain program's by a relative error of at most 0.0003.
Values sent between devices are 32-bit elements; how exact they have to be, the bound alone decides.
No kernel may reach another device: no remote copies, remote signals or barrier semaphores. Data moves between devices by JAX's collectives and lax.ppermute only.
A program may use at most 64 MiB of HBM per device.

v0:
```python
import math

import jax
import jax.numpy as jnp
from jax import lax
from jax.sharding import PartitionSpec as P


def partial_sigma(full_vector, conn, left_ops, right_ops, own_first, coupling):
    precise = lax.Precision.HIGHEST
    term_dev, sec_dev, blk = (left_ops.shape[0], left_ops.shape[1], left_ops.shape[2])
    nsec = full_vector.shape[0]
    pairs = term_dev * sec_dev
    links = conn.reshape(pairs)
    source = full_vector[links]
    own = lax.dynamic_slice_in_dim(full_vector, own_first, sec_dev, 0)
    own = jnp.broadcast_to(own[None], (term_dev, sec_dev, blk, blk)).reshape(pairs, blk, blk)
    left_term = left_ops.reshape(pairs, blk, blk)
    right_term = right_ops.reshape(pairs, blk, blk)
    middle = jnp.einsum("pij,pjk->pik", left_term, source, precision=precise)
    joint = coupling * own + jnp.einsum("pik,plk->pil", middle, right_term, precision=precise)
    returned = jnp.einsum("pji,pjk->pik", left_term, joint, precision=precise)
    returned = jnp.einsum("pik,pkl->pil", returned, right_term, precision=precise)
    own_ids = own_first + jnp.tile(jnp.arange(sec_dev, dtype=jnp.int32), term_dev)
    targets = jnp.concatenate([own_ids, links])
    onehot = (targets[None, :] == jnp.arange(nsec, dtype=jnp.int32)[:, None]).astype(jnp.float32)
    values = jnp.concatenate([coupling * joint, returned]).reshape(2 * pairs, blk * blk)
    return jnp.dot(onehot, values, precision=precise).reshape(nsec, blk, blk)


def davidson(trial, diagonal, apply, inner_sums):
    (trial_norm,) = inner_sums(((trial, trial),))
    trial = trial / jnp.sqrt(trial_norm)
    image = apply(trial)
    (theta,) = inner_sums(((trial, image),))
    residue = image - theta * trial
    shifted = diagonal - theta
    fresh = residue * shifted / (shifted * shifted + 1.0)
    (correlation,) = inner_sums(((trial, fresh),))
    fresh = fresh - correlation * trial
    (length,) = inner_sums(((fresh, fresh),))
    fresh = fresh / jnp.sqrt(length)
    fresh_image = apply(fresh)
    cross, corner = inner_sums(((trial, fresh_image), (fresh, fresh_image)))
    spread = (theta - corner) / 2.0
    lowest = (theta + corner) / 2.0 - jnp.sqrt(spread * spread + cross * cross)
    keep = corner - lowest
    turn = -cross
    length = jnp.sqrt(keep * keep + turn * turn)
    keep = keep / length
    turn = turn / length
    trial = keep * trial + turn * fresh
    return (trial, lowest)


def body(psi_start, diagonal, sector_sizes, conn, left_ops, right_ops):
    sec_dev, blk = (psi_start.shape[0], psi_start.shape[1])
    n_sector = lax.axis_size("sector")
    nsec = sec_dev * n_sector
    nterm = conn.shape[0] * lax.axis_size(("terms", "rep"))
    coupling = 1.0 / math.sqrt(nterm)
    ncell = float(nsec * blk * blk)
    own_first = lax.axis_index("sector") * sec_dev
    row_ids = jnp.arange(blk, dtype=jnp.int32)
    live_full = (
        (row_ids[None, :, None] < sector_sizes[:, 0][:, None, None])
        & (row_ids[None, None, :] < sector_sizes[:, 1][:, None, None])
    ).astype(jnp.float32)

    def sigma_terms(full_vector):
        return partial_sigma(full_vector, conn, left_ops, right_ops, own_first, coupling)

    full_start, full_diag = (
        lax.all_gather(psi_start, "sector", axis=0, tiled=True),
        lax.all_gather(diagonal, "sector", axis=0, tiled=True),
    )

    def apply_whole(vector):
        reduced = lax.psum(sigma_terms(vector), ("terms", "sector", "rep"))
        return live_full * (full_diag * vector + reduced)

    def local_sums(pairs_list):
        stacked = jnp.stack([jnp.sum(first * second) / ncell for first, second in pairs_list])
        return tuple((stacked[index] for index in range(len(pairs_list))))

    trial, theta = davidson(live_full * full_start, full_diag, apply_whole, local_sums)
    eigvector = lax.dynamic_slice_in_dim(trial, own_first, sec_dev, 0)
    return (eigvector, jnp.reshape(theta, (1,)))


def solution(mesh):
    in_specs = (
        P(("groups", "sector"), None, None),
        P(("groups", "sector"), None, None),
        P("groups", None),
        P(("groups", "terms", "rep"), "sector"),
        P(("groups", "terms", "rep"), "sector", None, None),
        P(("groups", "terms", "rep"), "sector", None, None),
    )
    out_specs = (P(("groups", "sector"), None, None), P("groups"))
    return jax.shard_map(body, mesh=mesh, in_specs=in_specs, out_specs=out_specs, check_vma=False)
```

profile of v0, /device:TPU:0, one launch (start us, length us, event | category | flops | bytes accessed | tf_op | source)
XLA Modules:
  0.0 262.5 jit_solution(12790228688396361047)
XLA Ops:
  7.2 0.0 copy-start
  7.2 0.0 all-reduce.4.cloned.1.call-start
  7.2 0.7 fusion.18
  8.0 0.7 concatenate.10
  8.7 1.0 slice_reduce_fusion.1
  9.7 0.1 iota_compare_fusion.1
  9.8 10.2 %all_gather.7 = f32[2,256,256]{2,1,0:T(8,128)S(1)} all-gather(f32[1,256,256]{2,1,0:T(8,128)} %param.6), channel_id=1, replica_groups=mesh['groups'=2,'terms'=4,'sector'=2,'rep'=2] {'sector'}, dimensions={0}, use_global_device_ids=true | all-gather | bytes 786432 | tf_op jit(solution)/shard_map/all_gather | solution.py:74
  20.0 1.9 multiply_reduce_fusion.5
  22.5 1.1 broadcast_divide_fusion.1
  23.6 0.0 copy-start.4
  23.6 0.8 copy-done.4
  24.5 1.5 dynamic-slice_multiply_fusion.1
  26.0 1.6 gather_fusion
  27.6 0.0 copy-done.1
  27.6 2.4 fusion.12
  30.0 0.0 copy-done
  30.0 1.2 broadcast_multiply_fusion.1
  31.2 1.9 fusion.10
  33.1 1.1 fusion.3
  34.2 0.1 maximum_bitcast_fusion
  34.4 0.0 copy-start.6
  34.4 3.0 %fusion.16 = f32[2,256,256]{2,0,1:T(2,128)} fusion(s32[8]{0:T(128)S(1)} %concatenate.10, f32[1,8,256,256]{3,2,1,0:T(8,128)S(1)} %maximum_bitcast_fusion), kind=kOutput, calls=%fused_computation.46 | convolution fusion | flops 12582928 | bytes 2621472 | tf_op jit(solution)/shard_map/dot_general | solution.py:28
  37.4 0.0 all-reduce.4.cloned.1.call-update
  37.4 0.0 all-reduce.6.cloned.1.call-start
  37.5 0.0 copy-done.6
  37.5 8.3 %all_gather.6 = f32[2,256,256]{2,1,0:T(8,128)S(1)} all-gather(f32[1,256,256]{2,1,0:T(8,128)S(1)} %copy-done.6), channel_id=1, replica_groups=mesh['groups'=2,'terms'=4,'sector'=2,'rep'=2] {'sector'}, dimensions={0}, use_global_device_ids=true | all-gather | bytes 786432 | tf_op jit(solution)/shard_map/all_gather | solution.py:75
  45.8 83.2 %all-reduce.4.cloned.1.call-done = f32[2,256,256]{2,0,1:T(2,128)} async-done(((f32[2,256,256]{2,0,1:T(2,128)}), f32[2,256,256]{2,0,1:T(2,128)}) %all-reduce.4.cloned.1.call-update) | async-done | bytes 524304 | tf_op jit(solution)/shard_map/psum | solution.py:79
  129.1 3.1 %multiply_reduce_fusion.4 = f32[]{:T(128)} fusion(f32[2,256,256]{2,0,1:T(2,128)} %all-reduce.4.cloned.1.call-done, pred[2,256]{1,0:T(4,128)(4,1)S(1)} %iota_compare_fusion.1, pred[2,256]{0,1:T(8,128)(4,1)S(1)} %iota_compare_fusion, f32[2,256,256]{2,1,0:T(8,128)S(1)} %all_gather.6, f32[]{:T(128)S(6)} %sqrt.12, f32[2,256,256]{2,1,0:T(8,128)S(1)} %all_gather.7), kind=kLoop, calls=%fused_computation.29 | loop fusion | flops 1048575 | bytes 1573896 | tf_op jit(solution)/shard_map/reduce_sum | solution.py:83
  132.8 3.9 %multiply_reduce_fusion.3 = (f32[]{:T(128)}, f32[2,256,256]{2,0,1:T(2,128)}) fusion(f32[]{:T(128)S(6)} %div.46, f32[2,256,256]{2,0,1:T(2,128)} %all-reduce.4.cloned.1.call-done, f32[2,256,256]{2,1,0:T(8,128)S(1)} %all_gather.6, pred[2,256]{1,0:T(4,128)(4,1)S(1)} %iota_compare_fusion.1, pred[2,256]{0,1:T(8,128)(4,1)S(1)} %iota_compare_fusion, f32[]{:T(128)S(6)} %sqrt.12, ...), kind=kLoop, calls=%fused_computation.27 | loop fusion | flops 1966079 | bytes 2098188 | tf_op jit(solution)/shard_map/reduce_sum | solution.py:83
  137.4 2.9 %multiply_reduce_fusion.2 = f32[]{:T(128)} fusion(f32[2,256,256]{2,0,1:T(2,128)} %get-tuple-element.13, f32[]{:T(128)S(6)} %div.48, f32[]{:T(128)S(6)} %sqrt.12, f32[2,256,256]{2,1,0:T(8,128)S(1)} %all_gather.7, pred[2,256]{1,0:T(4,128)(4,1)S(1)} %iota_compare_fusion.1, pred[2,256]{0,1:T(8,128)(4,1)S(1)} %iota_compare_fusion), kind=kLoop, calls=%fused_computation.25 | loop fusion | flops 917503 | bytes 1049612 | tf_op jit(solution)/shard_map/reduce_sum | solution.py:83
  140.2 0.0 copy-done.2
  140.9 2.0 broadcast_divide_fusion
  143.0 0.4 dynamic-slice_multiply_fusion
  143.4 0.8 copy.25
  144.2 2.6 %gather_fusion.1 = f32[4,256,256]{2,1,0:T(8,128)} fusion(f32[2,256,256]{2,1,0:T(8,128)} %copy.25, s32[1024]{0:T(1024)S(1)} %pad_clamp_fusion), kind=kCustom, calls=%fused_computation.1 | custom fusion | bytes 2097168 | tf_op jit(solution)/shard_map/gather | solution.py:15
  146.9 2.4 fusion.8
  149.2 1.2 broadcast_multiply_fusion
  150.4 1.9 fusion.6
  152.3 1.1 fusion
  153.5 0.1 maximum_bitcast_fusion.1
  153.6 0.0 copy-start.3
  153.6 0.0 copy-start.5
  153.6 3.0 %fusion.14 = f32[2,256,256]{2,0,1:T(2,128)} fusion(s32[8]{0:T(128)S(1)} %concatenate.10, f32[1,8,256,256]{3,2,1,0:T(8,128)S(1)} %maximum_bitcast_fusion.1), kind=kOutput, calls=%fused_computation.44 | convolution fusion | flops 12582928 | bytes 2621472 | tf_op jit(solution)/shard_map/dot_general | solution.py:28
  156.6 0.0 all-reduce.6.cloned.1.call-update
  156.7 90.6 %all-reduce.6.cloned.1.call-done = f32[2,256,256]{2,0,1:T(2,128)} async-done(((f32[2,256,256]{2,0,1:T(2,128)}), f32[2,256,256]{2,0,1:T(2,128)}) %all-reduce.6.cloned.1.call-update) | async-done | bytes 524304 | tf_op jit(solution)/shard_map/psum | solution.py:79
  247.3 3.2 %multiply_reduce_fusion.1 = (f32[]{:T(128)}, f32[]{:T(128)}) fusion(f32[2,256,256]{2,0,1:T(2,128)S(1)} %broadcast_divide_fusion, f32[2,256,256]{2,0,1:T(2,128)} %all-reduce.6.cloned.1.call-done, f32[2,256,256]{2,1,0:T(8,128)S(1)} %copy-done.3, pred[2,256]{1,0:T(4,128)(4,1)S(1)} %iota_compare_fusion.1, pred[2,256]{0,1:T(8,128)(4,1)S(1)} %iota_compare_fusion, ...), kind=kLoop, calls=%fused_computation.24 | loop fusion | flops 1310718 | bytes 2098188 | tf_op jit(solution)/shard_map/reduce_sum | solution.py:83
  253.3 0.5 multiply_add_fusion
  253.8 0.7 copy.30
  (9 shorter events, 0.1 us)
Async XLA Ops:
  7.2 22.8 %copy-start = (f32[4,1,256,256]{3,2,1,0:T(8,128)S(1)}, f32[4,1,256,256]{3,2,1,0:T(8,128)}, u32[]{:S(2)}) copy-start(f32[4,1,256,256]{3,2,1,0:T(8,128)} %param.11) | copy-start | bytes 3145732
  7.2 121.9 %all-reduce.4.cloned.1.call-start = ((), (), s32[]{:S(2)}) async-start(), calls=%async_computation | async-start | bytes 1048576 | tf_op jit(solution)/shard_map/psum | solution.py:79
  23.6 0.8 copy-start.4
  24.4 3.2 %copy-start.1 = (f32[4,1,256,256]{3,2,1,0:T(8,128)S(1)}, f32[4,1,256,256]{3,2,1,0:T(8,128)}, u32[]{:S(2)}) copy-start(f32[4,1,256,256]{3,2,1,0:T(8,128)} %param.10) | copy-start | bytes 3145732
  34.4 3.1 %copy-start.6 = (f32[1,256,256]{2,1,0:T(8,128)S(1)}, f32[1,256,256]{2,1,0:T(8,128)}, u32[]{:S(2)}) copy-start(f32[1,256,256]{2,1,0:T(8,128)} %param.7) | copy-start | bytes 786436
  37.4 209.9 %all-reduce.6.cloned.1.call-start = ((), (), s32[]{:S(2)}) async-start(), calls=%async_computation.1 | async-start | bytes 1048576 | tf_op jit(solution)/shard_map/psum | solution.py:79
  45.8 94.4 %copy-start.2 = (f32[2,256,256]{2,1,0:T(8,128)}, f32[2,256,256]{2,1,0:T(8,128)S(1)}, u32[]{:S(2)}) copy-start(f32[2,256,256]{2,1,0:T(8,128)S(1)} %all_gather.6) | copy-start | bytes 1572868
  153.6 93.6 %copy-start.3 = (f32[2,256,256]{2,1,0:T(8,128)S(1)}, f32[2,256,256]{2,1,0:T(8,128)}, u32[]{:S(2)}) copy-start(f32[2,256,256]{2,1,0:T(8,128)} %copy-done.2) | copy-start | bytes 1572868
  153.6 99.6 %copy-start.5 = (f32[2,256,256]{2,0,1:T(2,128)S(1)}, f32[2,256,256]{2,0,1:T(2,128)}, u32[]{:S(2)}) copy-start(f32[2,256,256]{2,0,1:T(2,128)} %copy-done.4) | copy-start | bytes 1572868
Sparse Core Ops, SparseCore 0:
  37.5 91.4 all-reduce.3
  156.8 90.4 all-reduce.5
where the time goes:
time: 263 us; the launch traced here: 262 us
  waiting for transfers between devices  174 us (66%)
  other arithmetic  21.5 us (8%)
  between operations  20.8 us (8%)
  matrix products  19.2 us (7%)
  blocking collectives  18.5 us (7%)
  local copies, waits for them, and re-layouts  8.41 us (3%)
    psum x2, waiting for transfers between devices, apply_whole(): reduced = lax.psum(sigma_terms(vector), ('terms', 'sector', 'rep'))  174 us
    reduce_sum x5, other arithmetic, local_sums(): jnp.sum(first * second) / ncell  15 us
    all_gather x1, blocking collectives, body(): lax.all_gather(psi_start, 'sector', axis=0, tiled=True)  10.2 us
    all_gather x1, blocking collectives, body(): lax.all_gather(diagonal, 'sector', axis=0, tiled=True)  8.35 us
    dot_general x2, matrix products, partial_sigma(): return jnp.dot(onehot, values, precision=precise).reshape(nsec, blk, blk)  6.01 us
  transfers between devices with their start and end apart: 2, of which 2 were waited for; matrix products, arithmetic and copies ran while one was open for 0% of the time, Pallas kernels for 0%

commit v1 on v0

v1 whole, which is shorter than its diff:
```python
import functools
import math

import jax
import jax.numpy as jnp
from jax import lax
from jax.experimental import pallas as pl
from jax.experimental.pallas import tpu as pltpu
from jax.sharding import PartitionSpec as P

F32 = jnp.float32
BF16 = jnp.bfloat16
PAD = 8
PARAMS = pltpu.CompilerParams(vmem_limit_bytes=40 * 1024 * 1024)
NN = (((1,), (0,)), ((), ()))
NT = (((1,), (1,)), ((), ()))
TN = (((0,), (0,)), ((), ()))


def split(x):
    high = x.astype(BF16)
    return high, (x - high.astype(F32)).astype(BF16)


def product(a, b, dims):
    dot = functools.partial(lax.dot_general, dimension_numbers=dims, preferred_element_type=F32)
    return dot(a[0], b[0]) + (dot(a[0], b[1]) + dot(a[1], b[0]))


def live_mask(sizes_ref, sector, rows, cols, first=0):
    row = lax.broadcasted_iota(jnp.int32, (rows, cols), 0) + first
    col = lax.broadcasted_iota(jnp.int32, (rows, cols), 1)
    return (row < sizes_ref[sector, 0]) & (col < sizes_ref[sector, 1])


def total(x):
    return jnp.sum(x, keepdims=True)


def image_kernel(coupling, weight, where_ref, sizes_ref, conn_ref, *refs):
    nsec = sizes_ref.shape[0]
    psi_ref, diag_ref = refs[:2]
    halves = refs[2 : 2 + 2 * (nsec - 1)]
    left_ref, right_ref, keep_ref, send_ref, full_ref, acc, high, low = refs[2 + 2 * (nsec - 1) :]
    blk = psi_ref.shape[0]
    half = blk // 2
    nterm = left_ref.shape[0]
    me, core = where_ref[0], where_ref[1]
    mine = pl.ds(pl.multiple_of(core * half, half), half)
    other = pl.ds(pl.multiple_of((1 - core) * half, half), half)
    full_ref[0] = psi_ref[...]
    for slot in range(1, nsec):
        full_ref[slot, mine, :] = halves[2 * slot - 2][...]
        full_ref[slot, other, :] = halves[2 * slot - 1][...]
    for slot in range(nsec):
        value = jnp.where(live_mask(sizes_ref, me ^ slot, blk, blk), full_ref[slot], 0.0)
        full_ref[slot] = value
        high[slot], low[slot] = split(value)
        acc[slot] = jnp.zeros((blk, blk), F32)
    own = full_ref[0]
    scalar = total(own * own * diag_ref[...]) * weight
    slots = [conn_ref[term, 0] ^ me for term in range(nterm)]
    lefts = [split(left_ref[term]) for term in range(nterm)]
    rights = [split(right_ref[term]) for term in range(nterm)]
    middles = [product(lefts[i], (high[slots[i]], low[slots[i]]), NN) for i in range(nterm)]
    joints = [coupling * own + product(split(middles[i]), rights[i], NT) for i in range(nterm)]
    for joint in joints:
        scalar = scalar + total(joint * joint)
    acc[0] = coupling * sum(joints[1:], joints[0])
    inner = [product(split(joints[i]), rights[i], NN) for i in range(nterm)]
    for i in range(nterm):
        acc[slots[i]] += product(lefts[i], split(inner[i]), TN)
    for slot in range(nsec):
        keep_ref[slot, :half, :] = acc[slot, mine, :]
        send_ref[slot, :half, :] = acc[slot, other, :]
        keep_ref[slot, half:, :] = jnp.broadcast_to(scalar, (PAD, blk))
        send_ref[slot, half:, :] = jnp.broadcast_to(scalar, (PAD, blk))


def fresh_kernel(ncell, nparts, where_ref, sizes_ref, *refs):
    parts = refs[:nparts]
    full_ref, diag_ref, fresh_ref, cross_ref = refs[nparts:]
    blk = full_ref.shape[-1]
    half = blk // 2
    me, core = where_ref[0], where_ref[1]
    first = pl.multiple_of(core * half, half)
    norm = total(full_ref[...] * full_ref[...]).reshape(1, 1) / ncell
    scale = 1.0 / jnp.sqrt(norm)
    summed = parts[0][...]
    for part in parts[1:]:
        summed = summed + part[...]
    theta = summed[half : half + 1, :1] / (ncell * norm)
    trial = full_ref[0, pl.ds(first, half), :] * scale
    diag = diag_ref[pl.ds(first, half), :]
    image = jnp.where(live_mask(sizes_ref, me, half, blk, first), diag * trial + summed[:half] * scale, 0.0)
    residue = image - theta * trial
    shifted = diag - theta
    fresh = residue * shifted / (shifted * shifted + 1.0)
    fresh_ref[...] = fresh
    row = lax.broadcasted_iota(jnp.int32, cross_ref.shape, 0)
    cross_ref[...] = jnp.where(row == 0, total(residue * fresh), theta)


def corner_kernel(coupling, weight, ncell, share, where_ref, conn_ref, *refs):
    full_ref = refs[0]
    nsec = full_ref.shape[0]
    halves = refs[1 : 1 + 2 * nsec]
    diag_ref, left_ref, right_ref, cross_ref, sums_ref, fresh_ref, info_ref, work, high, low = refs[1 + 2 * nsec :]
    blk = diag_ref.shape[0]
    half = blk // 2
    nterm = left_ref.shape[0]
    me, core = where_ref[0], where_ref[1]
    mine = pl.ds(pl.multiple_of(core * half, half), half)
    other = pl.ds(pl.multiple_of((1 - core) * half, half), half)
    for slot in range(nsec):
        work[slot, mine, :] = halves[2 * slot][...]
        work[slot, other, :] = halves[2 * slot + 1][...]
    start = full_ref[...]
    raw = work[...]
    norm = total(start * start).reshape(1, 1) / ncell
    overlap = total(start * raw).reshape(1, 1) / ncell
    fresh = raw - (overlap / norm)[None] * start
    length = total(fresh * fresh).reshape(1, 1) / ncell
    for slot in range(nsec):
        high[slot], low[slot] = split(fresh[slot])
    own = fresh[0]
    fresh_ref[...] = own
    scalar = total(own * own * diag_ref[...]) * weight
    slots = [conn_ref[term, 0] ^ me for term in range(nterm)]
    middles = [product(split(left_ref[i]), (high[slots[i]], low[slots[i]]), NN) for i in range(nterm)]
    joints = [coupling * own + product(split(middles[i]), split(right_ref[i]), NT) for i in range(nterm)]
    for joint in joints:
        scalar = scalar + total(joint * joint)
    row = lax.broadcasted_iota(jnp.int32, sums_ref.shape, 0)
    cross = cross_ref[...][:1, :1] * share
    sums_ref[...] = jnp.where(row == 0, scalar, cross)
    info_ref[...] = jnp.where(row == 0, norm, jnp.where(row == 1, length, cross_ref[...][1:2, :1]))


def result_kernel(ncell, sums_ref, info_ref, full_ref, fresh_ref, vector_ref, energy_ref):
    sums, info = sums_ref[...], info_ref[...]
    norm, length, theta = info[0:1, :1], info[1:2, :1], info[2:3, :1]
    corner = sums[0:1, :1] / (ncell * length)
    cross = sums[1:2, :1] / (ncell * jnp.sqrt(length))
    spread = (theta - corner) / 2.0
    lowest = (theta + corner) / 2.0 - jnp.sqrt(spread * spread + cross * cross)
    keep = corner - lowest
    turn = -cross
    size = jnp.sqrt(keep * keep + turn * turn)
    keep = keep / size
    turn = turn / size
    vector_ref[0] = (keep / jnp.sqrt(norm)) * full_ref[0] + (turn / jnp.sqrt(length)) * fresh_ref[...]
    energy_ref[...] = jnp.broadcast_to(lowest, energy_ref.shape)


def across(x, axis, step):
    size = lax.axis_size(axis)
    return lax.ppermute(x, axis, [(i, i ^ step) for i in range(size)])


def body(psi_start, diagonal, sector_sizes, conn, left_ops, right_ops):
    blk = psi_start.shape[-1]
    half = blk // 2
    nterm_dev = conn.shape[0]
    nsec, nz, nrep = lax.axis_size("sector"), lax.axis_size("terms"), lax.axis_size("rep")
    coupling = 1.0 / math.sqrt(nterm_dev * nz * nrep)
    ncell = float(nsec * blk * blk)
    me, core = lax.axis_index("sector"), lax.axis_index("rep")
    where = jnp.stack([me, core]).astype(jnp.int32)
    psi, diag = psi_start[0], diagonal[0]
    left, right = left_ops[:, 0], right_ops[:, 0]
    vmem, smem = pl.BlockSpec(memory_space=pltpu.VMEM), pl.BlockSpec(memory_space=pltpu.SMEM)

    mine = lax.dynamic_slice_in_dim(psi, core * half, half, 0)
    halves = []
    for step in range(1, nsec):
        near = across(mine, "sector", step)
        halves += [near, across(near, "rep", 1)]
    keep, send, full = pl.pallas_call(
        functools.partial(image_kernel, coupling, 1.0 / (nz * nrep)),
        out_shape=[
            jax.ShapeDtypeStruct((nsec, half + PAD, blk), F32),
            jax.ShapeDtypeStruct((nsec, half + PAD, blk), F32),
            jax.ShapeDtypeStruct((nsec, blk, blk), F32),
        ],
        in_specs=[smem] * 3 + [vmem] * (len(halves) + 4),
        out_specs=[vmem] * 3,
        scratch_shapes=[
            pltpu.VMEM((nsec, blk, blk), F32),
            pltpu.VMEM((nsec, blk, blk), BF16),
            pltpu.VMEM((nsec, blk, blk), BF16),
        ],
        compiler_params=PARAMS,
        name="image",
    )(where, sector_sizes, conn, psi, diag, *halves, left, right)

    chip = keep + across(send, "rep", 1)
    part = chip[0]
    for step in range(1, nsec):
        part = part + across(chip[step], "sector", step)
    parts = [part] + [across(part, "terms", step) for step in range(1, nz)]
    fresh, cross = pl.pallas_call(
        functools.partial(fresh_kernel, ncell, nz),
        out_shape=[jax.ShapeDtypeStruct((half, blk), F32), jax.ShapeDtypeStruct((8, 128), F32)],
        in_specs=[smem] * 2 + [vmem] * (nz + 2),
        out_specs=[vmem] * 2,
        compiler_params=PARAMS,
        name="fresh",
    )(where, sector_sizes, *parts, full, diag)

    halves = []
    for step in range(nsec):
        near = across(fresh, "sector", step) if step else fresh
        halves += [near, across(near, "rep", 1)]
    sums, direction, info = pl.pallas_call(
        functools.partial(corner_kernel, coupling, 1.0 / (nz * nrep), ncell, 1.0 / nz),
        out_shape=[
            jax.ShapeDtypeStruct((8, 128), F32),
            jax.ShapeDtypeStruct((blk, blk), F32),
            jax.ShapeDtypeStruct((8, 128), F32),
        ],
        in_specs=[smem] * 2 + [vmem] * (len(halves) + 5),
        out_specs=[vmem] * 3,
        scratch_shapes=[
            pltpu.VMEM((nsec, blk, blk), F32),
            pltpu.VMEM((nsec, blk, blk), BF16),
            pltpu.VMEM((nsec, blk, blk), BF16),
        ],
        compiler_params=PARAMS,
        name="corner",
    )(where, conn, full, *halves, diag, left, right, cross)

    for axis in ("rep", "sector", "terms"):
        step = 1
        while step < lax.axis_size(axis):
            sums = sums + across(sums, axis, step)
            step *= 2
    vector, energy = pl.pallas_call(
        functools.partial(result_kernel, ncell),
        out_shape=[jax.ShapeDtypeStruct((1, blk, blk), F32), jax.ShapeDtypeStruct((8, 128), F32)],
        in_specs=[vmem] * 4,
        out_specs=[vmem] * 2,
        compiler_params=PARAMS,
        name="result",
    )(sums, info, full, direction)
    return vector, energy[0, :1]


def solution(mesh):
    in_specs = (
        P(("groups", "sector"), None, None),
        P(("groups", "sector"), None, None),
        P("groups", None),
        P(("groups", "terms", "rep"), "sector"),
        P(("groups", "terms", "rep"), "sector", None, None),
        P(("groups", "terms", "rep"), "sector", None, None),
    )
    out_specs = (P(("groups", "sector"), None, None), P("groups"))
    return jax.shard_map(body, mesh=mesh, in_specs=in_specs, out_specs=out_specs, check_vma=False)
```

time: 263 us -> 63.2 us (0.24)
  waiting for transfers between devices: 174 us -> 35.1 us
  other arithmetic: 21.5 us -> 0.14 us
  between operations: 20.8 us -> 0.72 us
  matrix products: 19.2 us -> 0 us
  blocking collectives: 18.5 us -> 0 us
  starting transfers between devices: 0.08 us -> 13.9 us
  Pallas kernels: 0 us -> 6.81 us
    psum x2 -> x0, waiting for transfers between devices: 174 us -> none  [apply_whole(): reduced = lax.psum(sigma_terms(vector), ('terms', 'sector', 'rep'))]
    ppermute x0 -> x14, waiting for transfers between devices: none -> 35.1 us  [across(): return lax.ppermute(x, axis, [(i, i ^ step) for i in range(size)])]
    dot_general x10 -> x0, matrix products: 19.2 us -> none  [the longest x2 6.01 us: partial_sigma(): return jnp.dot(onehot, values, precision=precise).reshape(nsec, blk, blk)]
    all_gather x2 -> x0, blocking collectives: 18.5 us -> none  [the longest x1 10.2 us: body(): lax.all_gather(psi_start, 'sector', axis=0, tiled=True)]
    reduce_sum x5 -> x0, other arithmetic: 15 us -> none  [local_sums(): jnp.sum(first * second) / ncell]
    ppermute x0 -> x14, starting transfers between devices: none -> 13.9 us  [across(): return lax.ppermute(x, axis, [(i, i ^ step) for i in range(size)])]
    pallas_call x0 -> x4, Pallas kernels: none -> 6.81 us  [the longest x1 2.73 us: body(): pl.pallas_call(functools.partial(image_kernel, coupling, 1.0 / (nz * nrep...]
    gather x2 -> x0, local copies, waits for them, and re-layouts: 4.25 us -> none  [partial_sigma(): source = full_vector[links]]
  transfers between devices with their start and end apart: 2 -> 14, of which waited for: 2 -> 12; matrix products, arithmetic and copies ran while one was open for 0% -> 0% of each run, Pallas kernels for 0% -> 0%
where the time goes in v1:
time: 63.2 us; the launch traced here: 62.9 us
  waiting for transfers between devices  35.1 us (56%)
  starting transfers between devices  13.9 us (22%)
  Pallas kernels  6.81 us (11%)
  local copies, waits for them, and re-layouts  6.32 us (10%)
  between operations  0.72 us (1%)
    ppermute x14, waiting for transfers between devices, across(): return lax.ppermute(x, axis, [(i, i ^ step) for i in range(size)])  35.1 us
    ppermute x14, starting transfers between devices, across(): return lax.ppermute(x, axis, [(i, i ^ step) for i in range(size)])  13.9 us
    unnamed x17, local copies, waits for them, and re-layouts  4.84 us
    pallas_call x1, Pallas kernels, body(): pl.pallas_call(functools.partial(image_kernel, coupling, 1.0 / (nz * nrep...  2.73 us
    pallas_call x1, Pallas kernels, body(): pl.pallas_call(functools.partial(corner_kernel, coupling, 1.0 / (nz * nre...  2.19 us
  transfers between devices with their start and end apart: 14, of which 12 were waited for; matrix products, arithmetic and copies ran while one was open for 0% of the time, Pallas kernels for 0%

profile of v1, /device:TPU:0, one launch (start us, length us, event | category | flops | bytes accessed | tf_op | source)
XLA Modules:
  0.0 62.9 jit_solution(6267724041801878977)
XLA Ops:
  0.6 0.0 copy-start.4
  0.6 1.0 %dynamic-slice_bitcast_fusion = f32[128,256]{1,0:T(8,128)S(1)} fusion(f32[1,256,256]{2,1,0:T(8,128)} %param.6, s32[]{:T(128)S(6)} %select_n.3), kind=kLoop, calls=%fused_computation.3 | loop fusion | bytes 262148 | tf_op jit(solution)/shard_map/dynamic_slice | solution.py:174
  1.6 3.0 %collective-permute-start = (f32[128,256]{1,0:T(8,128)S(1)}, f32[128,256]{1,0:T(8,128)S(1)}, u32[]{:S(2)}, u32[]{:S(2)}) collective-permute-start(f32[128,256]{1,0:T(8,128)S(1)} %dynamic-slice_bitcast_fusion), channel_id=1, source_target_pairs={{0,2},{2,0},{1,3},{3,1},{4,6},{6,4},{5,7},{7,5},{8,10},{10,8},{9,1... | collective-permute-start | bytes 393224 | tf_op jit(solution)/shard_map/ppermute | solution.py:158
  4.6 3.5 %collective-permute-done.refs_2_ = f32[128,256]{1,0:T(8,128)S(1)} collective-permute-done((f32[128,256]{1,0:T(8,128)S(1)}, f32[128,256]{1,0:T(8,128)S(1)}, u32[]{:S(2)}, u32[]{:S(2)}) %collective-permute-start) | collective-permute-done | bytes 131104 | tf_op jit(solution)/shard_map/ppermute | solution.py:158
  8.1 0.0 collective-permute-start.1
  8.1 0.0 copy-start.7
  8.1 0.7 %copy-done.7 = s32[4,1]{0,1:T(1,128)S(1)} copy-done((s32[4,1]{0,1:T(1,128)S(1)}, s32[4,1]{0,1:T(1,128)}, u32[]{:S(2)}) %copy-start.7) | copy-done | bytes 40
  8.8 0.1 copy.9.conn_ref
  8.9 0.1 pad_add_fusion.where_ref
  8.9 0.5 collective-permute-done.1.refs_3_
  9.5 0.0 copy-start.6
  9.5 0.0 copy-done.4
  9.5 0.7 %copy-done.6 = s32[2,2]{1,0:T(2,128)S(1)} copy-done((s32[2,2]{1,0:T(2,128)S(1)}, s32[2,2]{1,0:T(2,128)}, u32[]{:S(2)}) %copy-start.6) | copy-done | bytes 40
  10.1 1.2 %copy-done = f32[4,1,256,256]{3,2,1,0:T(8,128)S(1)} copy-done((f32[4,1,256,256]{3,2,1,0:T(8,128)S(1)}, f32[4,1,256,256]{3,2,1,0:T(8,128)}, u32[]{:S(2)}) %copy-start) | copy-done | bytes 1048600
  11.4 1.2 %copy-done.2 = f32[4,1,256,256]{3,2,1,0:T(8,128)S(1)} copy-done((f32[4,1,256,256]{3,2,1,0:T(8,128)S(1)}, f32[4,1,256,256]{3,2,1,0:T(8,128)}, u32[]{:S(2)}) %copy-start.2) | copy-done | bytes 1048600
  12.6 0.9 %copy-done.5 = f32[1,256,256]{2,1,0:T(8,128)S(1)} copy-done((f32[1,256,256]{2,1,0:T(8,128)S(1)}, f32[1,256,256]{2,1,0:T(8,128)}, u32[]{:S(2)}) %copy-start.5) | copy-done | bytes 262168
  13.5 2.7 %image.1 = (f32[2,136,256]{2,1,0:T(8,128)S(1)}, f32[2,136,256]{2,1,0:T(8,128)S(1)}, f32[2,256,256]{2,1,0:T(8,128)S(1)}) custom-call(s32[2]{0:T(128)S(1)} %pad_add_fusion.where_ref, s32[2,2]{1,0:T(2,128)S(1)} %copy-done.6, s32[4,1]{1,0:T(4,128)S(1)} %copy.9.conn_ref, f32[256,256]{1,0:T(8,128)S(1)} %bitcast.22, f32[256,256]{1,0:T(8,128)S(1)} %bitcast.19, ...), custom_call_target="tpu_custom_call" | custom-call | tf_op jit(solution)/shard_map/image/pallas_call | solution.py:179
  16.3 0.2 collective-permute-start.2
  16.5 1.4 %collective-permute-done.2 = f32[2,136,256]{2,1,0:T(8,128)S(1)} collective-permute-done((f32[2,136,256]{2,1,0:T(8,128)S(1)}, f32[2,136,256]{2,1,0:T(8,128)S(1)}, u32[]{:S(2)}, u32[]{:S(2)}) %collective-permute-start.2) | collective-permute-done | bytes 278560 | tf_op jit(solution)/shard_map/ppermute | solution.py:158
  17.9 0.0 copy-start.1
  18.0 1.8 %collective-permute-start.3 = (f32[136,256]{1,0:T(8,128)S(1)}, f32[136,256]{1,0:T(8,128)S(1)}, u32[]{:S(2)}, u32[]{:S(2)}) collective-permute-start(f32[136,256]{1,0:T(8,128)S(1)} %slice_bitcast_fusion), channel_id=1, source_target_pairs={{0,2},{2,0},{1,3},{3,1},{4,6},{6,4},{5,7},{7,5},{8,10},{10,8},{9,1... | collective-permute-start | bytes 417800 | tf_op jit(solution)/shard_map/ppermute | solution.py:158
  19.8 4.0 %collective-permute-done.3 = f32[136,256]{1,0:T(8,128)S(1)} collective-permute-done((f32[136,256]{1,0:T(8,128)S(1)}, f32[136,256]{1,0:T(8,128)S(1)}, u32[]{:S(2)}, u32[]{:S(2)}) %collective-permute-start.3) | collective-permute-done | bytes 139296 | tf_op jit(solution)/shard_map/ppermute | solution.py:158
  23.8 3.9 %collective-permute-start.6 = (f32[136,256]{1,0:T(8,128)S(1)}, f32[136,256]{1,0:T(8,128)S(1)}, u32[]{:S(2)}, u32[]{:S(2)}) collective-permute-start(f32[136,256]{1,0:T(8,128)S(1)} %fusion.refs_0_), channel_id=1, source_target_pairs={{0,12},{4,8},{8,4},{12,0},{1,13},{5,9},{9,5},{13,1},{2,14},{6,10},... | collective-permute-start | bytes 417800 | tf_op jit(solution)/shard_map/ppermute | solution.py:158
  27.7 0.0 collective-permute-start.5
  27.7 0.6 %collective-permute-start.4 = (f32[136,256]{1,0:T(8,128)S(1)}, f32[136,256]{1,0:T(8,128)S(1)}, u32[]{:S(2)}, u32[]{:S(2)}) collective-permute-start(f32[136,256]{1,0:T(8,128)S(1)} %fusion.refs_0_), channel_id=1, source_target_pairs={{0,4},{4,0},{8,12},{12,8},{1,5},{5,1},{9,13},{13,9},{2,6},{6,2},{1... | collective-permute-start | bytes 417800 | tf_op jit(solution)/shard_map/ppermute | solution.py:158
  28.3 4.0 %collective-permute-done.6.refs_3_ = f32[136,256]{1,0:T(8,128)S(1)} collective-permute-done((f32[136,256]{1,0:T(8,128)S(1)}, f32[136,256]{1,0:T(8,128)S(1)}, u32[]{:S(2)}, u32[]{:S(2)}) %collective-permute-start.6) | collective-permute-done | bytes 139296 | tf_op jit(solution)/shard_map/ppermute | solution.py:158
  32.3 6.6 %collective-permute-done.5.refs_2_ = f32[136,256]{1,0:T(8,128)S(1)} collective-permute-done((f32[136,256]{1,0:T(8,128)S(1)}, f32[136,256]{1,0:T(8,128)S(1)}, u32[]{:S(2)}, u32[]{:S(2)}) %collective-permute-start.5) | collective-permute-done | bytes 139296 | tf_op jit(solution)/shard_map/ppermute | solution.py:158
  39.0 0.0 collective-permute-done.4.refs_1_
  39.0 1.0 %fresh.1 = (f32[128,256]{1,0:T(8,128)S(1)}, f32[8,128]{1,0:T(8,128)S(1)}) custom-call(s32[2]{0:T(128)S(1)} %pad_add_fusion.where_ref, s32[2,2]{1,0:T(2,128)S(1)} %copy-done.6, f32[136,256]{1,0:T(8,128)S(1)} %fusion.refs_0_, f32[136,256]{1,0:T(8,128)S(1)} %collective-permute-done.4.refs_1_, f32[136,256]{1,0:T(8,128)S(1)} %collective-permute-done.5.refs_2_, ...), custom_call_target="tpu_custom_call" | custom-call | tf_op jit(solution)/shard_map/fresh/pallas_call | solution.py:202
  40.0 1.6 %collective-permute-start.8 = (f32[128,256]{1,0:T(8,128)S(1)}, f32[128,256]{1,0:T(8,128)S(1)}, u32[]{:S(2)}, u32[]{:S(2)}) collective-permute-start(f32[128,256]{1,0:T(8,128)S(1)} %get-tuple-element.15.refs_1_), channel_id=1, source_target_pairs={{0,2},{2,0},{1,3},{3,1},{4,6},{6,4},{5,7},{7,5},{8,10},{10,8},{9,1... | collective-permute-start | bytes 393224 | tf_op jit(solution)/shard_map/ppermute | solution.py:158
  41.6 0.0 collective-permute-start.7
  41.6 3.5 %collective-permute-done.8.refs_3_ = f32[128,256]{1,0:T(8,128)S(1)} collective-permute-done((f32[128,256]{1,0:T(8,128)S(1)}, f32[128,256]{1,0:T(8,128)S(1)}, u32[]{:S(2)}, u32[]{:S(2)}) %collective-permute-start.8) | collective-permute-done | bytes 131104 | tf_op jit(solution)/shard_map/ppermute | solution.py:158
  45.1 0.0 collective-permute-start.9
  45.1 0.0 collective-permute-done.7.refs_2_
  45.1 1.3 %collective-permute-done.9.refs_4_ = f32[128,256]{1,0:T(8,128)S(1)} collective-permute-done((f32[128,256]{1,0:T(8,128)S(1)}, f32[128,256]{1,0:T(8,128)S(1)}, u32[]{:S(2)}, u32[]{:S(2)}) %collective-permute-start.9) | collective-permute-done | bytes 131104 | tf_op jit(solution)/shard_map/ppermute | solution.py:158
  46.4 0.0 copy-done.3
  46.4 0.0 copy-done.1
  46.4 2.2 %corner.1 = (f32[8,128]{1,0:T(8,128)S(1)}, f32[256,256]{1,0:T(8,128)S(1)}, f32[8,128]{1,0:T(8,128)S(1)}) custom-call(s32[2]{0:T(128)S(1)} %pad_add_fusion.where_ref, s32[4,1]{1,0:T(4,128)S(1)} %copy.9.conn_ref, f32[2,256,256]{2,1,0:T(8,128)S(1)} %get-tuple-element.12.refs_4_.refs_0_.full_ref, f32[128,256]{1,0:T(8,128)S(1)} %get-tuple-element.15.refs_1_, ...), custom_call_target="tpu_custom_call" | custom-call | tf_op jit(solution)/shard_map/corner/pallas_call | solution.py:215
  48.6 0.2 collective-permute-start.10
  48.8 1.0 %collective-permute-done.10 = f32[8,128]{1,0:T(8,128)S(1)} collective-permute-done((f32[8,128]{1,0:T(8,128)S(1)}, f32[8,128]{1,0:T(8,128)S(1)}, u32[]{:S(2)}, u32[]{:S(2)}) %collective-permute-start.10) | collective-permute-done | bytes 4128 | tf_op jit(solution)/shard_map/ppermute | solution.py:158
  49.8 1.5 %collective-permute-start.11 = (f32[8,128]{1,0:T(8,128)S(1)}, f32[8,128]{1,0:T(8,128)S(1)}, u32[]{:S(2)}, u32[]{:S(2)}) collective-permute-start(f32[8,128]{1,0:T(8,128)S(1)} %add.24), channel_id=1, source_target_pairs={{0,2},{2,0},{1,3},{3,1},{4,6},{6,4},{5,7},{7,5},{8,10},{10,8},{9,1... | collective-permute-start | bytes 12296 | tf_op jit(solution)/shard_map/ppermute | solution.py:158
  51.3 2.1 %collective-permute-done.11 = f32[8,128]{1,0:T(8,128)S(1)} collective-permute-done((f32[8,128]{1,0:T(8,128)S(1)}, f32[8,128]{1,0:T(8,128)S(1)}, u32[]{:S(2)}, u32[]{:S(2)}) %collective-permute-start.11) | collective-permute-done | bytes 4128 | tf_op jit(solution)/shard_map/ppermute | solution.py:158
  53.5 0.0 collective-permute-start.12
  53.5 3.6 %collective-permute-done.12 = f32[8,128]{1,0:T(8,128)S(1)} collective-permute-done((f32[8,128]{1,0:T(8,128)S(1)}, f32[8,128]{1,0:T(8,128)S(1)}, u32[]{:S(2)}, u32[]{:S(2)}) %collective-permute-start.12) | collective-permute-done | bytes 4128 | tf_op jit(solution)/shard_map/ppermute | solution.py:158
  57.1 1.0 %collective-permute-start.13 = (f32[8,128]{1,0:T(8,128)S(1)}, f32[8,128]{1,0:T(8,128)S(1)}, u32[]{:S(2)}, u32[]{:S(2)}) collective-permute-start(f32[8,128]{1,0:T(8,128)S(1)} %add.26), channel_id=1, source_target_pairs={{0,8},{4,12},{8,0},{12,4},{1,9},{5,13},{9,1},{13,5},{2,10},{6,14},... | collective-permute-start | bytes 12296 | tf_op jit(solution)/shard_map/ppermute | solution.py:158
  58.1 3.5 %collective-permute-done.13 = f32[8,128]{1,0:T(8,128)S(1)} collective-permute-done((f32[8,128]{1,0:T(8,128)S(1)}, f32[8,128]{1,0:T(8,128)S(1)}, u32[]{:S(2)}, u32[]{:S(2)}) %collective-permute-start.13) | collective-permute-done | bytes 4128 | tf_op jit(solution)/shard_map/ppermute | solution.py:158
  61.6 0.8 %result.1 = (f32[1,256,256]{2,1,0:T(8,128)}, f32[8,128]{1,0:T(8,128)S(1)}) custom-call(f32[8,128]{1,0:T(8,128)S(1)} %add.27.sums_ref, f32[8,128]{1,0:T(8,128)S(1)} %get-tuple-element.18.info_ref, f32[2,256,256]{2,1,0:T(8,128)S(1)} %get-tuple-element.12.refs_4_.refs_0_.full_ref, f32[256,256]{1,0:T(8,128)S(1)} %get-tuple-element.19.fresh_ref), custom_call_target="tpu_custom_call" | custom-call | tf_op jit(solution)/shard_map/result/pallas_call | solution.py:238
  62.4 0.5 slice.11
  (11 shorter events, 0.1 us)
Async XLA Ops:
  0.6 8.8 %copy-start.4 = (f32[1,256,256]{2,1,0:T(8,128)S(1)}, f32[1,256,256]{2,1,0:T(8,128)}, u32[]{:S(2)}) copy-start(f32[1,256,256]{2,1,0:T(8,128)} %param.7) | copy-start | bytes 786436
  1.6 6.5 %collective-permute-start = (f32[128,256]{1,0:T(8,128)S(1)}, f32[128,256]{1,0:T(8,128)S(1)}, u32[]{:S(2)}, u32[]{:S(2)}) collective-permute-start(f32[128,256]{1,0:T(8,128)S(1)} %dynamic-slice_bitcast_fusion), channel_id=1, source_target_pairs={{0,2},{2,0},{1,3},{3,1},{4,6},{6,4},{5,7},{7,5},{8,10},{10,8},{9,1... | collective-permute-start | bytes 393224 | tf_op jit(solution)/shard_map/ppermute | solution.py:158
  8.1 1.3 %collective-permute-start.1 = (f32[128,256]{1,0:T(8,128)S(1)}, f32[128,256]{1,0:T(8,128)S(1)}, u32[]{:S(2)}, u32[]{:S(2)}) collective-permute-start(f32[128,256]{1,0:T(8,128)S(1)} %collective-permute-done.refs_2_), channel_id=1, source_target_pairs={{0,1},{1,0},{2,3},{3,2},{4,5},{5,4},{6,7},{7,6},{8,9},{9,8},{10,11... | collective-permute-start | bytes 393224 | tf_op jit(solution)/shard_map/ppermute | solution.py:158
  8.1 0.7 %copy-start.7 = (s32[4,1]{0,1:T(1,128)S(1)}, s32[4,1]{0,1:T(1,128)}, u32[]{:S(2)}) copy-start(s32[4,1]{0,1:T(1,128)} %param.9) | copy-start | bytes 52
  9.5 0.7 %copy-start.6 = (s32[2,2]{1,0:T(2,128)S(1)}, s32[2,2]{1,0:T(2,128)}, u32[]{:S(2)}) copy-start(s32[2,2]{1,0:T(2,128)} %sizes_ref.3) | copy-start | bytes 52
  10.1 1.2 %copy-start = (f32[4,1,256,256]{3,2,1,0:T(8,128)S(1)}, f32[4,1,256,256]{3,2,1,0:T(8,128)}, u32[]{:S(2)}) copy-start(f32[4,1,256,256]{3,2,1,0:T(8,128)} %param.10) | copy-start | bytes 3145732
  11.4 1.2 %copy-start.2 = (f32[4,1,256,256]{3,2,1,0:T(8,128)S(1)}, f32[4,1,256,256]{3,2,1,0:T(8,128)}, u32[]{:S(2)}) copy-start(f32[4,1,256,256]{3,2,1,0:T(8,128)} %param.11) | copy-start | bytes 3145732
  12.6 0.9 %copy-start.5 = (f32[1,256,256]{2,1,0:T(8,128)S(1)}, f32[1,256,256]{2,1,0:T(8,128)}, u32[]{:S(2)}) copy-start(f32[1,256,256]{2,1,0:T(8,128)} %param.6) | copy-start | bytes 786436
  16.3 1.6 %collective-permute-start.2 = (f32[2,136,256]{2,1,0:T(8,128)S(1)}, f32[2,136,256]{2,1,0:T(8,128)S(1)}, u32[]{:S(2)}, u32[]{:S(2)}) collective-permute-start(f32[2,136,256]{2,1,0:T(8,128)S(1)} %get-tuple-element.14), channel_id=1, source_target_pairs={{0,1},{1,0},{2,3},{3,2},{4,5},{5,4},{6,7},{7,6},{8,9},{9,8},{10,11... | collective-permute-start | bytes 835592 | tf_op jit(solution)/shard_map/ppermute | solution.py:158
  17.9 28.5 %copy-start.3 = (f32[4,1,256,256]{3,2,1,0:T(8,128)S(1)}, f32[4,1,256,256]{3,2,1,0:T(8,128)}, u32[]{:S(2)}) copy-start(f32[4,1,256,256]{3,2,1,0:T(8,128)} %param.11) | copy-start | bytes 3145732
  17.9 28.5 %copy-start.1 = (f32[4,1,256,256]{3,2,1,0:T(8,128)S(1)}, f32[4,1,256,256]{3,2,1,0:T(8,128)}, u32[]{:S(2)}) copy-start(f32[4,1,256,256]{3,2,1,0:T(8,128)} %param.10) | copy-start | bytes 3145732
  18.0 5.8 %collective-permute-start.3 = (f32[136,256]{1,0:T(8,128)S(1)}, f32[136,256]{1,0:T(8,128)S(1)}, u32[]{:S(2)}, u32[]{:S(2)}) collective-permute-start(f32[136,256]{1,0:T(8,128)S(1)} %slice_bitcast_fusion), channel_id=1, source_target_pairs={{0,2},{2,0},{1,3},{3,1},{4,6},{6,4},{5,7},{7,5},{8,10},{10,8},{9,1... | collective-permute-start | bytes 417800 | tf_op jit(solution)/shard_map/ppermute | solution.py:158
  23.8 8.5 %collective-permute-start.6 = (f32[136,256]{1,0:T(8,128)S(1)}, f32[136,256]{1,0:T(8,128)S(1)}, u32[]{:S(2)}, u32[]{:S(2)}) collective-permute-start(f32[136,256]{1,0:T(8,128)S(1)} %fusion.refs_0_), channel_id=1, source_target_pairs={{0,12},{4,8},{8,4},{12,0},{1,13},{5,9},{9,5},{13,1},{2,14},{6,10},... | collective-permute-start | bytes 417800 | tf_op jit(solution)/shard_map/ppermute | solution.py:158
  27.7 11.3 %collective-permute-start.5 = (f32[136,256]{1,0:T(8,128)S(1)}, f32[136,256]{1,0:T(8,128)S(1)}, u32[]{:S(2)}, u32[]{:S(2)}) collective-permute-start(f32[136,256]{1,0:T(8,128)S(1)} %fusion.refs_0_), channel_id=1, source_target_pairs={{0,8},{4,12},{8,0},{12,4},{1,9},{5,13},{9,1},{13,5},{2,10},{6,14},... | collective-permute-start | bytes 417800 | tf_op jit(solution)/shard_map/ppermute | solution.py:158
  27.7 11.3 %collective-permute-start.4 = (f32[136,256]{1,0:T(8,128)S(1)}, f32[136,256]{1,0:T(8,128)S(1)}, u32[]{:S(2)}, u32[]{:S(2)}) collective-permute-start(f32[136,256]{1,0:T(8,128)S(1)} %fusion.refs_0_), channel_id=1, source_target_pairs={{0,4},{4,0},{8,12},{12,8},{1,5},{5,1},{9,13},{13,9},{2,6},{6,2},{1... | collective-permute-start | bytes 417800 | tf_op jit(solution)/shard_map/ppermute | solution.py:158
  40.0 5.0 %collective-permute-start.8 = (f32[128,256]{1,0:T(8,128)S(1)}, f32[128,256]{1,0:T(8,128)S(1)}, u32[]{:S(2)}, u32[]{:S(2)}) collective-permute-start(f32[128,256]{1,0:T(8,128)S(1)} %get-tuple-element.15.refs_1_), channel_id=1, source_target_pairs={{0,2},{2,0},{1,3},{3,1},{4,6},{6,4},{5,7},{7,5},{8,10},{10,8},{9,1... | collective-permute-start | bytes 393224 | tf_op jit(solution)/shard_map/ppermute | solution.py:158
  41.6 3.5 %collective-permute-start.7 = (f32[128,256]{1,0:T(8,128)S(1)}, f32[128,256]{1,0:T(8,128)S(1)}, u32[]{:S(2)}, u32[]{:S(2)}) collective-permute-start(f32[128,256]{1,0:T(8,128)S(1)} %get-tuple-element.15.refs_1_), channel_id=1, source_target_pairs={{0,1},{1,0},{2,3},{3,2},{4,5},{5,4},{6,7},{7,6},{8,9},{9,8},{10,11... | collective-permute-start | bytes 393224 | tf_op jit(solution)/shard_map/ppermute | solution.py:158
  45.1 1.3 %collective-permute-start.9 = (f32[128,256]{1,0:T(8,128)S(1)}, f32[128,256]{1,0:T(8,128)S(1)}, u32[]{:S(2)}, u32[]{:S(2)}) collective-permute-start(f32[128,256]{1,0:T(8,128)S(1)} %collective-permute-done.8.refs_3_), channel_id=1, source_target_pairs={{0,1},{1,0},{2,3},{3,2},{4,5},{5,4},{6,7},{7,6},{8,9},{9,8},{10,11... | collective-permute-start | bytes 393224 | tf_op jit(solution)/shard_map/ppermute | solution.py:158
  48.6 1.2 %collective-permute-start.10 = (f32[8,128]{1,0:T(8,128)S(1)}, f32[8,128]{1,0:T(8,128)S(1)}, u32[]{:S(2)}, u32[]{:S(2)}) collective-permute-start(f32[8,128]{1,0:T(8,128)S(1)} %get-tuple-element.17), channel_id=1, source_target_pairs={{0,1},{1,0},{2,3},{3,2},{4,5},{5,4},{6,7},{7,6},{8,9},{9,8},{10,11... | collective-permute-start | bytes 12296 | tf_op jit(solution)/shard_map/ppermute | solution.py:158
  49.8 3.6 %collective-permute-start.11 = (f32[8,128]{1,0:T(8,128)S(1)}, f32[8,128]{1,0:T(8,128)S(1)}, u32[]{:S(2)}, u32[]{:S(2)}) collective-permute-start(f32[8,128]{1,0:T(8,128)S(1)} %add.24), channel_id=1, source_target_pairs={{0,2},{2,0},{1,3},{3,1},{4,6},{6,4},{5,7},{7,5},{8,10},{10,8},{9,1... | collective-permute-start | bytes 12296 | tf_op jit(solution)/shard_map/ppermute | solution.py:158
  53.5 3.6 %collective-permute-start.12 = (f32[8,128]{1,0:T(8,128)S(1)}, f32[8,128]{1,0:T(8,128)S(1)}, u32[]{:S(2)}, u32[]{:S(2)}) collective-permute-start(f32[8,128]{1,0:T(8,128)S(1)} %add.25), channel_id=1, source_target_pairs={{0,4},{4,0},{8,12},{12,8},{1,5},{5,1},{9,13},{13,9},{2,6},{6,2},{1... | collective-permute-start | bytes 12296 | tf_op jit(solution)/shard_map/ppermute | solution.py:158
  57.1 4.5 %collective-permute-start.13 = (f32[8,128]{1,0:T(8,128)S(1)}, f32[8,128]{1,0:T(8,128)S(1)}, u32[]{:S(2)}, u32[]{:S(2)}) collective-permute-start(f32[8,128]{1,0:T(8,128)S(1)} %add.26), channel_id=1, source_target_pairs={{0,8},{4,12},{8,0},{12,4},{1,9},{5,13},{9,1},{13,5},{2,10},{6,14},... | collective-permute-start | bytes 12296 | tf_op jit(solution)/shard_map/ppermute | solution.py:158

commit v2 on v1

v2 whole, which is shorter than its diff:
```python
import functools
import math

import jax
import jax.numpy as jnp
from jax import lax
from jax.experimental import pallas as pl
from jax.experimental.pallas import tpu as pltpu
from jax.sharding import PartitionSpec as P

F32 = jnp.float32
BF16 = jnp.bfloat16
PREPARE = 49
LANES = 128
PAD = 8
PARAMS = pltpu.CompilerParams(vmem_limit_bytes=40 * 1024 * 1024)
NN = (((1,), (0,)), ((), ()))
NT = (((1,), (1,)), ((), ()))


def split(x):
    high = x.astype(BF16)
    return high, (x - high.astype(F32)).astype(BF16)


def product(a, b, dims):
    dot = functools.partial(lax.dot_general, dimension_numbers=dims, preferred_element_type=F32)
    return dot(a[0], b[0]) + (dot(a[0], b[1]) + dot(a[1], b[0]))


def live_mask(sizes_ref, sector, first, rows, cols):
    row = lax.broadcasted_iota(jnp.int32, (rows, cols), 0) + first
    col = lax.broadcasted_iota(jnp.int32, (rows, cols), 1)
    return ((row < sizes_ref[sector, 0]) & (col < sizes_ref[sector, 1])).astype(F32)


def total(x):
    return jnp.sum(x, keepdims=True)


def halves_of(half):
    core = lax.axis_index("rep")
    mine = pl.ds(pl.multiple_of(core * half, half), half)
    other = pl.ds(pl.multiple_of((1 - core) * half, half), half)
    return mine, other


def prepare_kernel(weight, sizes_ref, conn_ref, psi_hbm, diag_hbm, left_hbm, right_hbm, *refs):
    lh, ll, th, tl, rh, rl, mask_ref, own_ref, slot_ref, stat_ref, psi, diag, left, right, vector_sem, left_sem, right_sem = refs
    nterm = left.shape[0]
    vectors = [
        pltpu.make_async_copy(psi_hbm.at[0], psi, vector_sem.at[0]),
        pltpu.make_async_copy(diag_hbm.at[0], diag, vector_sem.at[1]),
    ]
    lefts = [pltpu.make_async_copy(left_hbm.at[i, 0], left.at[i], left_sem.at[i]) for i in range(nterm)]
    rights = [pltpu.make_async_copy(right_hbm.at[i, 0], right.at[i], right_sem.at[i]) for i in range(nterm)]
    for copy in vectors + lefts + rights:
        copy.start()
    me = lax.axis_index("sector")
    nsec, half, blk = mask_ref.shape
    first = lax.axis_index("rep") * half
    for slot in range(nsec):
        mask_ref[slot] = live_mask(sizes_ref, me ^ slot, first, half, blk)
    for term in range(nterm):
        slot_ref[term] = jnp.full(slot_ref.shape[1:], conn_ref[term] ^ me, jnp.int32)
    for copy in vectors:
        copy.wait()
    own = psi[...] * live_mask(sizes_ref, me, 0, blk, blk)
    own_ref[...] = own
    square = own * own
    row = lax.broadcasted_iota(jnp.int32, stat_ref.shape, 0)
    stat_ref[...] = jnp.where(row == 0, total(square), total(square * diag[...]) * weight)
    for term in range(nterm):
        lefts[term].wait()
        value = left[term]
        lh[term], ll[term] = split(value)
        th[term], tl[term] = split(value.T)
    for term in range(nterm):
        rights[term].wait()
        rh[term], rl[term] = split(right[term])


def pick(slot_ref, term, blocks):
    blk = blocks[0].shape[0]
    slot = jnp.broadcast_to(slot_ref[term, :1, :], (blk, blk))
    value = blocks[0]
    for index in range(1, len(blocks)):
        value = jnp.where(slot == index, blocks[index], value)
    return value


def image_kernel(coupling, ncell, nsec, *refs):
    halves = refs[: 2 * (nsec - 1)]
    own_ref, slot_ref, stat_ref = refs[2 * (nsec - 1) : 2 * (nsec - 1) + 3]
    lh, ll, th, tl, rh, rl, keep_ref, send_ref, full_ref, norm_ref, acc = refs[2 * (nsec - 1) + 3 :]
    blk = own_ref.shape[0]
    half = blk // 2
    nterm = lh.shape[0]
    mine, other = halves_of(half)
    own = own_ref[...]
    full_ref[0] = own
    for slot in range(1, nsec):
        full_ref[slot, mine, :] = halves[2 * slot - 2][...]
        full_ref[slot, other, :] = halves[2 * slot - 1][...]
    blocks = [own] + [full_ref[slot] for slot in range(1, nsec)]
    norm = stat_ref[:1, :1]
    for block in blocks[1:]:
        norm = norm + total(block * block)
    norm_ref[...] = jnp.broadcast_to(norm / ncell, norm_ref.shape)
    terms = range(nterm)
    middles = [product((lh[i], ll[i]), split(pick(slot_ref, i, blocks)), NN) for i in terms]
    joints = [coupling * own + product(split(middles[i]), (rh[i], rl[i]), NT) for i in terms]
    squares = joints[0] * joints[0]
    for joint in joints[1:]:
        squares = squares + joint * joint
    scalar = stat_ref[1:2, :1] + total(squares)
    inner = [product(split(joints[i]), (rh[i], rl[i]), NN) for i in terms]
    returned = [product((th[i], tl[i]), split(inner[i]), NN) for i in terms]
    for slot in range(nsec):
        value = coupling * sum(joints[1:], joints[0]) if slot == 0 else jnp.zeros((blk, blk), F32)
        for i in terms:
            target = jnp.broadcast_to(slot_ref[i, :1, :], (blk, blk))
            value = value + jnp.where(target == slot, returned[i], 0.0)
        acc[slot] = value
        for ref, rows in ((keep_ref, mine), (send_ref, other)):
            for tile in range(blk // LANES):
                ref[slot, tile * half : (tile + 1) * half, :] = acc[slot, rows, tile * LANES : (tile + 1) * LANES]
            ref[slot, blk // LANES * half :, :] = jnp.broadcast_to(scalar, (PAD, LANES))


def fresh_kernel(ncell, nparts, *refs):
    parts = refs[:nparts]
    full_ref, mask_ref, diag_ref, norm_ref, fresh_ref, cross_ref = refs[nparts:]
    half, blk = fresh_ref.shape
    mine, _ = halves_of(half)
    norm = norm_ref[:1, :1]
    scale = 1.0 / jnp.sqrt(norm)
    summed = parts[0][...]
    for part in parts[1:]:
        summed = summed + part[...]
    tiles = blk // LANES
    theta = summed[tiles * half : tiles * half + 1, :1] / (ncell * norm)
    summed = jnp.concatenate([summed[tile * half : (tile + 1) * half] for tile in range(tiles)], axis=1)
    trial = full_ref[0, mine, :] * scale
    diag = diag_ref[mine, :]
    image = (diag * trial + summed * scale) * mask_ref[0]
    residue = image - theta * trial
    shifted = diag - theta
    fresh = residue * shifted / (shifted * shifted + 1.0)
    fresh_ref[...] = fresh
    row = lax.broadcasted_iota(jnp.int32, cross_ref.shape, 0)
    cross_ref[...] = jnp.where(row == 0, total(residue * fresh), theta)


def corner_kernel(coupling, weight, ncell, share, nsec, *refs):
    halves = refs[: 2 * nsec]
    full_ref, diag_ref, norm_ref, cross_ref, slot_ref, lh, ll, rh, rl = refs[2 * nsec : 2 * nsec + 9]
    sums_ref, fresh_ref, info_ref, work = refs[2 * nsec + 9 :]
    blk = diag_ref.shape[0]
    nterm = lh.shape[0]
    mine, other = halves_of(blk // 2)
    for slot in range(nsec):
        work[slot, mine, :] = halves[2 * slot][...]
        work[slot, other, :] = halves[2 * slot + 1][...]
    norm = norm_ref[:1, :1]
    start = [full_ref[slot] for slot in range(nsec)]
    raw = [work[slot] for slot in range(nsec)]
    overlap = start[0] * raw[0]
    for slot in range(1, nsec):
        overlap = overlap + start[slot] * raw[slot]
    overlap = total(overlap) / (ncell * norm)
    fresh = [raw[slot] - overlap * start[slot] for slot in range(nsec)]
    length = fresh[0] * fresh[0]
    for slot in range(1, nsec):
        length = length + fresh[slot] * fresh[slot]
    length = total(length) / ncell
    own = fresh[0]
    fresh_ref[...] = own
    terms = range(nterm)
    middles = [product((lh[i], ll[i]), split(pick(slot_ref, i, fresh)), NN) for i in terms]
    joints = [coupling * own + product(split(middles[i]), (rh[i], rl[i]), NT) for i in terms]
    squares = weight * own * own * diag_ref[...]
    for joint in joints:
        squares = squares + joint * joint
    row = lax.broadcasted_iota(jnp.int32, sums_ref.shape, 0)
    sums_ref[...] = jnp.where(row == 0, total(squares), cross_ref[:1, :1] * share)
    info_ref[...] = jnp.where(row == 0, norm, jnp.where(row == 1, length, cross_ref[1:2, :1]))


def result_kernel(ncell, sums_ref, info_ref, full_ref, fresh_ref, vector_ref, energy_ref):
    sums, info = sums_ref[...], info_ref[...]
    norm, length, theta = info[0:1, :1], info[1:2, :1], info[2:3, :1]
    corner = sums[0:1, :1] / (ncell * length)
    cross = sums[1:2, :1] / (ncell * jnp.sqrt(length))
    spread = (theta - corner) / 2.0
    lowest = (theta + corner) / 2.0 - jnp.sqrt(spread * spread + cross * cross)
    keep = corner - lowest
    turn = -cross
    size = jnp.sqrt(keep * keep + turn * turn)
    keep = keep / size
    turn = turn / size
    vector_ref[0] = (keep / jnp.sqrt(norm)) * full_ref[0] + (turn / jnp.sqrt(length)) * fresh_ref[...]
    energy_ref[0] = jnp.sum(lowest)


def across(x, axis, step):
    size = lax.axis_size(axis)
    return lax.ppermute(x, axis, [(i, i ^ step) for i in range(size)])


def diagonally(x, axis, step):
    size = lax.axis_size(axis)
    return lax.ppermute(x, (axis, "rep"), [(2 * i + c, 2 * (i ^ step) + 1 - c) for i in range(size) for c in range(2)])


def body(psi_start, diagonal, sector_sizes, conn, left_ops, right_ops):
    blk = psi_start.shape[-1]
    half = blk // 2
    nterm_dev = conn.shape[0]
    nsec, nz, nrep = lax.axis_size("sector"), lax.axis_size("terms"), lax.axis_size("rep")
    coupling = 1.0 / math.sqrt(nterm_dev * nz * nrep)
    weight = 1.0 / (nz * nrep)
    ncell = float(nsec * blk * blk)
    core = lax.axis_index("rep")
    psi, diag = psi_start[0], diagonal[0]
    vmem, smem, hbm = (pl.BlockSpec(memory_space=space) for space in (pltpu.VMEM, pltpu.SMEM, pltpu.HBM))
    shape = jax.ShapeDtypeStruct

    mine = lax.dynamic_slice_in_dim(psi, core * half, half, 0)
    halves = []
    for step in range(1, nsec):
        near = across(mine, "sector", step)
        halves.append(near)

    operator = (nterm_dev, blk, blk)
    *ops, mask, own, slots, stat = pl.pallas_call(
        functools.partial(prepare_kernel, weight),
        out_shape=[shape(operator, BF16)] * 6
        + [shape((nsec, half, blk), F32), shape((blk, blk), F32), shape((nterm_dev, 8, blk), jnp.int32), shape((8, 128), F32)],
        in_specs=[smem] * 2 + [hbm] * 4,
        out_specs=[vmem] * 10,
        scratch_shapes=[
            pltpu.VMEM((blk, blk), F32),
            pltpu.VMEM((blk, blk), F32),
            pltpu.VMEM(operator, F32),
            pltpu.VMEM(operator, F32),
            pltpu.SemaphoreType.DMA((2,)),
            pltpu.SemaphoreType.DMA((nterm_dev,)),
            pltpu.SemaphoreType.DMA((nterm_dev,)),
        ],
        compiler_params=pltpu.CompilerParams(vmem_limit_bytes=PREPARE * 1024 * 1024),
        name="prepare",
    )(sector_sizes, conn[:, 0], psi_start, diagonal, left_ops, right_ops)
    lh, ll, th, tl, rh, rl = ops
    masked = [near * mask[slot] for slot, near in enumerate(halves, 1)]
    halves = [part for near in masked for part in (near, across(near, "rep", 1))]

    keep, send, full, norm = pl.pallas_call(
        functools.partial(image_kernel, coupling, ncell, nsec),
        out_shape=[
            shape((nsec, blk // LANES * half + PAD, LANES), F32),
            shape((nsec, blk // LANES * half + PAD, LANES), F32),
            shape((nsec, blk, blk), F32),
            shape((8, 128), F32),
        ],
        in_specs=[vmem] * (len(halves) + 9),
        out_specs=[vmem] * 4,
        scratch_shapes=[pltpu.VMEM((nsec, blk, blk), F32)],
        compiler_params=PARAMS,
        name="image",
    )(*halves, own, slots, stat, lh, ll, th, tl, rh, rl)

    chip = keep + across(send, "rep", 1)
    part = chip[0]
    for step in range(1, nsec):
        part = part + across(chip[step], "sector", step)
    parts = [part] + [across(part, "terms", step) for step in range(1, nz)]
    fresh, cross = pl.pallas_call(
        functools.partial(fresh_kernel, ncell, nz),
        out_shape=[shape((half, blk), F32), shape((8, 128), F32)],
        in_specs=[vmem] * (nz + 4),
        out_specs=[vmem] * 2,
        compiler_params=PARAMS,
        name="fresh",
    )(*parts, full, mask, diag, norm)

    halves = []
    for step in range(nsec):
        near = across(fresh, "sector", step) if step else fresh
        halves += [near, across(near, "rep", 1)]
    sums, direction, info = pl.pallas_call(
        functools.partial(corner_kernel, coupling, weight, ncell, 1.0 / nz, nsec),
        out_shape=[shape((8, 128), F32), shape((blk, blk), F32), shape((8, 128), F32)],
        in_specs=[vmem] * (len(halves) + 9),
        out_specs=[vmem] * 3,
        scratch_shapes=[pltpu.VMEM((nsec, blk, blk), F32)],
        compiler_params=PARAMS,
        name="corner",
    )(*halves, full, diag, norm, cross, slots, lh, ll, rh, rl)

    sums = sums + across(sums, "rep", 1)
    for axis in ("sector", "terms"):
        parts = [diagonally(sums, axis, step) for step in range(1, lax.axis_size(axis))]
        sums = functools.reduce(lambda x, y: x + y, parts, sums)
    vector, energy = pl.pallas_call(
        functools.partial(result_kernel, ncell),
        out_shape=[shape((1, blk, blk), F32), shape((1,), F32)],
        in_specs=[vmem] * 4,
        out_specs=[vmem, smem],
        compiler_params=PARAMS,
        name="result",
    )(sums, info, full, direction)
    return vector, energy


def solution(mesh):
    in_specs = (
        P(("groups", "sector"), None, None),
        P(("groups", "sector"), None, None),
        P("groups", None),
        P(("groups", "terms", "rep"), "sector"),
        P(("groups", "terms", "rep"), "sector", None, None),
        P(("groups", "terms", "rep"), "sector", None, None),
    )
    out_specs = (P(("groups", "sector"), None, None), P("groups"))
    return jax.shard_map(body, mesh=mesh, in_specs=in_specs, out_specs=out_specs, check_vma=False)
```

time: 63.2 us -> 53.8 us (0.85)
  waiting for transfers between devices: 35.1 us -> 26.9 us
  local copies, waits for them, and re-layouts: 6.32 us -> 1.93 us
  starting transfers between devices: 13.9 us -> 16.6 us
    ppermute x14 -> x11, waiting for transfers between devices: 35.1 us -> 22.9 us  [across(): return lax.ppermute(x, axis, [(i, i ^ step) for i in range(size)])]
    ppermute x0 -> x4, starting transfers between devices: none -> 5.14 us  [diagonally(): lax.ppermute(x, (axis, 'rep'), [(2 * i + c, 2 * (i ^ step) + 1 - c) for i...]
    ppermute x0 -> x4, waiting for transfers between devices: none -> 4.07 us  [diagonally(): lax.ppermute(x, (axis, 'rep'), [(2 * i + c, 2 * (i ^ step) + 1 - c) for i...]
    unnamed x17 -> x8, local copies, waits for them, and re-layouts: 4.84 us -> 0.96 us
    ppermute x14 -> x11, starting transfers between devices: 13.9 us -> 11.4 us  [across(): return lax.ppermute(x, axis, [(i, i ^ step) for i in range(size)])]
    pallas_call x4 -> x5, Pallas kernels: 6.81 us -> 7.3 us  [the longest x1 2.4 us: body(): pl.pallas_call(functools.partial(prepare_kernel, weight), out_shape=[shap...]
  transfers between devices with their start and end apart: 14 -> 15, of which waited for: 12 -> 12; matrix products, arithmetic and copies ran while one was open for 0% -> 0% of each run, Pallas kernels for 0% -> 4%
where the time goes in v2:
time: 53.8 us; the launch traced here: 53.6 us
  waiting for transfers between devices  26.9 us (50%)
  starting transfers between devices  16.6 us (31%)
  Pallas kernels  7.3 us (14%)
  local copies, waits for them, and re-layouts  1.93 us (4%)
  between operations  0.74 us (1%)
    ppermute x11, waiting for transfers between devices, across(): return lax.ppermute(x, axis, [(i, i ^ step) for i in range(size)])  22.9 us
    ppermute x11, starting transfers between devices, across(): return lax.ppermute(x, axis, [(i, i ^ step) for i in range(size)])  11.4 us
    ppermute x4, starting transfers between devices, diagonally(): lax.ppermute(x, (axis, 'rep'), [(2 * i + c, 2 * (i ^ step) + 1 - c) for i...  5.14 us
    ppermute x4, waiting for transfers between devices, diagonally(): lax.ppermute(x, (axis, 'rep'), [(2 * i + c, 2 * (i ^ step) + 1 - c) for i...  4.07 us
    pallas_call x1, Pallas kernels, body(): pl.pallas_call(functools.partial(prepare_kernel, weight), out_shape=[shap...  2.4 us
    pallas_call x1, Pallas kernels, body(): pl.pallas_call(functools.partial(image_kernel, coupling, ncell, nsec), ou...  2.23 us
    pallas_call x1, Pallas kernels, body(): pl.pallas_call(functools.partial(corner_kernel, coupling, weight, ncell,...  1.58 us
  transfers between devices with their start and end apart: 15, of which 12 were waited for; matrix products, arithmetic and copies ran while one was open for 0% of the time, Pallas kernels for 4%

profile of v2, /device:TPU:0, one launch (start us, length us, event | category | flops | bytes accessed | tf_op | source)
XLA Modules:
  0.0 53.6 jit_solution(5533044194302748614)
XLA Ops:
  0.6 0.0 copy-start
  0.6 1.0 %dynamic-slice_bitcast_fusion = f32[128,256]{1,0:T(8,128)S(1)} fusion(f32[1,256,256]{2,1,0:T(8,128)} %psi_hbm.1, s32[]{:T(128)S(6)} %select_n.3), kind=kLoop, calls=%fused_computation.4 | loop fusion | bytes 262148 | tf_op jit(solution)/shard_map/dynamic_slice | solution.py:229
  1.6 0.0 copy-start.2
  1.6 0.0 copy-start.3
  1.6 3.0 %collective-permute-start = (f32[128,256]{1,0:T(8,128)S(1)}, f32[128,256]{1,0:T(8,128)S(1)}, u32[]{:S(2)}, u32[]{:S(2)}) collective-permute-start(f32[128,256]{1,0:T(8,128)S(1)} %dynamic-slice_bitcast_fusion), channel_id=1, source_target_pairs={{0,2},{2,0},{1,3},{3,1},{4,6},{6,4},{5,7},{7,5},{8,10},{10,8},{9,1... | collective-permute-start | bytes 393224 | tf_op jit(solution)/shard_map/ppermute | solution.py:208
  4.6 0.0 copy-done
  4.6 0.0 copy-done.2
  4.6 0.0 copy-done.3
  4.6 0.0 copy-start.1
  4.6 0.9 %copy-done.1 = f32[1,256,256]{2,1,0:T(8,128)S(1)} copy-done((f32[1,256,256]{2,1,0:T(8,128)S(1)}, f32[1,256,256]{2,1,0:T(8,128)}, u32[]{:S(2)}) %copy-start.1) | copy-done | bytes 262168
  5.6 2.4 %prepare.1 = (bf16[4,256,256]{2,1,0:T(8,128)(2,1)S(1)}, bf16[4,256,256]{2,1,0:T(8,128)(2,1)S(1)}, bf16[4,256,256]{2,1,0:T(8,128)(2,1)S(1)}, bf16[4,256,256]{2,1,...) custom-call(s32[2,2]{1,0:T(2,128)S(1)} %copy-done.2, ...), custom_call_target="tpu_custom_call" | custom-call | tf_op jit(solution)/shard_map/prepare/pallas_call | solution.py:236
  8.0 0.1 collective-permute-done
  8.2 0.1 collective-permute-start.1
  8.2 1.3 %collective-permute-done.1.refs_1_ = f32[128,256]{1,0:T(8,128)S(1)} collective-permute-done((f32[128,256]{1,0:T(8,128)S(1)}, f32[128,256]{1,0:T(8,128)S(1)}, u32[]{:S(2)}, u32[]{:S(2)}) %collective-permute-start.1) | collective-permute-done | bytes 131104 | tf_op jit(solution)/shard_map/ppermute | solution.py:208
  9.6 2.2 %image.1 = (f32[2,264,128]{2,1,0:T(8,128)S(1)}, f32[2,264,128]{2,1,0:T(8,128)S(1)}, f32[2,256,256]{2,1,0:T(8,128)S(1)}, f32[8,128]{1,0:T(8,128)S(1)}) custom-call(f32[128,256]{1,0:T(8,128)S(1)} %bitcast_multiply_fusion.refs_0_, f32[128,256]{1,0:T(8,128)S(1)} %collective-permute-done.1.refs_1_, f32[256,256]{1,0:T(8,128)S(1)} %get-tuple-element.22.refs_2_, ...), custom_call_target="tpu_custom_call" | custom-call | tf_op jit(solution)/shard_map/image/pallas_call | solution.py:258
  11.8 0.2 collective-permute-start.2
  12.0 1.4 %collective-permute-done.2 = f32[2,264,128]{2,1,0:T(8,128)S(1)} collective-permute-done((f32[2,264,128]{2,1,0:T(8,128)S(1)}, f32[2,264,128]{2,1,0:T(8,128)S(1)}, u32[]{:S(2)}, u32[]{:S(2)}) %collective-permute-start.2) | collective-permute-done | bytes 270368 | tf_op jit(solution)/shard_map/ppermute | solution.py:208
  13.5 1.8 %collective-permute-start.3 = (f32[264,128]{1,0:T(8,128)S(1)}, f32[264,128]{1,0:T(8,128)S(1)}, u32[]{:S(2)}, u32[]{:S(2)}) collective-permute-start(f32[264,128]{1,0:T(8,128)S(1)} %slice_bitcast_fusion), channel_id=1, source_target_pairs={{0,2},{2,0},{1,3},{3,1},{4,6},{6,4},{5,7},{7,5},{8,10},{10,8},{9,1... | collective-permute-start | bytes 405512 | tf_op jit(solution)/shard_map/ppermute | solution.py:208
  15.3 3.9 %collective-permute-done.3 = f32[264,128]{1,0:T(8,128)S(1)} collective-permute-done((f32[264,128]{1,0:T(8,128)S(1)}, f32[264,128]{1,0:T(8,128)S(1)}, u32[]{:S(2)}, u32[]{:S(2)}) %collective-permute-start.3) | collective-permute-done | bytes 135200 | tf_op jit(solution)/shard_map/ppermute | solution.py:208
  19.2 3.9 %collective-permute-start.6 = (f32[264,128]{1,0:T(8,128)S(1)}, f32[264,128]{1,0:T(8,128)S(1)}, u32[]{:S(2)}, u32[]{:S(2)}) collective-permute-start(f32[264,128]{1,0:T(8,128)S(1)} %fusion.refs_0_), channel_id=1, source_target_pairs={{0,12},{4,8},{8,4},{12,0},{1,13},{5,9},{9,5},{13,1},{2,14},{6,10},... | collective-permute-start | bytes 405512 | tf_op jit(solution)/shard_map/ppermute | solution.py:208
  23.1 0.0 collective-permute-start.5
  23.1 0.6 %collective-permute-start.4 = (f32[264,128]{1,0:T(8,128)S(1)}, f32[264,128]{1,0:T(8,128)S(1)}, u32[]{:S(2)}, u32[]{:S(2)}) collective-permute-start(f32[264,128]{1,0:T(8,128)S(1)} %fusion.refs_0_), channel_id=1, source_target_pairs={{0,4},{4,0},{8,12},{12,8},{1,5},{5,1},{9,13},{13,9},{2,6},{6,2},{1... | collective-permute-start | bytes 405512 | tf_op jit(solution)/shard_map/ppermute | solution.py:208
  23.8 3.9 %collective-permute-done.6.refs_3_ = f32[264,128]{1,0:T(8,128)S(1)} collective-permute-done((f32[264,128]{1,0:T(8,128)S(1)}, f32[264,128]{1,0:T(8,128)S(1)}, u32[]{:S(2)}, u32[]{:S(2)}) %collective-permute-start.6) | collective-permute-done | bytes 135200 | tf_op jit(solution)/shard_map/ppermute | solution.py:208
  27.6 6.4 %collective-permute-done.5.refs_2_ = f32[264,128]{1,0:T(8,128)S(1)} collective-permute-done((f32[264,128]{1,0:T(8,128)S(1)}, f32[264,128]{1,0:T(8,128)S(1)}, u32[]{:S(2)}, u32[]{:S(2)}) %collective-permute-start.5) | collective-permute-done | bytes 135200 | tf_op jit(solution)/shard_map/ppermute | solution.py:208
  34.0 0.0 collective-permute-done.4.refs_1_
  34.0 0.3 fresh.1
  34.3 1.6 %collective-permute-start.8 = (f32[128,256]{1,0:T(8,128)S(1)}, f32[128,256]{1,0:T(8,128)S(1)}, u32[]{:S(2)}, u32[]{:S(2)}) collective-permute-start(f32[128,256]{1,0:T(8,128)S(1)} %get-tuple-element.35.refs_0_), channel_id=1, source_target_pairs={{0,2},{2,0},{1,3},{3,1},{4,6},{6,4},{5,7},{7,5},{8,10},{10,8},{9,1... | collective-permute-start | bytes 393224 | tf_op jit(solution)/shard_map/ppermute | solution.py:208
  35.8 0.0 collective-permute-start.7
  35.8 3.5 %collective-permute-done.8.refs_2_ = f32[128,256]{1,0:T(8,128)S(1)} collective-permute-done((f32[128,256]{1,0:T(8,128)S(1)}, f32[128,256]{1,0:T(8,128)S(1)}, u32[]{:S(2)}, u32[]{:S(2)}) %collective-permute-start.8) | collective-permute-done | bytes 131104 | tf_op jit(solution)/shard_map/ppermute | solution.py:208
  39.3 0.0 collective-permute-start.9
  39.3 0.0 collective-permute-done.7.refs_1_
  39.3 1.3 %collective-permute-done.9.refs_3_ = f32[128,256]{1,0:T(8,128)S(1)} collective-permute-done((f32[128,256]{1,0:T(8,128)S(1)}, f32[128,256]{1,0:T(8,128)S(1)}, u32[]{:S(2)}, u32[]{:S(2)}) %collective-permute-start.9) | collective-permute-done | bytes 131104 | tf_op jit(solution)/shard_map/ppermute | solution.py:208
  40.7 1.6 %corner.1 = (f32[8,128]{1,0:T(8,128)S(1)}, f32[256,256]{1,0:T(8,128)S(1)}, f32[8,128]{1,0:T(8,128)S(1)}) custom-call(f32[128,256]{1,0:T(8,128)S(1)} %get-tuple-element.35.refs_0_, f32[128,256]{1,0:T(8,128)S(1)} %collective-permute-done.7.refs_1_, f32[128,256]{1,0:T(8,128)S(1)} %collective-permute-done.8.refs_2_, ...), custom_call_target="tpu_custom_call" | custom-call | tf_op jit(solution)/shard_map/corner/pallas_call | solution.py:291
  42.3 0.2 collective-permute-start.10
  42.5 1.0 %collective-permute-done.10 = f32[8,128]{1,0:T(8,128)S(1)} collective-permute-done((f32[8,128]{1,0:T(8,128)S(1)}, f32[8,128]{1,0:T(8,128)S(1)}, u32[]{:S(2)}, u32[]{:S(2)}) %collective-permute-start.10) | collective-permute-done | bytes 4128 | tf_op jit(solution)/shard_map/ppermute | solution.py:208
  43.5 1.3 %collective-permute-start.11 = (f32[8,128]{1,0:T(8,128)S(1)}, f32[8,128]{1,0:T(8,128)S(1)}, u32[]{:S(2)}, u32[]{:S(2)}) collective-permute-start(f32[8,128]{1,0:T(8,128)S(1)} %add.27), channel_id=1, source_target_pairs={{0,3},{1,2},{2,1},{3,0},{4,7},{5,6},{6,5},{7,4},{8,11},{9,10},{10,... | collective-permute-start | bytes 12296 | tf_op jit(solution)/shard_map/ppermute | solution.py:213
  44.8 1.8 %collective-permute-done.11 = f32[8,128]{1,0:T(8,128)S(1)} collective-permute-done((f32[8,128]{1,0:T(8,128)S(1)}, f32[8,128]{1,0:T(8,128)S(1)}, u32[]{:S(2)}, u32[]{:S(2)}) %collective-permute-start.11) | collective-permute-done | bytes 4128 | tf_op jit(solution)/shard_map/ppermute | solution.py:213
  46.5 2.2 %collective-permute-start.14 = (f32[8,128]{1,0:T(8,128)S(1)}, f32[8,128]{1,0:T(8,128)S(1)}, u32[]{:S(2)}, u32[]{:S(2)}) collective-permute-start(f32[8,128]{1,0:T(8,128)S(1)} %add.28), channel_id=1, source_target_pairs={{0,13},{1,12},{4,9},{5,8},{8,5},{9,4},{12,1},{13,0},{2,15},{3,14},... | collective-permute-start | bytes 12296 | tf_op jit(solution)/shard_map/ppermute | solution.py:213
  48.8 0.0 collective-permute-start.13
  48.8 1.6 %collective-permute-start.12 = (f32[8,128]{1,0:T(8,128)S(1)}, f32[8,128]{1,0:T(8,128)S(1)}, u32[]{:S(2)}, u32[]{:S(2)}) collective-permute-start(f32[8,128]{1,0:T(8,128)S(1)} %add.28), channel_id=1, source_target_pairs={{0,5},{1,4},{4,1},{5,0},{8,13},{9,12},{12,9},{13,8},{2,7},{3,6},{6... | collective-permute-start | bytes 12296 | tf_op jit(solution)/shard_map/ppermute | solution.py:213
  50.4 0.9 %collective-permute-done.14 = f32[8,128]{1,0:T(8,128)S(1)} collective-permute-done((f32[8,128]{1,0:T(8,128)S(1)}, f32[8,128]{1,0:T(8,128)S(1)}, u32[]{:S(2)}, u32[]{:S(2)}) %collective-permute-start.14) | collective-permute-done | bytes 4128 | tf_op jit(solution)/shard_map/ppermute | solution.py:213
  51.4 1.3 %collective-permute-done.13 = f32[8,128]{1,0:T(8,128)S(1)} collective-permute-done((f32[8,128]{1,0:T(8,128)S(1)}, f32[8,128]{1,0:T(8,128)S(1)}, u32[]{:S(2)}, u32[]{:S(2)}) %collective-permute-start.13) | collective-permute-done | bytes 4128 | tf_op jit(solution)/shard_map/ppermute | solution.py:213
  52.7 0.0 collective-permute-done.12
  52.7 0.8 %result.1 = (f32[1,256,256]{2,1,0:T(8,128)}, f32[1]{0:T(128)}) custom-call(f32[8,128]{1,0:T(8,128)S(1)} %add_add_fusion.sums_ref, f32[8,128]{1,0:T(8,128)S(1)} %get-tuple-element.38.info_ref, f32[2,256,256]{2,1,0:T(8,128)S(1)} %get-tuple-element.33.refs_4_.full_ref, f32[256,256]{1,0:T(8,128)S(1)} %get-tuple-element.39.fresh_ref), custom_call_target="tpu_custom_call" | custom-call | tf_op jit(solution)/shard_map/result/pallas_call | solution.py:305
  (7 shorter events, 0.1 us)
Async XLA Ops:
  0.6 4.0 %copy-start = (f32[1,256,256]{2,1,0:T(8,128)S(1)}, f32[1,256,256]{2,1,0:T(8,128)}, u32[]{:S(2)}) copy-start(f32[1,256,256]{2,1,0:T(8,128)} %diag_hbm.1) | copy-start | bytes 786436
  1.6 3.0 %copy-start.2 = (s32[2,2]{1,0:T(2,128)S(1)}, s32[2,2]{1,0:T(2,128)}, u32[]{:S(2)}) copy-start(s32[2,2]{1,0:T(2,128)} %sizes_ref.1) | copy-start | bytes 52
  1.6 3.0 %copy-start.3 = (s32[4,1]{0,1:T(1,128)S(1)}, s32[4,1]{0,1:T(1,128)}, u32[]{:S(2)}) copy-start(s32[4,1]{0,1:T(1,128)} %param.9) | copy-start | bytes 52
  1.6 6.5 %collective-permute-start = (f32[128,256]{1,0:T(8,128)S(1)}, f32[128,256]{1,0:T(8,128)S(1)}, u32[]{:S(2)}, u32[]{:S(2)}) collective-permute-start(f32[128,256]{1,0:T(8,128)S(1)} %dynamic-slice_bitcast_fusion), channel_id=1, source_target_pairs={{0,2},{2,0},{1,3},{3,1},{4,6},{6,4},{5,7},{7,5},{8,10},{10,8},{9,1... | collective-permute-start | bytes 393224 | tf_op jit(solution)/shard_map/ppermute | solution.py:208
  4.6 1.0 %copy-start.1 = (f32[1,256,256]{2,1,0:T(8,128)S(1)}, f32[1,256,256]{2,1,0:T(8,128)}, u32[]{:S(2)}) copy-start(f32[1,256,256]{2,1,0:T(8,128)} %psi_hbm.1) | copy-start | bytes 786436
  8.2 1.4 %collective-permute-start.1 = (f32[128,256]{1,0:T(8,128)S(1)}, f32[128,256]{1,0:T(8,128)S(1)}, u32[]{:S(2)}, u32[]{:S(2)}) collective-permute-start(f32[128,256]{1,0:T(8,128)S(1)} %bitcast_multiply_fusion.refs_0_), channel_id=1, source_target_pairs={{0,1},{1,0},{2,3},{3,2},{4,5},{5,4},{6,7},{7,6},{8,9},{9,8},{10,11... | collective-permute-start | bytes 393224 | tf_op jit(solution)/shard_map/ppermute | solution.py:208
  11.8 1.6 %collective-permute-start.2 = (f32[2,264,128]{2,1,0:T(8,128)S(1)}, f32[2,264,128]{2,1,0:T(8,128)S(1)}, u32[]{:S(2)}, u32[]{:S(2)}) collective-permute-start(f32[2,264,128]{2,1,0:T(8,128)S(1)} %get-tuple-element.32), channel_id=1, source_target_pairs={{0,1},{1,0},{2,3},{3,2},{4,5},{5,4},{6,7},{7,6},{8,9},{9,8},{10,11... | collective-permute-start | bytes 811016 | tf_op jit(solution)/shard_map/ppermute | solution.py:208
  13.5 5.7 %collective-permute-start.3 = (f32[264,128]{1,0:T(8,128)S(1)}, f32[264,128]{1,0:T(8,128)S(1)}, u32[]{:S(2)}, u32[]{:S(2)}) collective-permute-start(f32[264,128]{1,0:T(8,128)S(1)} %slice_bitcast_fusion), channel_id=1, source_target_pairs={{0,2},{2,0},{1,3},{3,1},{4,6},{6,4},{5,7},{7,5},{8,10},{10,8},{9,1... | collective-permute-start | bytes 405512 | tf_op jit(solution)/shard_map/ppermute | solution.py:208
  19.2 8.5 %collective-permute-start.6 = (f32[264,128]{1,0:T(8,128)S(1)}, f32[264,128]{1,0:T(8,128)S(1)}, u32[]{:S(2)}, u32[]{:S(2)}) collective-permute-start(f32[264,128]{1,0:T(8,128)S(1)} %fusion.refs_0_), channel_id=1, source_target_pairs={{0,12},{4,8},{8,4},{12,0},{1,13},{5,9},{9,5},{13,1},{2,14},{6,10},... | collective-permute-start | bytes 405512 | tf_op jit(solution)/shard_map/ppermute | solution.py:208
  23.1 10.9 %collective-permute-start.5 = (f32[264,128]{1,0:T(8,128)S(1)}, f32[264,128]{1,0:T(8,128)S(1)}, u32[]{:S(2)}, u32[]{:S(2)}) collective-permute-start(f32[264,128]{1,0:T(8,128)S(1)} %fusion.refs_0_), channel_id=1, source_target_pairs={{0,8},{4,12},{8,0},{12,4},{1,9},{5,13},{9,1},{13,5},{2,10},{6,14},... | collective-permute-start | bytes 405512 | tf_op jit(solution)/shard_map/ppermute | solution.py:208
  23.1 10.9 %collective-permute-start.4 = (f32[264,128]{1,0:T(8,128)S(1)}, f32[264,128]{1,0:T(8,128)S(1)}, u32[]{:S(2)}, u32[]{:S(2)}) collective-permute-start(f32[264,128]{1,0:T(8,128)S(1)} %fusion.refs_0_), channel_id=1, source_target_pairs={{0,4},{4,0},{8,12},{12,8},{1,5},{5,1},{9,13},{13,9},{2,6},{6,2},{1... | collective-permute-start | bytes 405512 | tf_op jit(solution)/shard_map/ppermute | solution.py:208
  34.3 5.0 %collective-permute-start.8 = (f32[128,256]{1,0:T(8,128)S(1)}, f32[128,256]{1,0:T(8,128)S(1)}, u32[]{:S(2)}, u32[]{:S(2)}) collective-permute-start(f32[128,256]{1,0:T(8,128)S(1)} %get-tuple-element.35.refs_0_), channel_id=1, source_target_pairs={{0,2},{2,0},{1,3},{3,1},{4,6},{6,4},{5,7},{7,5},{8,10},{10,8},{9,1... | collective-permute-start | bytes 393224 | tf_op jit(solution)/shard_map/ppermute | solution.py:208
  35.8 3.5 %collective-permute-start.7 = (f32[128,256]{1,0:T(8,128)S(1)}, f32[128,256]{1,0:T(8,128)S(1)}, u32[]{:S(2)}, u32[]{:S(2)}) collective-permute-start(f32[128,256]{1,0:T(8,128)S(1)} %get-tuple-element.35.refs_0_), channel_id=1, source_target_pairs={{0,1},{1,0},{2,3},{3,2},{4,5},{5,4},{6,7},{7,6},{8,9},{9,8},{10,11... | collective-permute-start | bytes 393224 | tf_op jit(solution)/shard_map/ppermute | solution.py:208
  39.3 1.3 %collective-permute-start.9 = (f32[128,256]{1,0:T(8,128)S(1)}, f32[128,256]{1,0:T(8,128)S(1)}, u32[]{:S(2)}, u32[]{:S(2)}) collective-permute-start(f32[128,256]{1,0:T(8,128)S(1)} %collective-permute-done.8.refs_2_), channel_id=1, source_target_pairs={{0,1},{1,0},{2,3},{3,2},{4,5},{5,4},{6,7},{7,6},{8,9},{9,8},{10,11... | collective-permute-start | bytes 393224 | tf_op jit(solution)/shard_map/ppermute | solution.py:208
  42.3 1.2 %collective-permute-start.10 = (f32[8,128]{1,0:T(8,128)S(1)}, f32[8,128]{1,0:T(8,128)S(1)}, u32[]{:S(2)}, u32[]{:S(2)}) collective-permute-start(f32[8,128]{1,0:T(8,128)S(1)} %get-tuple-element.37), channel_id=1, source_target_pairs={{0,1},{1,0},{2,3},{3,2},{4,5},{5,4},{6,7},{7,6},{8,9},{9,8},{10,11... | collective-permute-start | bytes 12296 | tf_op jit(solution)/shard_map/ppermute | solution.py:208
  43.5 3.0 %collective-permute-start.11 = (f32[8,128]{1,0:T(8,128)S(1)}, f32[8,128]{1,0:T(8,128)S(1)}, u32[]{:S(2)}, u32[]{:S(2)}) collective-permute-start(f32[8,128]{1,0:T(8,128)S(1)} %add.27), channel_id=1, source_target_pairs={{0,3},{1,2},{2,1},{3,0},{4,7},{5,6},{6,5},{7,4},{8,11},{9,10},{10,... | collective-permute-start | bytes 12296 | tf_op jit(solution)/shard_map/ppermute | solution.py:213
  46.5 4.8 %collective-permute-start.14 = (f32[8,128]{1,0:T(8,128)S(1)}, f32[8,128]{1,0:T(8,128)S(1)}, u32[]{:S(2)}, u32[]{:S(2)}) collective-permute-start(f32[8,128]{1,0:T(8,128)S(1)} %add.28), channel_id=1, source_target_pairs={{0,13},{1,12},{4,9},{5,8},{8,5},{9,4},{12,1},{13,0},{2,15},{3,14},... | collective-permute-start | bytes 12296 | tf_op jit(solution)/shard_map/ppermute | solution.py:213
  48.8 3.9 %collective-permute-start.13 = (f32[8,128]{1,0:T(8,128)S(1)}, f32[8,128]{1,0:T(8,128)S(1)}, u32[]{:S(2)}, u32[]{:S(2)}) collective-permute-start(f32[8,128]{1,0:T(8,128)S(1)} %add.28), channel_id=1, source_target_pairs={{0,9},{1,8},{4,13},{5,12},{8,1},{9,0},{12,5},{13,4},{2,11},{3,10},... | collective-permute-start | bytes 12296 | tf_op jit(solution)/shard_map/ppermute | solution.py:213
  48.8 3.9 %collective-permute-start.12 = (f32[8,128]{1,0:T(8,128)S(1)}, f32[8,128]{1,0:T(8,128)S(1)}, u32[]{:S(2)}, u32[]{:S(2)}) collective-permute-start(f32[8,128]{1,0:T(8,128)S(1)} %add.28), channel_id=1, source_target_pairs={{0,5},{1,4},{4,1},{5,0},{8,13},{9,12},{12,9},{13,8},{2,7},{3,6},{6... | collective-permute-start | bytes 12296 | tf_op jit(solution)/shard_map/ppermute | solution.py:213

commit v3 on v2

--- a/solution.py
+++ b/solution.py
@@ -128,19 +128,16 @@
             ref[slot, blk // LANES * half :, :] = jnp.broadcast_to(scalar, (PAD, LANES))
 
 
-def fresh_kernel(ncell, nparts, *refs):
-    parts = refs[:nparts]
-    full_ref, mask_ref, diag_ref, norm_ref, fresh_ref, cross_ref = refs[nparts:]
-    half, blk = fresh_ref.shape
+def fresh_kernel(ncell, ntile, *refs):
+    parts = refs[: 2 * ntile]
+    full_ref, mask_ref, diag_ref, norm_ref, fresh_ref, cross_ref = refs[2 * ntile :]
+    half = fresh_ref.shape[0]
     mine, _ = halves_of(half)
     norm = norm_ref[:1, :1]
     scale = 1.0 / jnp.sqrt(norm)
-    summed = parts[0][...]
-    for part in parts[1:]:
-        summed = summed + part[...]
-    tiles = blk // LANES
-    theta = summed[tiles * half : tiles * half + 1, :1] / (ncell * norm)
-    summed = jnp.concatenate([summed[tile * half : (tile + 1) * half] for tile in range(tiles)], axis=1)
+    sums = [parts[2 * tile][...] + parts[2 * tile + 1][...] for tile in range(ntile)]
+    theta = sums[-1][half : half + 1, :1] / (ncell * norm)
+    summed = jnp.concatenate([tile[:half] for tile in sums], axis=1)
     trial = full_ref[0, mine, :] * scale
     diag = diag_ref[mine, :]
     image = (diag * trial + summed * scale) * mask_ref[0]
@@ -271,14 +268,23 @@
     )(*halves, own, slots, stat, lh, ll, th, tl, rh, rl)
 
     chip = keep + across(send, "rep", 1)
-    part = chip[0]
-    for step in range(1, nsec):
-        part = part + across(chip[step], "sector", step)
-    parts = [part] + [across(part, "terms", step) for step in range(1, nz)]
+    ntile = blk // LANES
+    bounds = [tile * half for tile in range(ntile)] + [ntile * half + PAD]
+    parts = []
+    for tile, (low, high) in enumerate(zip(bounds[:-1], bounds[1:])):
+        part = chip[0, low:high]
+        for step in range(1, nsec):
+            part = part + across(chip[step, low:high], "sector", step)
+        steps = [1 << bit for bit in range(nz.bit_length() - 1)]
+        if tile % 2:
+            steps.reverse()
+        for step in steps[:-1]:
+            part = part + across(part, "terms", step)
+        parts += [part, across(part, "terms", steps[-1])]
     fresh, cross = pl.pallas_call(
-        functools.partial(fresh_kernel, ncell, nz),
+        functools.partial(fresh_kernel, ncell, ntile),
         out_shape=[shape((half, blk), F32), shape((8, 128), F32)],
-        in_specs=[vmem] * (nz + 4),
+        in_specs=[vmem] * (len(parts) + 4),
         out_specs=[vmem] * 2,
         compiler_params=PARAMS,
         name="fresh",

time: 53.8 us -> 50.8 us (0.944)
  waiting for transfers between devices: 26.9 us -> 18 us
  starting transfers between devices: 16.6 us -> 22.5 us
    ppermute x11 -> x13, waiting for transfers between devices: 22.9 us -> 14.1 us  [across(): return lax.ppermute(x, axis, [(i, i ^ step) for i in range(size)])]
    ppermute x11 -> x13, starting transfers between devices: 11.4 us -> 17.3 us  [across(): return lax.ppermute(x, axis, [(i, i ^ step) for i in range(size)])]
  transfers between devices with their start and end apart: 15 -> 17, of which waited for: 12 -> 13; matrix products, arithmetic and copies ran while one was open for 0% -> 0% of each run, Pallas kernels for 4% -> 5%
where the time goes in v3:
time: 50.8 us; the launch traced here: 50.6 us
  starting transfers between devices  22.5 us (44%)
  waiting for transfers between devices  18 us (35%)
  Pallas kernels  7.3 us (14%)
  local copies, waits for them, and re-layouts  1.93 us (4%)
  between operations  0.75 us (1%)
    ppermute x13, starting transfers between devices, across(): return lax.ppermute(x, axis, [(i, i ^ step) for i in range(size)])  17.3 us
    ppermute x13, waiting for transfers between devices, across(): return lax.ppermute(x, axis, [(i, i ^ step) for i in range(size)])  14.1 us
    ppermute x4, starting transfers between devices, diagonally(): lax.ppermute(x, (axis, 'rep'), [(2 * i + c, 2 * (i ^ step) + 1 - c) for i...  5.22 us
    ppermute x4, waiting for transfers between devices, diagonally(): lax.ppermute(x, (axis, 'rep'), [(2 * i + c, 2 * (i ^ step) + 1 - c) for i...  3.89 us
    pallas_call x1, Pallas kernels, body(): pl.pallas_call(functools.partial(prepare_kernel, weight), out_shape=[shap...  2.4 us
    pallas_call x1, Pallas kernels, body(): pl.pallas_call(functools.partial(image_kernel, coupling, ncell, nsec), ou...  2.23 us
    pallas_call x1, Pallas kernels, body(): pl.pallas_call(functools.partial(corner_kernel, coupling, weight, ncell,...  1.58 us
  transfers between devices with their start and end apart: 17, of which 13 were waited for; matrix products, arithmetic and copies ran while one was open for 0% of the time, Pallas kernels for 5%

profile of v3, /device:TPU:0, one launch (start us, length us, event | category | flops | bytes accessed | tf_op | source)
XLA Modules:
  0.0 50.6 jit_solution(15677409864061574427)
XLA Ops:
  0.6 0.0 copy-start
  0.6 1.0 %dynamic-slice_bitcast_fusion = f32[128,256]{1,0:T(8,128)S(1)} fusion(f32[1,256,256]{2,1,0:T(8,128)} %psi_hbm.1, s32[]{:T(128)S(6)} %select_n.3), kind=kLoop, calls=%fused_computation.1 | loop fusion | bytes 262148 | tf_op jit(solution)/shard_map/dynamic_slice | solution.py:226
  1.6 0.0 copy-start.2
  1.6 0.0 copy-start.3
  1.6 3.0 %collective-permute-start = (f32[128,256]{1,0:T(8,128)S(1)}, f32[128,256]{1,0:T(8,128)S(1)}, u32[]{:S(2)}, u32[]{:S(2)}) collective-permute-start(f32[128,256]{1,0:T(8,128)S(1)} %dynamic-slice_bitcast_fusion), channel_id=1, source_target_pairs={{0,2},{2,0},{1,3},{3,1},{4,6},{6,4},{5,7},{7,5},{8,10},{10,8},{9,1... | collective-permute-start | bytes 393224 | tf_op jit(solution)/shard_map/ppermute | solution.py:205
  4.6 0.0 copy-done
  4.6 0.0 copy-done.2
  4.6 0.0 copy-done.3
  4.6 0.0 copy-start.1
  4.6 0.9 %copy-done.1 = f32[1,256,256]{2,1,0:T(8,128)S(1)} copy-done((f32[1,256,256]{2,1,0:T(8,128)S(1)}, f32[1,256,256]{2,1,0:T(8,128)}, u32[]{:S(2)}) %copy-start.1) | copy-done | bytes 262168
  5.6 2.4 %prepare.1 = (bf16[4,256,256]{2,1,0:T(8,128)(2,1)S(1)}, bf16[4,256,256]{2,1,0:T(8,128)(2,1)S(1)}, bf16[4,256,256]{2,1,0:T(8,128)(2,1)S(1)}, bf16[4,256,256]{2,1,...) custom-call(s32[2,2]{1,0:T(2,128)S(1)} %copy-done.2, ...), custom_call_target="tpu_custom_call" | custom-call | tf_op jit(solution)/shard_map/prepare/pallas_call | solution.py:233
  8.0 0.1 collective-permute-done
  8.2 0.1 collective-permute-start.1
  8.2 1.3 %collective-permute-done.1.refs_1_ = f32[128,256]{1,0:T(8,128)S(1)} collective-permute-done((f32[128,256]{1,0:T(8,128)S(1)}, f32[128,256]{1,0:T(8,128)S(1)}, u32[]{:S(2)}, u32[]{:S(2)}) %collective-permute-start.1) | collective-permute-done | bytes 131104 | tf_op jit(solution)/shard_map/ppermute | solution.py:205
  9.6 2.2 %image.1 = (f32[2,264,128]{2,1,0:T(8,128)S(1)}, f32[2,264,128]{2,1,0:T(8,128)S(1)}, f32[2,256,256]{2,1,0:T(8,128)S(1)}, f32[8,128]{1,0:T(8,128)S(1)}) custom-call(f32[128,256]{1,0:T(8,128)S(1)} %bitcast_multiply_fusion.refs_0_, f32[128,256]{1,0:T(8,128)S(1)} %collective-permute-done.1.refs_1_, f32[256,256]{1,0:T(8,128)S(1)} %get-tuple-element.22.refs_2_, ...), custom_call_target="tpu_custom_call" | custom-call | tf_op jit(solution)/shard_map/image/pallas_call | solution.py:255
  11.8 0.2 collective-permute-start.2
  12.0 1.4 %collective-permute-done.2 = f32[2,264,128]{2,1,0:T(8,128)S(1)} collective-permute-done((f32[2,264,128]{2,1,0:T(8,128)S(1)}, f32[2,264,128]{2,1,0:T(8,128)S(1)}, u32[]{:S(2)}, u32[]{:S(2)}) %collective-permute-start.2) | collective-permute-done | bytes 270368 | tf_op jit(solution)/shard_map/ppermute | solution.py:205
  13.5 1.8 %collective-permute-start.6 = (f32[136,128]{1,0:T(8,128)S(1)}, f32[136,128]{1,0:T(8,128)S(1)}, u32[]{:S(2)}, u32[]{:S(2)}) collective-permute-start(f32[136,128]{1,0:T(8,128)S(1)} %slice_bitcast_fusion), channel_id=1, source_target_pairs={{0,2},{2,0},{1,3},{3,1},{4,6},{6,4},{5,7},{7,5},{8,10},{10,8},{9,1... | collective-permute-start | bytes 208904 | tf_op jit(solution)/shard_map/ppermute | solution.py:205
  15.3 0.3 collective-permute-start.3
  15.6 2.4 %collective-permute-done.6 = f32[136,128]{1,0:T(8,128)S(1)} collective-permute-done((f32[136,128]{1,0:T(8,128)S(1)}, f32[136,128]{1,0:T(8,128)S(1)}, u32[]{:S(2)}, u32[]{:S(2)}) %collective-permute-start.6) | collective-permute-done | bytes 69664 | tf_op jit(solution)/shard_map/ppermute | solution.py:205
  18.0 3.2 %collective-permute-start.7 = (f32[136,128]{1,0:T(8,128)S(1)}, f32[136,128]{1,0:T(8,128)S(1)}, u32[]{:S(2)}, u32[]{:S(2)}) collective-permute-start(f32[136,128]{1,0:T(8,128)S(1)} %fusion), channel_id=1, source_target_pairs={{0,8},{4,12},{8,0},{12,4},{1,9},{5,13},{9,1},{13,5},{2,10},{6,14},... | collective-permute-start | bytes 208904 | tf_op jit(solution)/shard_map/ppermute | solution.py:205
  21.2 0.0 collective-permute-done.3
  21.2 1.6 %collective-permute-start.4 = (f32[128,128]{1,0:T(8,128)S(1)}, f32[128,128]{1,0:T(8,128)S(1)}, u32[]{:S(2)}, u32[]{:S(2)}) collective-permute-start(f32[128,128]{1,0:T(8,128)S(1)} %fusion.1), channel_id=1, source_target_pairs={{0,4},{4,0},{8,12},{12,8},{1,5},{5,1},{9,13},{13,9},{2,6},{6,2},{1... | collective-permute-start | bytes 196616 | tf_op jit(solution)/shard_map/ppermute | solution.py:205
  22.9 0.7 %collective-permute-done.7 = f32[136,128]{1,0:T(8,128)S(1)} collective-permute-done((f32[136,128]{1,0:T(8,128)S(1)}, f32[136,128]{1,0:T(8,128)S(1)}, u32[]{:S(2)}, u32[]{:S(2)}) %collective-permute-start.7) | collective-permute-done | bytes 69664 | tf_op jit(solution)/shard_map/ppermute | solution.py:205
  23.6 1.9 %collective-permute-start.8 = (f32[136,128]{1,0:T(8,128)S(1)}, f32[136,128]{1,0:T(8,128)S(1)}, u32[]{:S(2)}, u32[]{:S(2)}) collective-permute-start(f32[136,128]{1,0:T(8,128)S(1)} %add.38.refs_2_), channel_id=1, source_target_pairs={{0,4},{4,0},{8,12},{12,8},{1,5},{5,1},{9,13},{13,9},{2,6},{6,2},{1... | collective-permute-start | bytes 208904 | tf_op jit(solution)/shard_map/ppermute | solution.py:205
  25.5 0.1 collective-permute-done.4
  25.6 3.3 %collective-permute-start.5 = (f32[128,128]{1,0:T(8,128)S(1)}, f32[128,128]{1,0:T(8,128)S(1)}, u32[]{:S(2)}, u32[]{:S(2)}) collective-permute-start(f32[128,128]{1,0:T(8,128)S(1)} %add.36.refs_0_), channel_id=1, source_target_pairs={{0,8},{4,12},{8,0},{12,4},{1,9},{5,13},{9,1},{13,5},{2,10},{6,14},... | collective-permute-start | bytes 196616 | tf_op jit(solution)/shard_map/ppermute | solution.py:205
  28.9 2.3 %collective-permute-done.5.refs_1_ = f32[128,128]{1,0:T(8,128)S(1)} collective-permute-done((f32[128,128]{1,0:T(8,128)S(1)}, f32[128,128]{1,0:T(8,128)S(1)}, u32[]{:S(2)}, u32[]{:S(2)}) %collective-permute-start.5) | collective-permute-done | bytes 65568 | tf_op jit(solution)/shard_map/ppermute | solution.py:205
  31.1 0.0 collective-permute-done.8.refs_3_
  31.1 0.3 fresh.1
  31.4 1.6 %collective-permute-start.10 = (f32[128,256]{1,0:T(8,128)S(1)}, f32[128,256]{1,0:T(8,128)S(1)}, u32[]{:S(2)}, u32[]{:S(2)}) collective-permute-start(f32[128,256]{1,0:T(8,128)S(1)} %get-tuple-element.35.refs_0_), channel_id=1, source_target_pairs={{0,2},{2,0},{1,3},{3,1},{4,6},{6,4},{5,7},{7,5},{8,10},{10,8},{9,1... | collective-permute-start | bytes 393224 | tf_op jit(solution)/shard_map/ppermute | solution.py:205
  33.0 0.0 collective-permute-start.9
  33.0 3.4 %collective-permute-done.10.refs_2_ = f32[128,256]{1,0:T(8,128)S(1)} collective-permute-done((f32[128,256]{1,0:T(8,128)S(1)}, f32[128,256]{1,0:T(8,128)S(1)}, u32[]{:S(2)}, u32[]{:S(2)}) %collective-permute-start.10) | collective-permute-done | bytes 131104 | tf_op jit(solution)/shard_map/ppermute | solution.py:205
  36.4 0.0 collective-permute-start.11
  36.4 0.0 collective-permute-done.9.refs_1_
  36.4 1.3 %collective-permute-done.11.refs_3_ = f32[128,256]{1,0:T(8,128)S(1)} collective-permute-done((f32[128,256]{1,0:T(8,128)S(1)}, f32[128,256]{1,0:T(8,128)S(1)}, u32[]{:S(2)}, u32[]{:S(2)}) %collective-permute-start.11) | collective-permute-done | bytes 131104 | tf_op jit(solution)/shard_map/ppermute | solution.py:205
  37.8 1.6 %corner.1 = (f32[8,128]{1,0:T(8,128)S(1)}, f32[256,256]{1,0:T(8,128)S(1)}, f32[8,128]{1,0:T(8,128)S(1)}) custom-call(f32[128,256]{1,0:T(8,128)S(1)} %get-tuple-element.35.refs_0_, f32[128,256]{1,0:T(8,128)S(1)} %collective-permute-done.9.refs_1_, f32[128,256]{1,0:T(8,128)S(1)} %collective-permute-done.10.refs_2_, ...), custom_call_target="tpu_custom_call" | custom-call | tf_op jit(solution)/shard_map/corner/pallas_call | solution.py:297
  39.4 0.2 collective-permute-start.12
  39.6 1.0 %collective-permute-done.12 = f32[8,128]{1,0:T(8,128)S(1)} collective-permute-done((f32[8,128]{1,0:T(8,128)S(1)}, f32[8,128]{1,0:T(8,128)S(1)}, u32[]{:S(2)}, u32[]{:S(2)}) %collective-permute-start.12) | collective-permute-done | bytes 4128 | tf_op jit(solution)/shard_map/ppermute | solution.py:205
  40.6 1.3 %collective-permute-start.13 = (f32[8,128]{1,0:T(8,128)S(1)}, f32[8,128]{1,0:T(8,128)S(1)}, u32[]{:S(2)}, u32[]{:S(2)}) collective-permute-start(f32[8,128]{1,0:T(8,128)S(1)} %add.39), channel_id=1, source_target_pairs={{0,3},{1,2},{2,1},{3,0},{4,7},{5,6},{6,5},{7,4},{8,11},{9,10},{10,... | collective-permute-start | bytes 12296 | tf_op jit(solution)/shard_map/ppermute | solution.py:210
  41.9 1.7 %collective-permute-done.13 = f32[8,128]{1,0:T(8,128)S(1)} collective-permute-done((f32[8,128]{1,0:T(8,128)S(1)}, f32[8,128]{1,0:T(8,128)S(1)}, u32[]{:S(2)}, u32[]{:S(2)}) %collective-permute-start.13) | collective-permute-done | bytes 4128 | tf_op jit(solution)/shard_map/ppermute | solution.py:210
  43.6 2.1 %collective-permute-start.16 = (f32[8,128]{1,0:T(8,128)S(1)}, f32[8,128]{1,0:T(8,128)S(1)}, u32[]{:S(2)}, u32[]{:S(2)}) collective-permute-start(f32[8,128]{1,0:T(8,128)S(1)} %add.40), channel_id=1, source_target_pairs={{0,13},{1,12},{4,9},{5,8},{8,5},{9,4},{12,1},{13,0},{2,15},{3,14},... | collective-permute-start | bytes 12296 | tf_op jit(solution)/shard_map/ppermute | solution.py:210
  45.8 0.5 %collective-permute-start.15 = (f32[8,128]{1,0:T(8,128)S(1)}, f32[8,128]{1,0:T(8,128)S(1)}, u32[]{:S(2)}, u32[]{:S(2)}) collective-permute-start(f32[8,128]{1,0:T(8,128)S(1)} %add.40), channel_id=1, source_target_pairs={{0,9},{1,8},{4,13},{5,12},{8,1},{9,0},{12,5},{13,4},{2,11},{3,10},... | collective-permute-start | bytes 12296 | tf_op jit(solution)/shard_map/ppermute | solution.py:210
  46.3 1.2 %collective-permute-start.14 = (f32[8,128]{1,0:T(8,128)S(1)}, f32[8,128]{1,0:T(8,128)S(1)}, u32[]{:S(2)}, u32[]{:S(2)}) collective-permute-start(f32[8,128]{1,0:T(8,128)S(1)} %add.40), channel_id=1, source_target_pairs={{0,5},{1,4},{4,1},{5,0},{8,13},{9,12},{12,9},{13,8},{2,7},{3,6},{6... | collective-permute-start | bytes 12296 | tf_op jit(solution)/shard_map/ppermute | solution.py:210
  47.5 0.9 %collective-permute-done.16 = f32[8,128]{1,0:T(8,128)S(1)} collective-permute-done((f32[8,128]{1,0:T(8,128)S(1)}, f32[8,128]{1,0:T(8,128)S(1)}, u32[]{:S(2)}, u32[]{:S(2)}) %collective-permute-start.16) | collective-permute-done | bytes 4128 | tf_op jit(solution)/shard_map/ppermute | solution.py:210
  48.5 1.2 %collective-permute-done.15 = f32[8,128]{1,0:T(8,128)S(1)} collective-permute-done((f32[8,128]{1,0:T(8,128)S(1)}, f32[8,128]{1,0:T(8,128)S(1)}, u32[]{:S(2)}, u32[]{:S(2)}) %collective-permute-start.15) | collective-permute-done | bytes 4128 | tf_op jit(solution)/shard_map/ppermute | solution.py:210
  49.7 0.0 collective-permute-done.14
  49.7 0.8 %result.1 = (f32[1,256,256]{2,1,0:T(8,128)}, f32[1]{0:T(128)}) custom-call(f32[8,128]{1,0:T(8,128)S(1)} %add_add_fusion.sums_ref, f32[8,128]{1,0:T(8,128)S(1)} %get-tuple-element.38.info_ref, f32[2,256,256]{2,1,0:T(8,128)S(1)} %get-tuple-element.33.refs_4_.full_ref, f32[256,256]{1,0:T(8,128)S(1)} %get-tuple-element.39.fresh_ref), custom_call_target="tpu_custom_call" | custom-call | tf_op jit(solution)/shard_map/result/pallas_call | solution.py:311
  (11 shorter events, 0.1 us)
Async XLA Ops:
  0.6 4.0 %copy-start = (f32[1,256,256]{2,1,0:T(8,128)S(1)}, f32[1,256,256]{2,1,0:T(8,128)}, u32[]{:S(2)}) copy-start(f32[1,256,256]{2,1,0:T(8,128)} %diag_hbm.1) | copy-start | bytes 786436
  1.6 3.0 %copy-start.2 = (s32[2,2]{1,0:T(2,128)S(1)}, s32[2,2]{1,0:T(2,128)}, u32[]{:S(2)}) copy-start(s32[2,2]{1,0:T(2,128)} %sizes_ref.1) | copy-start | bytes 52
  1.6 3.0 %copy-start.3 = (s32[4,1]{0,1:T(1,128)S(1)}, s32[4,1]{0,1:T(1,128)}, u32[]{:S(2)}) copy-start(s32[4,1]{0,1:T(1,128)} %param.9) | copy-start | bytes 52
  1.6 6.5 %collective-permute-start = (f32[128,256]{1,0:T(8,128)S(1)}, f32[128,256]{1,0:T(8,128)S(1)}, u32[]{:S(2)}, u32[]{:S(2)}) collective-permute-start(f32[128,256]{1,0:T(8,128)S(1)} %dynamic-slice_bitcast_fusion), channel_id=1, source_target_pairs={{0,2},{2,0},{1,3},{3,1},{4,6},{6,4},{5,7},{7,5},{8,10},{10,8},{9,1... | collective-permute-start | bytes 393224 | tf_op jit(solution)/shard_map/ppermute | solution.py:205
  4.6 1.0 %copy-start.1 = (f32[1,256,256]{2,1,0:T(8,128)S(1)}, f32[1,256,256]{2,1,0:T(8,128)}, u32[]{:S(2)}) copy-start(f32[1,256,256]{2,1,0:T(8,128)} %psi_hbm.1) | copy-start | bytes 786436
  8.2 1.4 %collective-permute-start.1 = (f32[128,256]{1,0:T(8,128)S(1)}, f32[128,256]{1,0:T(8,128)S(1)}, u32[]{:S(2)}, u32[]{:S(2)}) collective-permute-start(f32[128,256]{1,0:T(8,128)S(1)} %bitcast_multiply_fusion.refs_0_), channel_id=1, source_target_pairs={{0,1},{1,0},{2,3},{3,2},{4,5},{5,4},{6,7},{7,6},{8,9},{9,8},{10,11... | collective-permute-start | bytes 393224 | tf_op jit(solution)/shard_map/ppermute | solution.py:205
  11.8 1.6 %collective-permute-start.2 = (f32[2,264,128]{2,1,0:T(8,128)S(1)}, f32[2,264,128]{2,1,0:T(8,128)S(1)}, u32[]{:S(2)}, u32[]{:S(2)}) collective-permute-start(f32[2,264,128]{2,1,0:T(8,128)S(1)} %get-tuple-element.32), channel_id=1, source_target_pairs={{0,1},{1,0},{2,3},{3,2},{4,5},{5,4},{6,7},{7,6},{8,9},{9,8},{10,11... | collective-permute-start | bytes 811016 | tf_op jit(solution)/shard_map/ppermute | solution.py:205
  13.5 4.5 %collective-permute-start.6 = (f32[136,128]{1,0:T(8,128)S(1)}, f32[136,128]{1,0:T(8,128)S(1)}, u32[]{:S(2)}, u32[]{:S(2)}) collective-permute-start(f32[136,128]{1,0:T(8,128)S(1)} %slice_bitcast_fusion), channel_id=1, source_target_pairs={{0,2},{2,0},{1,3},{3,1},{4,6},{6,4},{5,7},{7,5},{8,10},{10,8},{9,1... | collective-permute-start | bytes 208904 | tf_op jit(solution)/shard_map/ppermute | solution.py:205
  15.3 5.9 %collective-permute-start.3 = (f32[128,128]{1,0:T(8,128)S(1)}, f32[128,128]{1,0:T(8,128)S(1)}, u32[]{:S(2)}, u32[]{:S(2)}) collective-permute-start(f32[128,128]{1,0:T(8,128)S(1)} %slice_bitcast_fusion.2), channel_id=1, source_target_pairs={{0,2},{2,0},{1,3},{3,1},{4,6},{6,4},{5,7},{7,5},{8,10},{10,8},{9,1... | collective-permute-start | bytes 196616 | tf_op jit(solution)/shard_map/ppermute | solution.py:205
  18.0 5.6 %collective-permute-start.7 = (f32[136,128]{1,0:T(8,128)S(1)}, f32[136,128]{1,0:T(8,128)S(1)}, u32[]{:S(2)}, u32[]{:S(2)}) collective-permute-start(f32[136,128]{1,0:T(8,128)S(1)} %fusion), channel_id=1, source_target_pairs={{0,8},{4,12},{8,0},{12,4},{1,9},{5,13},{9,1},{13,5},{2,10},{6,14},... | collective-permute-start | bytes 208904 | tf_op jit(solution)/shard_map/ppermute | solution.py:205
  21.2 4.3 %collective-permute-start.4 = (f32[128,128]{1,0:T(8,128)S(1)}, f32[128,128]{1,0:T(8,128)S(1)}, u32[]{:S(2)}, u32[]{:S(2)}) collective-permute-start(f32[128,128]{1,0:T(8,128)S(1)} %fusion.1), channel_id=1, source_target_pairs={{0,4},{4,0},{8,12},{12,8},{1,5},{5,1},{9,13},{13,9},{2,6},{6,2},{1... | collective-permute-start | bytes 196616 | tf_op jit(solution)/shard_map/ppermute | solution.py:205
  23.6 7.5 %collective-permute-start.8 = (f32[136,128]{1,0:T(8,128)S(1)}, f32[136,128]{1,0:T(8,128)S(1)}, u32[]{:S(2)}, u32[]{:S(2)}) collective-permute-start(f32[136,128]{1,0:T(8,128)S(1)} %add.38.refs_2_), channel_id=1, source_target_pairs={{0,4},{4,0},{8,12},{12,8},{1,5},{5,1},{9,13},{13,9},{2,6},{6,2},{1... | collective-permute-start | bytes 208904 | tf_op jit(solution)/shard_map/ppermute | solution.py:205
  25.6 5.6 %collective-permute-start.5 = (f32[128,128]{1,0:T(8,128)S(1)}, f32[128,128]{1,0:T(8,128)S(1)}, u32[]{:S(2)}, u32[]{:S(2)}) collective-permute-start(f32[128,128]{1,0:T(8,128)S(1)} %add.36.refs_0_), channel_id=1, source_target_pairs={{0,8},{4,12},{8,0},{12,4},{1,9},{5,13},{9,1},{13,5},{2,10},{6,14},... | collective-permute-start | bytes 196616 | tf_op jit(solution)/shard_map/ppermute | solution.py:205
  31.4 5.0 %collective-permute-start.10 = (f32[128,256]{1,0:T(8,128)S(1)}, f32[128,256]{1,0:T(8,128)S(1)}, u32[]{:S(2)}, u32[]{:S(2)}) collective-permute-start(f32[128,256]{1,0:T(8,128)S(1)} %get-tuple-element.35.refs_0_), channel_id=1, source_target_pairs={{0,2},{2,0},{1,3},{3,1},{4,6},{6,4},{5,7},{7,5},{8,10},{10,8},{9,1... | collective-permute-start | bytes 393224 | tf_op jit(solution)/shard_map/ppermute | solution.py:205
  33.0 3.4 %collective-permute-start.9 = (f32[128,256]{1,0:T(8,128)S(1)}, f32[128,256]{1,0:T(8,128)S(1)}, u32[]{:S(2)}, u32[]{:S(2)}) collective-permute-start(f32[128,256]{1,0:T(8,128)S(1)} %get-tuple-element.35.refs_0_), channel_id=1, source_target_pairs={{0,1},{1,0},{2,3},{3,2},{4,5},{5,4},{6,7},{7,6},{8,9},{9,8},{10,11... | collective-permute-start | bytes 393224 | tf_op jit(solution)/shard_map/ppermute | solution.py:205
  36.4 1.3 %collective-permute-start.11 = (f32[128,256]{1,0:T(8,128)S(1)}, f32[128,256]{1,0:T(8,128)S(1)}, u32[]{:S(2)}, u32[]{:S(2)}) collective-permute-start(f32[128,256]{1,0:T(8,128)S(1)} %collective-permute-done.10.refs_2_), channel_id=1, source_target_pairs={{0,1},{1,0},{2,3},{3,2},{4,5},{5,4},{6,7},{7,6},{8,9},{9,8},{10,11... | collective-permute-start | bytes 393224 | tf_op jit(solution)/shard_map/ppermute | solution.py:205
  39.4 1.2 %collective-permute-start.12 = (f32[8,128]{1,0:T(8,128)S(1)}, f32[8,128]{1,0:T(8,128)S(1)}, u32[]{:S(2)}, u32[]{:S(2)}) collective-permute-start(f32[8,128]{1,0:T(8,128)S(1)} %get-tuple-element.37), channel_id=1, source_target_pairs={{0,1},{1,0},{2,3},{3,2},{4,5},{5,4},{6,7},{7,6},{8,9},{9,8},{10,11... | collective-permute-start | bytes 12296 | tf_op jit(solution)/shard_map/ppermute | solution.py:205
  40.6 3.0 %collective-permute-start.13 = (f32[8,128]{1,0:T(8,128)S(1)}, f32[8,128]{1,0:T(8,128)S(1)}, u32[]{:S(2)}, u32[]{:S(2)}) collective-permute-start(f32[8,128]{1,0:T(8,128)S(1)} %add.39), channel_id=1, source_target_pairs={{0,3},{1,2},{2,1},{3,0},{4,7},{5,6},{6,5},{7,4},{8,11},{9,10},{10,... | collective-permute-start | bytes 12296 | tf_op jit(solution)/shard_map/ppermute | solution.py:210
  43.6 4.8 %collective-permute-start.16 = (f32[8,128]{1,0:T(8,128)S(1)}, f32[8,128]{1,0:T(8,128)S(1)}, u32[]{:S(2)}, u32[]{:S(2)}) collective-permute-start(f32[8,128]{1,0:T(8,128)S(1)} %add.40), channel_id=1, source_target_pairs={{0,13},{1,12},{4,9},{5,8},{8,5},{9,4},{12,1},{13,0},{2,15},{3,14},... | collective-permute-start | bytes 12296 | tf_op jit(solution)/shard_map/ppermute | solution.py:210
  45.8 3.9 %collective-permute-start.15 = (f32[8,128]{1,0:T(8,128)S(1)}, f32[8,128]{1,0:T(8,128)S(1)}, u32[]{:S(2)}, u32[]{:S(2)}) collective-permute-start(f32[8,128]{1,0:T(8,128)S(1)} %add.40), channel_id=1, source_target_pairs={{0,9},{1,8},{4,13},{5,12},{8,1},{9,0},{12,5},{13,4},{2,11},{3,10},... | collective-permute-start | bytes 12296 | tf_op jit(solution)/shard_map/ppermute | solution.py:210
  46.3 3.4 %collective-permute-start.14 = (f32[8,128]{1,0:T(8,128)S(1)}, f32[8,128]{1,0:T(8,128)S(1)}, u32[]{:S(2)}, u32[]{:S(2)}) collective-permute-start(f32[8,128]{1,0:T(8,128)S(1)} %add.40), channel_id=1, source_target_pairs={{0,5},{1,4},{4,1},{5,0},{8,13},{9,12},{12,9},{13,8},{2,7},{3,6},{6... | collective-permute-start | bytes 12296 | tf_op jit(solution)/shard_map/ppermute | solution.py:210

commit v4 on v3

--- a/solution.py
+++ b/solution.py
@@ -23,9 +23,17 @@
     return high, (x - high.astype(F32)).astype(BF16)
 
 
+def dot(a, b):
+    return lax.dot_general(a, b, NN, preferred_element_type=F32)
+
+
+def half_product(a, b):
+    return dot(jnp.concatenate(a, axis=1), jnp.concatenate([b[0], b[0]], axis=0)) + dot(a[0], b[1])
+
+
 def product(a, b, dims):
-    dot = functools.partial(lax.dot_general, dimension_numbers=dims, preferred_element_type=F32)
-    return dot(a[0], b[0]) + (dot(a[0], b[1]) + dot(a[1], b[0]))
+    one = functools.partial(lax.dot_general, dimension_numbers=dims, preferred_element_type=F32)
+    return one(a[0], b[0]) + (one(a[0], b[1]) + one(a[1], b[0]))
 
 
 def live_mask(sizes_ref, sector, first, rows, cols):
@@ -46,7 +54,7 @@
 
 
 def prepare_kernel(weight, sizes_ref, conn_ref, psi_hbm, diag_hbm, left_hbm, right_hbm, *refs):
-    lh, ll, th, tl, rh, rl, mask_ref, own_ref, slot_ref, stat_ref, psi, diag, left, right, vector_sem, left_sem, right_sem = refs
+    lh, ll, th, tl, rh, rl, mask_ref, own_ref, diag_ref, slot_ref, stat_ref, psi, diag, left, right, vector_sem, left_sem, right_sem = refs
     nterm = left.shape[0]
     vectors = [
         pltpu.make_async_copy(psi_hbm.at[0], psi, vector_sem.at[0]),
@@ -65,14 +73,20 @@
         slot_ref[term] = jnp.full(slot_ref.shape[1:], conn_ref[term] ^ me, jnp.int32)
     for copy in vectors:
         copy.wait()
-    own = psi[...] * live_mask(sizes_ref, me, 0, blk, blk)
-    own_ref[...] = own
-    square = own * own
+    core = lax.axis_index("rep")
+    mine, other = halves_of(half)
+    diag_ref[:half] = diag[mine, :]
+    diag_ref[half:] = diag[other, :]
+    own_ref[:half] = psi[mine, :] * mask_ref[0]
+    own_ref[half:] = psi[other, :] * live_mask(sizes_ref, me, (1 - core) * half, half, blk)
+    square = own_ref[...] * own_ref[...]
     row = lax.broadcasted_iota(jnp.int32, stat_ref.shape, 0)
-    stat_ref[...] = jnp.where(row == 0, total(square), total(square * diag[...]) * weight)
+    stat_ref[...] = jnp.where(row == 0, total(square), total(square * diag_ref[...]) * weight)
     for term in range(nterm):
         lefts[term].wait()
-        value = left[term]
+        value = jnp.concatenate([left[term, mine, :], left[term, other, :]], axis=0)
+        parts = value[:, :half], value[:, half:]
+        value = jnp.concatenate([jnp.where(core == 0, *parts), jnp.where(core == 0, *parts[::-1])], axis=1)
         lh[term], ll[term] = split(value)
         th[term], tl[term] = split(value.T)
     for term in range(nterm):
@@ -81,65 +95,91 @@
 
 
 def pick(slot_ref, term, blocks):
-    blk = blocks[0].shape[0]
-    slot = jnp.broadcast_to(slot_ref[term, :1, :], (blk, blk))
+    slot = jnp.broadcast_to(slot_ref[term, :1, :], blocks[0].shape)
     value = blocks[0]
     for index in range(1, len(blocks)):
         value = jnp.where(slot == index, blocks[index], value)
     return value
 
 
+def partial_kernel(nsec, *refs):
+    nears = refs[:nsec]
+    slot_ref, lh, ll, part_ref = refs[nsec:]
+    half = lh.shape[-1] // 2
+    blocks = [near[:half] for near in nears]
+    for i in range(lh.shape[0]):
+        part_ref[i] = half_product((lh[i, :, :half], ll[i, :, :half]), split(pick(slot_ref, i, blocks)))
+
+
+def sum_rows(coupling, first, slot_ref, th, tl, inner, joints, scalar, out_ref):
+    blk = th.shape[-1]
+    half = blk // 2
+    rows = slice(first, first + half)
+    terms = range(th.shape[0])
+    returned = [product((th[i, rows, :], tl[i, rows, :]), inner[i], NN) for i in terms]
+    for slot in range(out_ref.shape[0]):
+        value = coupling * sum([joint[rows] for joint in joints[1:]], joints[0][rows]) if slot == 0 else jnp.zeros((half, blk), F32)
+        for i in terms:
+            target = jnp.broadcast_to(slot_ref[i, :1, :], (half, blk))
+            value = value + jnp.where(target == slot, returned[i], 0.0)
+        for tile in range(blk // LANES):
+            out_ref[slot, tile * half : (tile + 1) * half, :] = value[:, tile * LANES : (tile + 1) * LANES]
+        out_ref[slot, blk // LANES * half :, :] = jnp.broadcast_to(scalar, (PAD, LANES))
+
+
+def keep_kernel(coupling, slot_ref, norm_ref, joint_ref, th, tl, ih, il, keep_ref):
+    terms = range(th.shape[0])
+    inner = [(ih[i], il[i]) for i in terms]
+    sum_rows(coupling, 0, slot_ref, th, tl, inner, [joint_ref.at[i] for i in terms], norm_ref[1:2, :1], keep_ref)
+
+
 def image_kernel(coupling, ncell, nsec, *refs):
     halves = refs[: 2 * (nsec - 1)]
-    own_ref, slot_ref, stat_ref = refs[2 * (nsec - 1) : 2 * (nsec - 1) + 3]
-    lh, ll, th, tl, rh, rl, keep_ref, send_ref, full_ref, norm_ref, acc = refs[2 * (nsec - 1) + 3 :]
+    own_ref, part_ref, slot_ref, stat_ref = refs[2 * (nsec - 1) : 2 * (nsec - 1) + 4]
+    lh, ll, th, tl, rh, rl, send_ref, full_ref, norm_ref, joint_ref, ih, il = refs[2 * (nsec - 1) + 4 :]
     blk = own_ref.shape[0]
     half = blk // 2
     nterm = lh.shape[0]
-    mine, other = halves_of(half)
     own = own_ref[...]
-    full_ref[0] = own
-    for slot in range(1, nsec):
-        full_ref[slot, mine, :] = halves[2 * slot - 2][...]
-        full_ref[slot, other, :] = halves[2 * slot - 1][...]
-    blocks = [own] + [full_ref[slot] for slot in range(1, nsec)]
+    blocks = [own] + [
+        jnp.concatenate([halves[2 * slot - 2][...], halves[2 * slot - 1][...]], axis=0) for slot in range(1, nsec)
+    ]
+    for slot in range(nsec):
+        full_ref[slot] = blocks[slot]
     norm = stat_ref[:1, :1]
     for block in blocks[1:]:
         norm = norm + total(block * block)
-    norm_ref[...] = jnp.broadcast_to(norm / ncell, norm_ref.shape)
     terms = range(nterm)
-    middles = [product((lh[i], ll[i]), split(pick(slot_ref, i, blocks)), NN) for i in terms]
+    fars = [block[half:] for block in blocks]
+    middles = [
+        part_ref[i] + half_product((lh[i, :, half:], ll[i, :, half:]), split(pick(slot_ref, i, fars))) for i in terms
+    ]
     joints = [coupling * own + product(split(middles[i]), (rh[i], rl[i]), NT) for i in terms]
     squares = joints[0] * joints[0]
     for joint in joints[1:]:
         squares = squares + joint * joint
+    for i in terms:
+        joint_ref[i] = joints[i]
     scalar = stat_ref[1:2, :1] + total(squares)
-    inner = [product(split(joints[i]), (rh[i], rl[i]), NN) for i in terms]
-    returned = [product((th[i], tl[i]), split(inner[i]), NN) for i in terms]
-    for slot in range(nsec):
-        value = coupling * sum(joints[1:], joints[0]) if slot == 0 else jnp.zeros((blk, blk), F32)
-        for i in terms:
-            target = jnp.broadcast_to(slot_ref[i, :1, :], (blk, blk))
-            value = value + jnp.where(target == slot, returned[i], 0.0)
-        acc[slot] = value
-        for ref, rows in ((keep_ref, mine), (send_ref, other)):
-            for tile in range(blk // LANES):
-                ref[slot, tile * half : (tile + 1) * half, :] = acc[slot, rows, tile * LANES : (tile + 1) * LANES]
-            ref[slot, blk // LANES * half :, :] = jnp.broadcast_to(scalar, (PAD, LANES))
+    row = lax.broadcasted_iota(jnp.int32, norm_ref.shape, 0)
+    norm_ref[...] = jnp.where(row == 0, norm / ncell, scalar)
+    inner = [split(product(split(joints[i]), (rh[i], rl[i]), NN)) for i in terms]
+    for i in terms:
+        ih[i], il[i] = inner[i]
+    sum_rows(coupling, half, slot_ref, th, tl, inner, joints, scalar, send_ref)
 
 
 def fresh_kernel(ncell, ntile, *refs):
     parts = refs[: 2 * ntile]
     full_ref, mask_ref, diag_ref, norm_ref, fresh_ref, cross_ref = refs[2 * ntile :]
     half = fresh_ref.shape[0]
-    mine, _ = halves_of(half)
     norm = norm_ref[:1, :1]
     scale = 1.0 / jnp.sqrt(norm)
     sums = [parts[2 * tile][...] + parts[2 * tile + 1][...] for tile in range(ntile)]
     theta = sums[-1][half : half + 1, :1] / (ncell * norm)
     summed = jnp.concatenate([tile[:half] for tile in sums], axis=1)
-    trial = full_ref[0, mine, :] * scale
-    diag = diag_ref[mine, :]
+    trial = full_ref[0, :half] * scale
+    diag = diag_ref[:half]
     image = (diag * trial + summed * scale) * mask_ref[0]
     residue = image - theta * trial
     shifted = diag - theta
@@ -150,34 +190,31 @@
 
 
 def corner_kernel(coupling, weight, ncell, share, nsec, *refs):
-    halves = refs[: 2 * nsec]
-    full_ref, diag_ref, norm_ref, cross_ref, slot_ref, lh, ll, rh, rl = refs[2 * nsec : 2 * nsec + 9]
-    sums_ref, fresh_ref, info_ref, work = refs[2 * nsec + 9 :]
-    blk = diag_ref.shape[0]
-    nterm = lh.shape[0]
-    mine, other = halves_of(blk // 2)
-    for slot in range(nsec):
-        work[slot, mine, :] = halves[2 * slot][...]
-        work[slot, other, :] = halves[2 * slot + 1][...]
+    nears, fars = refs[:nsec], refs[nsec : 2 * nsec]
+    part_ref, joint_ref, full_ref, diag_ref, norm_ref, cross_ref, slot_ref, lh, ll, rh, rl = refs[2 * nsec : 2 * nsec + 11]
+    sums_ref, fresh_ref, info_ref = refs[2 * nsec + 11 :]
+    half = nears[0].shape[0]
+    terms = range(lh.shape[0])
+    blocks = [far[...] for far in fars]
+    middles = [
+        part_ref[i] + half_product((lh[i, :, half:], ll[i, :, half:]), split(pick(slot_ref, i, blocks))) for i in terms
+    ]
     norm = norm_ref[:1, :1]
-    start = [full_ref[slot] for slot in range(nsec)]
-    raw = [work[slot] for slot in range(nsec)]
-    overlap = start[0] * raw[0]
+    raw = [jnp.concatenate([nears[slot][...], blocks[slot]], axis=0) for slot in range(nsec)]
+    overlap = full_ref[0] * raw[0]
     for slot in range(1, nsec):
-        overlap = overlap + start[slot] * raw[slot]
+        overlap = overlap + full_ref[slot] * raw[slot]
     overlap = total(overlap) / (ncell * norm)
-    fresh = [raw[slot] - overlap * start[slot] for slot in range(nsec)]
+    fresh = [raw[slot] - overlap * full_ref[slot] for slot in range(nsec)]
     length = fresh[0] * fresh[0]
     for slot in range(1, nsec):
         length = length + fresh[slot] * fresh[slot]
     length = total(length) / ncell
-    own = fresh[0]
-    fresh_ref[...] = own
-    terms = range(nterm)
-    middles = [product((lh[i], ll[i]), split(pick(slot_ref, i, fresh)), NN) for i in terms]
-    joints = [coupling * own + product(split(middles[i]), (rh[i], rl[i]), NT) for i in terms]
-    squares = weight * own * own * diag_ref[...]
-    for joint in joints:
+    fresh_ref[...] = fresh[0]
+    squares = weight * fresh[0] * fresh[0] * diag_ref[...]
+    for i in terms:
+        joint = coupling * raw[0] + product(split(middles[i]), (rh[i], rl[i]), NT)
+        joint = joint - overlap * joint_ref[i]
         squares = squares + joint * joint
     row = lax.broadcasted_iota(jnp.int32, sums_ref.shape, 0)
     sums_ref[...] = jnp.where(row == 0, total(squares), cross_ref[:1, :1] * share)
@@ -196,7 +233,11 @@
     size = jnp.sqrt(keep * keep + turn * turn)
     keep = keep / size
     turn = turn / size
-    vector_ref[0] = (keep / jnp.sqrt(norm)) * full_ref[0] + (turn / jnp.sqrt(length)) * fresh_ref[...]
+    value = (keep / jnp.sqrt(norm)) * full_ref[0] + (turn / jnp.sqrt(length)) * fresh_ref[...]
+    half = value.shape[0] // 2
+    mine, other = halves_of(half)
+    vector_ref[0, mine, :] = value[:half]
+    vector_ref[0, other, :] = value[half:]
     energy_ref[0] = jnp.sum(lowest)
 
 
@@ -219,7 +260,7 @@
     weight = 1.0 / (nz * nrep)
     ncell = float(nsec * blk * blk)
     core = lax.axis_index("rep")
-    psi, diag = psi_start[0], diagonal[0]
+    psi = psi_start[0]
     vmem, smem, hbm = (pl.BlockSpec(memory_space=space) for space in (pltpu.VMEM, pltpu.SMEM, pltpu.HBM))
     shape = jax.ShapeDtypeStruct
 
@@ -230,12 +271,12 @@
         halves.append(near)
 
     operator = (nterm_dev, blk, blk)
-    *ops, mask, own, slots, stat = pl.pallas_call(
+    *ops, mask, own, diag, slots, stat = pl.pallas_call(
         functools.partial(prepare_kernel, weight),
         out_shape=[shape(operator, BF16)] * 6
-        + [shape((nsec, half, blk), F32), shape((blk, blk), F32), shape((nterm_dev, 8, blk), jnp.int32), shape((8, 128), F32)],
+        + [shape((nsec, half, blk), F32), shape((blk, blk), F32), shape((blk, blk), F32), shape((nterm_dev, 8, blk), jnp.int32), shape((8, 128), F32)],
         in_specs=[smem] * 2 + [hbm] * 4,
-        out_specs=[vmem] * 10,
+        out_specs=[vmem] * 11,
         scratch_shapes=[
             pltpu.VMEM((blk, blk), F32),
             pltpu.VMEM((blk, blk), F32),
@@ -252,21 +293,41 @@
     masked = [near * mask[slot] for slot, near in enumerate(halves, 1)]
     halves = [part for near in masked for part in (near, across(near, "rep", 1))]
 
-    keep, send, full, norm = pl.pallas_call(
+    def partial(nears):
+        return pl.pallas_call(
+            functools.partial(partial_kernel, nsec),
+            out_shape=shape(operator, F32),
+            in_specs=[vmem] * (nsec + 3),
+            out_specs=vmem,
+            compiler_params=PARAMS,
+            name="partial",
+        )(*nears, slots, lh, ll)
+
+    summed = shape((nsec, blk // LANES * half + PAD, LANES), F32)
+    send, full, norm, joints, *inner = pl.pallas_call(
         functools.partial(image_kernel, coupling, ncell, nsec),
         out_shape=[
-            shape((nsec, blk // LANES * half + PAD, LANES), F32),
-            shape((nsec, blk // LANES * half + PAD, LANES), F32),
+            summed,
             shape((nsec, blk, blk), F32),
             shape((8, 128), F32),
+            shape(operator, F32),
+            shape(operator, BF16),
+            shape(operator, BF16),
         ],
-        in_specs=[vmem] * (len(halves) + 9),
-        out_specs=[vmem] * 4,
-        scratch_shapes=[pltpu.VMEM((nsec, blk, blk), F32)],
+        in_specs=[vmem] * (len(halves) + 10),
+        out_specs=[vmem] * 6,
         compiler_params=PARAMS,
         name="image",
-    )(*halves, own, slots, stat, lh, ll, th, tl, rh, rl)
-
+    )(*halves, own, partial([own, *masked]), slots, stat, lh, ll, th, tl, rh, rl)
+
+    keep = pl.pallas_call(
+        functools.partial(keep_kernel, coupling),
+        out_shape=summed,
+        in_specs=[vmem] * 7,
+        out_specs=vmem,
+        compiler_params=PARAMS,
+        name="keep",
+    )(slots, norm, joints, th, tl, *inner)
     chip = keep + across(send, "rep", 1)
     ntile = blk // LANES
     bounds = [tile * half for tile in range(ntile)] + [ntile * half + PAD]
@@ -290,19 +351,16 @@
         name="fresh",
     )(*parts, full, mask, diag, norm)
 
-    halves = []
-    for step in range(nsec):
-        near = across(fresh, "sector", step) if step else fresh
-        halves += [near, across(near, "rep", 1)]
+    nears = [across(fresh, "sector", step) if step else fresh for step in range(nsec)]
+    fars = [across(near, "rep", 1) for near in nears]
     sums, direction, info = pl.pallas_call(
         functools.partial(corner_kernel, coupling, weight, ncell, 1.0 / nz, nsec),
         out_shape=[shape((8, 128), F32), shape((blk, blk), F32), shape((8, 128), F32)],
-        in_specs=[vmem] * (len(halves) + 9),
+        in_specs=[vmem] * (2 * nsec + 11),
         out_specs=[vmem] * 3,
-        scratch_shapes=[pltpu.VMEM((nsec, blk, blk), F32)],
         compiler_params=PARAMS,
         name="corner",
-    )(*halves, full, diag, norm, cross, slots, lh, ll, rh, rl)
+    )(*nears, *fars, partial(nears), joints, full, diag, norm, cross, slots, lh, ll, rh, rl)
 
     sums = sums + across(sums, "rep", 1)
     for axis in ("sector", "terms"):

time: 50.8 us -> 49.9 us (0.982)
  waiting for transfers between devices: 18 us -> 16.7 us
    ppermute x13, waiting for transfers between devices: 14.1 us -> 12.8 us  [across(): return lax.ppermute(x, axis, [(i, i ^ step) for i in range(size)])]
    pallas_call x0 -> x3, Pallas kernels: none -> 1.33 us  [the longest x2 0.93 us: partial(): pl.pallas_call(functools.partial(partial_kernel, nsec), out_shape=shape(o...]
  transfers between devices with their start and end apart: 17 -> 17, of which waited for: 13 -> 13; matrix products, arithmetic and copies ran while one was open for 0% -> 0% of each run, Pallas kernels for 5% -> 7%
where the time goes in v4:
time: 49.9 us; the launch traced here: 49.8 us
  starting transfers between devices  22.5 us (45%)
  waiting for transfers between devices  16.7 us (33%)
  Pallas kernels  7.8 us (16%)
  local copies, waits for them, and re-layouts  1.95 us (4%)
  between operations  0.78 us (2%)
    ppermute x13, starting transfers between devices, across(): return lax.ppermute(x, axis, [(i, i ^ step) for i in range(size)])  17.2 us
    ppermute x13, waiting for transfers between devices, across(): return lax.ppermute(x, axis, [(i, i ^ step) for i in range(size)])  12.8 us
    ppermute x4, starting transfers between devices, diagonally(): lax.ppermute(x, (axis, 'rep'), [(2 * i + c, 2 * (i ^ step) + 1 - c) for i...  5.22 us
    ppermute x4, waiting for transfers between devices, diagonally(): lax.ppermute(x, (axis, 'rep'), [(2 * i + c, 2 * (i ^ step) + 1 - c) for i...  3.89 us
    pallas_call x1, Pallas kernels, body(): pl.pallas_call(functools.partial(prepare_kernel, weight), out_shape=[shap...  2.4 us
    pallas_call x1, Pallas kernels, body(): pl.pallas_call(functools.partial(image_kernel, coupling, ncell, nsec), ou...  1.77 us
    pallas_call x1, Pallas kernels, body(): pl.pallas_call(functools.partial(corner_kernel, coupling, weight, ncell,...  1.2 us
  transfers between devices with their start and end apart: 17, of which 13 were waited for; matrix products, arithmetic and copies ran while one was open for 0% of the time, Pallas kernels for 7%

profile of v4, /device:TPU:0, one launch (start us, length us, event | category | flops | bytes accessed | tf_op | source)
XLA Modules:
  0.0 49.8 jit_solution(12861225390458324629)
XLA Ops:
  0.6 0.0 copy-start
  0.6 1.0 %dynamic-slice_bitcast_fusion = f32[128,256]{1,0:T(8,128)S(1)} fusion(f32[1,256,256]{2,1,0:T(8,128)} %psi_hbm.1, s32[]{:T(128)S(6)} %select_n.3), kind=kLoop, calls=%fused_computation.1 | loop fusion | bytes 262148 | tf_op jit(solution)/shard_map/dynamic_slice | solution.py:267
  1.6 0.0 copy-start.2
  1.6 0.0 copy-start.3
  1.6 3.0 %collective-permute-start = (f32[128,256]{1,0:T(8,128)S(1)}, f32[128,256]{1,0:T(8,128)S(1)}, u32[]{:S(2)}, u32[]{:S(2)}) collective-permute-start(f32[128,256]{1,0:T(8,128)S(1)} %dynamic-slice_bitcast_fusion), channel_id=1, source_target_pairs={{0,2},{2,0},{1,3},{3,1},{4,6},{6,4},{5,7},{7,5},{8,10},{10,8},{9,1... | collective-permute-start | bytes 393224 | tf_op jit(solution)/shard_map/ppermute | solution.py:246
  4.7 0.0 copy-done.2
  4.7 0.9 %copy-done.1 = f32[1,256,256]{2,1,0:T(8,128)S(1)} copy-done((f32[1,256,256]{2,1,0:T(8,128)S(1)}, f32[1,256,256]{2,1,0:T(8,128)}, u32[]{:S(2)}) %copy-start.1) | copy-done | bytes 262168
  5.6 2.4 %prepare.1 = (bf16[4,256,256]{2,1,0:T(8,128)(2,1)S(1)}, bf16[4,256,256]{2,1,0:T(8,128)(2,1)S(1)}, bf16[4,256,256]{2,1,0:T(8,128)(2,1)S(1)}, bf16[4,256,256]{2,1,...) custom-call(s32[2,2]{1,0:T(2,128)S(1)} %copy-done.2, ...), custom_call_target="tpu_custom_call" | custom-call | tf_op jit(solution)/shard_map/prepare/pallas_call | solution.py:274
  8.0 0.1 collective-permute-done
  8.2 0.1 collective-permute-start.1
  8.2 0.5 partial.2.refs_3_
  8.7 0.9 %collective-permute-done.1.refs_1_ = f32[128,256]{1,0:T(8,128)S(1)} collective-permute-done((f32[128,256]{1,0:T(8,128)S(1)}, f32[128,256]{1,0:T(8,128)S(1)}, u32[]{:S(2)}, u32[]{:S(2)}) %collective-permute-start.1) | collective-permute-done | bytes 131104 | tf_op jit(solution)/shard_map/ppermute | solution.py:246
  9.6 1.8 %image.1 = (f32[2,264,128]{2,1,0:T(8,128)S(1)}, f32[2,256,256]{2,1,0:T(8,128)S(1)}, f32[8,128]{1,0:T(8,128)S(1)}, f32[4,256,256]{2,1,0:T(8,128)S(1)}, bf16[4,256...) custom-call(f32[128,256]{1,0:T(8,128)S(1)} %bitcast_multiply_fusion.refs_1_.refs_0_, ...), custom_call_target="tpu_custom_call" | custom-call | tf_op jit(solution)/shard_map/image/pallas_call | solution.py:307
  11.4 0.2 collective-permute-start.2
  11.6 0.4 keep.1
  12.0 1.0 %collective-permute-done.2 = f32[2,264,128]{2,1,0:T(8,128)S(1)} collective-permute-done((f32[2,264,128]{2,1,0:T(8,128)S(1)}, f32[2,264,128]{2,1,0:T(8,128)S(1)}, u32[]{:S(2)}, u32[]{:S(2)}) %collective-permute-start.2) | collective-permute-done | bytes 270368 | tf_op jit(solution)/shard_map/ppermute | solution.py:246
  13.0 1.8 %collective-permute-start.6 = (f32[136,128]{1,0:T(8,128)S(1)}, f32[136,128]{1,0:T(8,128)S(1)}, u32[]{:S(2)}, u32[]{:S(2)}) collective-permute-start(f32[136,128]{1,0:T(8,128)S(1)} %slice_bitcast_fusion), channel_id=1, source_target_pairs={{0,2},{2,0},{1,3},{3,1},{4,6},{6,4},{5,7},{7,5},{8,10},{10,8},{9,1... | collective-permute-start | bytes 208904 | tf_op jit(solution)/shard_map/ppermute | solution.py:246
  14.8 0.3 collective-permute-start.3
  15.1 2.4 %collective-permute-done.6 = f32[136,128]{1,0:T(8,128)S(1)} collective-permute-done((f32[136,128]{1,0:T(8,128)S(1)}, f32[136,128]{1,0:T(8,128)S(1)}, u32[]{:S(2)}, u32[]{:S(2)}) %collective-permute-start.6) | collective-permute-done | bytes 69664 | tf_op jit(solution)/shard_map/ppermute | solution.py:246
  17.6 3.2 %collective-permute-start.7 = (f32[136,128]{1,0:T(8,128)S(1)}, f32[136,128]{1,0:T(8,128)S(1)}, u32[]{:S(2)}, u32[]{:S(2)}) collective-permute-start(f32[136,128]{1,0:T(8,128)S(1)} %fusion), channel_id=1, source_target_pairs={{0,8},{4,12},{8,0},{12,4},{1,9},{5,13},{9,1},{13,5},{2,10},{6,14},... | collective-permute-start | bytes 208904 | tf_op jit(solution)/shard_map/ppermute | solution.py:246
  20.8 0.0 collective-permute-done.3
  20.8 1.6 %collective-permute-start.4 = (f32[128,128]{1,0:T(8,128)S(1)}, f32[128,128]{1,0:T(8,128)S(1)}, u32[]{:S(2)}, u32[]{:S(2)}) collective-permute-start(f32[128,128]{1,0:T(8,128)S(1)} %fusion.1), channel_id=1, source_target_pairs={{0,4},{4,0},{8,12},{12,8},{1,5},{5,1},{9,13},{13,9},{2,6},{6,2},{1... | collective-permute-start | bytes 196616 | tf_op jit(solution)/shard_map/ppermute | solution.py:246
  22.4 0.7 %collective-permute-done.7 = f32[136,128]{1,0:T(8,128)S(1)} collective-permute-done((f32[136,128]{1,0:T(8,128)S(1)}, f32[136,128]{1,0:T(8,128)S(1)}, u32[]{:S(2)}, u32[]{:S(2)}) %collective-permute-start.7) | collective-permute-done | bytes 69664 | tf_op jit(solution)/shard_map/ppermute | solution.py:246
  23.2 1.9 %collective-permute-start.8 = (f32[136,128]{1,0:T(8,128)S(1)}, f32[136,128]{1,0:T(8,128)S(1)}, u32[]{:S(2)}, u32[]{:S(2)}) collective-permute-start(f32[136,128]{1,0:T(8,128)S(1)} %add.38.refs_2_), channel_id=1, source_target_pairs={{0,4},{4,0},{8,12},{12,8},{1,5},{5,1},{9,13},{13,9},{2,6},{6,2},{1... | collective-permute-start | bytes 208904 | tf_op jit(solution)/shard_map/ppermute | solution.py:246
  25.0 0.1 collective-permute-done.4
  25.1 3.3 %collective-permute-start.5 = (f32[128,128]{1,0:T(8,128)S(1)}, f32[128,128]{1,0:T(8,128)S(1)}, u32[]{:S(2)}, u32[]{:S(2)}) collective-permute-start(f32[128,128]{1,0:T(8,128)S(1)} %add.36.refs_0_), channel_id=1, source_target_pairs={{0,8},{4,12},{8,0},{12,4},{1,9},{5,13},{9,1},{13,5},{2,10},{6,14},... | collective-permute-start | bytes 196616 | tf_op jit(solution)/shard_map/ppermute | solution.py:246
  28.4 2.3 %collective-permute-done.5.refs_1_ = f32[128,128]{1,0:T(8,128)S(1)} collective-permute-done((f32[128,128]{1,0:T(8,128)S(1)}, f32[128,128]{1,0:T(8,128)S(1)}, u32[]{:S(2)}, u32[]{:S(2)}) %collective-permute-start.5) | collective-permute-done | bytes 65568 | tf_op jit(solution)/shard_map/ppermute | solution.py:246
  30.7 0.0 collective-permute-done.8.refs_3_
  30.7 0.3 fresh.1
  31.0 1.6 %collective-permute-start.9 = (f32[128,256]{1,0:T(8,128)S(1)}, f32[128,256]{1,0:T(8,128)S(1)}, u32[]{:S(2)}, u32[]{:S(2)}) collective-permute-start(f32[128,256]{1,0:T(8,128)S(1)} %get-tuple-element.41.refs_0_), channel_id=1, source_target_pairs={{0,2},{2,0},{1,3},{3,1},{4,6},{6,4},{5,7},{7,5},{8,10},{10,8},{9,1... | collective-permute-start | bytes 393224 | tf_op jit(solution)/shard_map/ppermute | solution.py:246
  32.6 0.0 collective-permute-start.10
  32.6 3.4 %collective-permute-done.9.refs_1_ = f32[128,256]{1,0:T(8,128)S(1)} collective-permute-done((f32[128,256]{1,0:T(8,128)S(1)}, f32[128,256]{1,0:T(8,128)S(1)}, u32[]{:S(2)}, u32[]{:S(2)}) %collective-permute-start.9) | collective-permute-done | bytes 131104 | tf_op jit(solution)/shard_map/ppermute | solution.py:246
  36.0 0.0 collective-permute-start.11
  36.0 0.5 partial.3.refs_4_
  36.5 0.0 collective-permute-done.10.refs_2_
  36.5 0.9 %collective-permute-done.11.refs_3_ = f32[128,256]{1,0:T(8,128)S(1)} collective-permute-done((f32[128,256]{1,0:T(8,128)S(1)}, f32[128,256]{1,0:T(8,128)S(1)}, u32[]{:S(2)}, u32[]{:S(2)}) %collective-permute-start.11) | collective-permute-done | bytes 131104 | tf_op jit(solution)/shard_map/ppermute | solution.py:246
  37.3 1.2 %corner.1 = (f32[8,128]{1,0:T(8,128)S(1)}, f32[256,256]{1,0:T(8,128)S(1)}, f32[8,128]{1,0:T(8,128)S(1)}) custom-call(f32[128,256]{1,0:T(8,128)S(1)} %get-tuple-element.41.refs_0_, f32[128,256]{1,0:T(8,128)S(1)} %collective-permute-done.9.refs_1_, f32[128,256]{1,0:T(8,128)S(1)} %collective-permute-done.10.refs_2_, ...), custom_call_target="tpu_custom_call" | custom-call | tf_op jit(solution)/shard_map/corner/pallas_call | solution.py:356
  38.6 0.2 collective-permute-start.12
  38.8 1.0 %collective-permute-done.12 = f32[8,128]{1,0:T(8,128)S(1)} collective-permute-done((f32[8,128]{1,0:T(8,128)S(1)}, f32[8,128]{1,0:T(8,128)S(1)}, u32[]{:S(2)}, u32[]{:S(2)}) %collective-permute-start.12) | collective-permute-done | bytes 4128 | tf_op jit(solution)/shard_map/ppermute | solution.py:246
  39.8 1.3 %collective-permute-start.13 = (f32[8,128]{1,0:T(8,128)S(1)}, f32[8,128]{1,0:T(8,128)S(1)}, u32[]{:S(2)}, u32[]{:S(2)}) collective-permute-start(f32[8,128]{1,0:T(8,128)S(1)} %add.39), channel_id=1, source_target_pairs={{0,3},{1,2},{2,1},{3,0},{4,7},{5,6},{6,5},{7,4},{8,11},{9,10},{10,... | collective-permute-start | bytes 12296 | tf_op jit(solution)/shard_map/ppermute | solution.py:251
  41.1 1.7 %collective-permute-done.13 = f32[8,128]{1,0:T(8,128)S(1)} collective-permute-done((f32[8,128]{1,0:T(8,128)S(1)}, f32[8,128]{1,0:T(8,128)S(1)}, u32[]{:S(2)}, u32[]{:S(2)}) %collective-permute-start.13) | collective-permute-done | bytes 4128 | tf_op jit(solution)/shard_map/ppermute | solution.py:251
  42.8 2.1 %collective-permute-start.16 = (f32[8,128]{1,0:T(8,128)S(1)}, f32[8,128]{1,0:T(8,128)S(1)}, u32[]{:S(2)}, u32[]{:S(2)}) collective-permute-start(f32[8,128]{1,0:T(8,128)S(1)} %add.40), channel_id=1, source_target_pairs={{0,13},{1,12},{4,9},{5,8},{8,5},{9,4},{12,1},{13,0},{2,15},{3,14},... | collective-permute-start | bytes 12296 | tf_op jit(solution)/shard_map/ppermute | solution.py:251
  45.0 0.5 %collective-permute-start.15 = (f32[8,128]{1,0:T(8,128)S(1)}, f32[8,128]{1,0:T(8,128)S(1)}, u32[]{:S(2)}, u32[]{:S(2)}) collective-permute-start(f32[8,128]{1,0:T(8,128)S(1)} %add.40), channel_id=1, source_target_pairs={{0,9},{1,8},{4,13},{5,12},{8,1},{9,0},{12,5},{13,4},{2,11},{3,10},... | collective-permute-start | bytes 12296 | tf_op jit(solution)/shard_map/ppermute | solution.py:251
  45.5 1.2 %collective-permute-start.14 = (f32[8,128]{1,0:T(8,128)S(1)}, f32[8,128]{1,0:T(8,128)S(1)}, u32[]{:S(2)}, u32[]{:S(2)}) collective-permute-start(f32[8,128]{1,0:T(8,128)S(1)} %add.40), channel_id=1, source_target_pairs={{0,5},{1,4},{4,1},{5,0},{8,13},{9,12},{12,9},{13,8},{2,7},{3,6},{6... | collective-permute-start | bytes 12296 | tf_op jit(solution)/shard_map/ppermute | solution.py:251
  46.7 0.9 %collective-permute-done.16 = f32[8,128]{1,0:T(8,128)S(1)} collective-permute-done((f32[8,128]{1,0:T(8,128)S(1)}, f32[8,128]{1,0:T(8,128)S(1)}, u32[]{:S(2)}, u32[]{:S(2)}) %collective-permute-start.16) | collective-permute-done | bytes 4128 | tf_op jit(solution)/shard_map/ppermute | solution.py:251
  47.7 1.2 %collective-permute-done.15 = f32[8,128]{1,0:T(8,128)S(1)} collective-permute-done((f32[8,128]{1,0:T(8,128)S(1)}, f32[8,128]{1,0:T(8,128)S(1)}, u32[]{:S(2)}, u32[]{:S(2)}) %collective-permute-start.15) | collective-permute-done | bytes 4128 | tf_op jit(solution)/shard_map/ppermute | solution.py:251
  48.9 0.0 collective-permute-done.14
  48.9 0.8 %result.1 = (f32[1,256,256]{2,1,0:T(8,128)}, f32[1]{0:T(128)}) custom-call(f32[8,128]{1,0:T(8,128)S(1)} %add_add_fusion.sums_ref, f32[8,128]{1,0:T(8,128)S(1)} %get-tuple-element.44.info_ref, f32[2,256,256]{2,1,0:T(8,128)S(1)} %get-tuple-element.39.refs_4_.refs_6_.full_ref, f32[256,256]{1,0:T(8,128)S(1)} %get-tuple-element.45.fresh_ref), custom_call_target="tpu_custom_call" | custom-call | tf_op jit(solution)/shard_map/result/pallas_call | solution.py:369
  (14 shorter events, 0.1 us)
Async XLA Ops:
  0.6 4.0 %copy-start = (f32[1,256,256]{2,1,0:T(8,128)S(1)}, f32[1,256,256]{2,1,0:T(8,128)}, u32[]{:S(2)}) copy-start(f32[1,256,256]{2,1,0:T(8,128)} %psi_hbm.1) | copy-start | bytes 786436
  1.6 3.0 %copy-start.2 = (s32[2,2]{1,0:T(2,128)S(1)}, s32[2,2]{1,0:T(2,128)}, u32[]{:S(2)}) copy-start(s32[2,2]{1,0:T(2,128)} %sizes_ref.1) | copy-start | bytes 52
  1.6 3.0 %copy-start.3 = (s32[4,1]{0,1:T(1,128)S(1)}, s32[4,1]{0,1:T(1,128)}, u32[]{:S(2)}) copy-start(s32[4,1]{0,1:T(1,128)} %param.9) | copy-start | bytes 52
  1.6 6.5 %collective-permute-start = (f32[128,256]{1,0:T(8,128)S(1)}, f32[128,256]{1,0:T(8,128)S(1)}, u32[]{:S(2)}, u32[]{:S(2)}) collective-permute-start(f32[128,256]{1,0:T(8,128)S(1)} %dynamic-slice_bitcast_fusion), channel_id=1, source_target_pairs={{0,2},{2,0},{1,3},{3,1},{4,6},{6,4},{5,7},{7,5},{8,10},{10,8},{9,1... | collective-permute-start | bytes 393224 | tf_op jit(solution)/shard_map/ppermute | solution.py:246
  4.7 1.0 %copy-start.1 = (f32[1,256,256]{2,1,0:T(8,128)S(1)}, f32[1,256,256]{2,1,0:T(8,128)}, u32[]{:S(2)}) copy-start(f32[1,256,256]{2,1,0:T(8,128)} %diag_hbm.1) | copy-start | bytes 786436
  8.2 1.4 %collective-permute-start.1 = (f32[128,256]{1,0:T(8,128)S(1)}, f32[128,256]{1,0:T(8,128)S(1)}, u32[]{:S(2)}, u32[]{:S(2)}) collective-permute-start(f32[128,256]{1,0:T(8,128)S(1)} %bitcast_multiply_fusion.refs_1_.refs_0_), channel_id=1, source_target_pairs={{0,1},{1,0},{2,3},{3,2},{4,5},{5,4},{6,7},{7,6},{8,9},{9,8},{10,11... | collective-permute-start | bytes 393224 | tf_op jit(solution)/shard_map/ppermute | solution.py:246
  11.4 1.6 %collective-permute-start.2 = (f32[2,264,128]{2,1,0:T(8,128)S(1)}, f32[2,264,128]{2,1,0:T(8,128)S(1)}, u32[]{:S(2)}, u32[]{:S(2)}) collective-permute-start(f32[2,264,128]{2,1,0:T(8,128)S(1)} %get-tuple-element.38), channel_id=1, source_target_pairs={{0,1},{1,0},{2,3},{3,2},{4,5},{5,4},{6,7},{7,6},{8,9},{9,8},{10,11... | collective-permute-start | bytes 811016 | tf_op jit(solution)/shard_map/ppermute | solution.py:246
  13.0 4.5 %collective-permute-start.6 = (f32[136,128]{1,0:T(8,128)S(1)}, f32[136,128]{1,0:T(8,128)S(1)}, u32[]{:S(2)}, u32[]{:S(2)}) collective-permute-start(f32[136,128]{1,0:T(8,128)S(1)} %slice_bitcast_fusion), channel_id=1, source_target_pairs={{0,2},{2,0},{1,3},{3,1},{4,6},{6,4},{5,7},{7,5},{8,10},{10,8},{9,1... | collective-permute-start | bytes 208904 | tf_op jit(solution)/shard_map/ppermute | solution.py:246
  14.8 5.9 %collective-permute-start.3 = (f32[128,128]{1,0:T(8,128)S(1)}, f32[128,128]{1,0:T(8,128)S(1)}, u32[]{:S(2)}, u32[]{:S(2)}) collective-permute-start(f32[128,128]{1,0:T(8,128)S(1)} %slice_bitcast_fusion.2), channel_id=1, source_target_pairs={{0,2},{2,0},{1,3},{3,1},{4,6},{6,4},{5,7},{7,5},{8,10},{10,8},{9,1... | collective-permute-start | bytes 196616 | tf_op jit(solution)/shard_map/ppermute | solution.py:246
  17.6 5.6 %collective-permute-start.7 = (f32[136,128]{1,0:T(8,128)S(1)}, f32[136,128]{1,0:T(8,128)S(1)}, u32[]{:S(2)}, u32[]{:S(2)}) collective-permute-start(f32[136,128]{1,0:T(8,128)S(1)} %fusion), channel_id=1, source_target_pairs={{0,8},{4,12},{8,0},{12,4},{1,9},{5,13},{9,1},{13,5},{2,10},{6,14},... | collective-permute-start | bytes 208904 | tf_op jit(solution)/shard_map/ppermute | solution.py:246
  20.8 4.3 %collective-permute-start.4 = (f32[128,128]{1,0:T(8,128)S(1)}, f32[128,128]{1,0:T(8,128)S(1)}, u32[]{:S(2)}, u32[]{:S(2)}) collective-permute-start(f32[128,128]{1,0:T(8,128)S(1)} %fusion.1), channel_id=1, source_target_pairs={{0,4},{4,0},{8,12},{12,8},{1,5},{5,1},{9,13},{13,9},{2,6},{6,2},{1... | collective-permute-start | bytes 196616 | tf_op jit(solution)/shard_map/ppermute | solution.py:246
  23.2 7.5 %collective-permute-start.8 = (f32[136,128]{1,0:T(8,128)S(1)}, f32[136,128]{1,0:T(8,128)S(1)}, u32[]{:S(2)}, u32[]{:S(2)}) collective-permute-start(f32[136,128]{1,0:T(8,128)S(1)} %add.38.refs_2_), channel_id=1, source_target_pairs={{0,4},{4,0},{8,12},{12,8},{1,5},{5,1},{9,13},{13,9},{2,6},{6,2},{1... | collective-permute-start | bytes 208904 | tf_op jit(solution)/shard_map/ppermute | solution.py:246
  25.1 5.6 %collective-permute-start.5 = (f32[128,128]{1,0:T(8,128)S(1)}, f32[128,128]{1,0:T(8,128)S(1)}, u32[]{:S(2)}, u32[]{:S(2)}) collective-permute-start(f32[128,128]{1,0:T(8,128)S(1)} %add.36.refs_0_), channel_id=1, source_target_pairs={{0,8},{4,12},{8,0},{12,4},{1,9},{5,13},{9,1},{13,5},{2,10},{6,14},... | collective-permute-start | bytes 196616 | tf_op jit(solution)/shard_map/ppermute | solution.py:246
  31.0 5.0 %collective-permute-start.9 = (f32[128,256]{1,0:T(8,128)S(1)}, f32[128,256]{1,0:T(8,128)S(1)}, u32[]{:S(2)}, u32[]{:S(2)}) collective-permute-start(f32[128,256]{1,0:T(8,128)S(1)} %get-tuple-element.41.refs_0_), channel_id=1, source_target_pairs={{0,2},{2,0},{1,3},{3,1},{4,6},{6,4},{5,7},{7,5},{8,10},{10,8},{9,1... | collective-permute-start | bytes 393224 | tf_op jit(solution)/shard_map/ppermute | solution.py:246
  32.6 3.9 %collective-permute-start.10 = (f32[128,256]{1,0:T(8,128)S(1)}, f32[128,256]{1,0:T(8,128)S(1)}, u32[]{:S(2)}, u32[]{:S(2)}) collective-permute-start(f32[128,256]{1,0:T(8,128)S(1)} %get-tuple-element.41.refs_0_), channel_id=1, source_target_pairs={{0,1},{1,0},{2,3},{3,2},{4,5},{5,4},{6,7},{7,6},{8,9},{9,8},{10,11... | collective-permute-start | bytes 393224 | tf_op jit(solution)/shard_map/ppermute | solution.py:246
  36.0 1.3 %collective-permute-start.11 = (f32[128,256]{1,0:T(8,128)S(1)}, f32[128,256]{1,0:T(8,128)S(1)}, u32[]{:S(2)}, u32[]{:S(2)}) collective-permute-start(f32[128,256]{1,0:T(8,128)S(1)} %collective-permute-done.9.refs_1_), channel_id=1, source_target_pairs={{0,1},{1,0},{2,3},{3,2},{4,5},{5,4},{6,7},{7,6},{8,9},{9,8},{10,11... | collective-permute-start | bytes 393224 | tf_op jit(solution)/shard_map/ppermute | solution.py:246
  38.6 1.2 %collective-permute-start.12 = (f32[8,128]{1,0:T(8,128)S(1)}, f32[8,128]{1,0:T(8,128)S(1)}, u32[]{:S(2)}, u32[]{:S(2)}) collective-permute-start(f32[8,128]{1,0:T(8,128)S(1)} %get-tuple-element.43), channel_id=1, source_target_pairs={{0,1},{1,0},{2,3},{3,2},{4,5},{5,4},{6,7},{7,6},{8,9},{9,8},{10,11... | collective-permute-start | bytes 12296 | tf_op jit(solution)/shard_map/ppermute | solution.py:246
  39.8 3.0 %collective-permute-start.13 = (f32[8,128]{1,0:T(8,128)S(1)}, f32[8,128]{1,0:T(8,128)S(1)}, u32[]{:S(2)}, u32[]{:S(2)}) collective-permute-start(f32[8,128]{1,0:T(8,128)S(1)} %add.39), channel_id=1, source_target_pairs={{0,3},{1,2},{2,1},{3,0},{4,7},{5,6},{6,5},{7,4},{8,11},{9,10},{10,... | collective-permute-start | bytes 12296 | tf_op jit(solution)/shard_map/ppermute | solution.py:251
  42.8 4.8 %collective-permute-start.16 = (f32[8,128]{1,0:T(8,128)S(1)}, f32[8,128]{1,0:T(8,128)S(1)}, u32[]{:S(2)}, u32[]{:S(2)}) collective-permute-start(f32[8,128]{1,0:T(8,128)S(1)} %add.40), channel_id=1, source_target_pairs={{0,13},{1,12},{4,9},{5,8},{8,5},{9,4},{12,1},{13,0},{2,15},{3,14},... | collective-permute-start | bytes 12296 | tf_op jit(solution)/shard_map/ppermute | solution.py:251
  45.0 3.9 %collective-permute-start.15 = (f32[8,128]{1,0:T(8,128)S(1)}, f32[8,128]{1,0:T(8,128)S(1)}, u32[]{:S(2)}, u32[]{:S(2)}) collective-permute-start(f32[8,128]{1,0:T(8,128)S(1)} %add.40), channel_id=1, source_target_pairs={{0,9},{1,8},{4,13},{5,12},{8,1},{9,0},{12,5},{13,4},{2,11},{3,10},... | collective-permute-start | bytes 12296 | tf_op jit(solution)/shard_map/ppermute | solution.py:251
  45.5 3.4 %collective-permute-start.14 = (f32[8,128]{1,0:T(8,128)S(1)}, f32[8,128]{1,0:T(8,128)S(1)}, u32[]{:S(2)}, u32[]{:S(2)}) collective-permute-start(f32[8,128]{1,0:T(8,128)S(1)} %add.40), channel_id=1, source_target_pairs={{0,5},{1,4},{4,1},{5,0},{8,13},{9,12},{12,9},{13,8},{2,7},{3,6},{6... | collective-permute-start | bytes 12296 | tf_op jit(solution)/shard_map/ppermute | solution.py:251

commit v5 on v4

--- a/solution.py
+++ b/solution.py
@@ -111,32 +111,32 @@
         part_ref[i] = half_product((lh[i, :, :half], ll[i, :, :half]), split(pick(slot_ref, i, blocks)))
 
 
-def sum_rows(coupling, first, slot_ref, th, tl, inner, joints, scalar, out_ref):
+def sum_rows(coupling, first, slot_ref, th, tl, inner, joints, scalar, out_refs):
     blk = th.shape[-1]
     half = blk // 2
     rows = slice(first, first + half)
     terms = range(th.shape[0])
     returned = [product((th[i, rows, :], tl[i, rows, :]), inner[i], NN) for i in terms]
-    for slot in range(out_ref.shape[0]):
+    for slot, out_ref in enumerate(out_refs):
         value = coupling * sum([joint[rows] for joint in joints[1:]], joints[0][rows]) if slot == 0 else jnp.zeros((half, blk), F32)
         for i in terms:
             target = jnp.broadcast_to(slot_ref[i, :1, :], (half, blk))
             value = value + jnp.where(target == slot, returned[i], 0.0)
         for tile in range(blk // LANES):
-            out_ref[slot, tile * half : (tile + 1) * half, :] = value[:, tile * LANES : (tile + 1) * LANES]
-        out_ref[slot, blk // LANES * half :, :] = jnp.broadcast_to(scalar, (PAD, LANES))
-
-
-def keep_kernel(coupling, slot_ref, norm_ref, joint_ref, th, tl, ih, il, keep_ref):
+            out_ref[tile * half : (tile + 1) * half, :] = value[:, tile * LANES : (tile + 1) * LANES]
+        out_ref[blk // LANES * half :, :] = jnp.broadcast_to(scalar, (PAD, LANES))
+
+
+def keep_kernel(coupling, slot_ref, norm_ref, joint_ref, th, tl, ih, il, *keep_refs):
     terms = range(th.shape[0])
     inner = [(ih[i], il[i]) for i in terms]
-    sum_rows(coupling, 0, slot_ref, th, tl, inner, [joint_ref.at[i] for i in terms], norm_ref[1:2, :1], keep_ref)
+    sum_rows(coupling, 0, slot_ref, th, tl, inner, [joint_ref.at[i] for i in terms], norm_ref[1:2, :1], keep_refs)
 
 
 def image_kernel(coupling, ncell, nsec, *refs):
     halves = refs[: 2 * (nsec - 1)]
     own_ref, part_ref, slot_ref, stat_ref = refs[2 * (nsec - 1) : 2 * (nsec - 1) + 4]
-    lh, ll, th, tl, rh, rl, send_ref, full_ref, norm_ref, joint_ref, ih, il = refs[2 * (nsec - 1) + 4 :]
+    lh, ll, th, tl, rh, rl, full_ref, norm_ref, joint_ref, ih, il, *send_refs = refs[2 * (nsec - 1) + 4 :]
     blk = own_ref.shape[0]
     half = blk // 2
     nterm = lh.shape[0]
@@ -154,7 +154,8 @@
     middles = [
         part_ref[i] + half_product((lh[i, :, half:], ll[i, :, half:]), split(pick(slot_ref, i, fars))) for i in terms
     ]
-    joints = [coupling * own + product(split(middles[i]), (rh[i], rl[i]), NT) for i in terms]
+    base = coupling * own
+    joints = [base + product(split(middles[i]), (rh[i], rl[i]), NT) for i in terms]
     squares = joints[0] * joints[0]
     for joint in joints[1:]:
         squares = squares + joint * joint
@@ -166,7 +167,7 @@
     inner = [split(product(split(joints[i]), (rh[i], rl[i]), NN)) for i in terms]
     for i in terms:
         ih[i], il[i] = inner[i]
-    sum_rows(coupling, half, slot_ref, th, tl, inner, joints, scalar, send_ref)
+    sum_rows(coupling, half, slot_ref, th, tl, inner, joints, scalar, send_refs)
 
 
 def fresh_kernel(ncell, ntile, *refs):
@@ -212,8 +213,9 @@
     length = total(length) / ncell
     fresh_ref[...] = fresh[0]
     squares = weight * fresh[0] * fresh[0] * diag_ref[...]
+    base = coupling * raw[0]
     for i in terms:
-        joint = coupling * raw[0] + product(split(middles[i]), (rh[i], rl[i]), NT)
+        joint = base + product(split(middles[i]), (rh[i], rl[i]), NT)
         joint = joint - overlap * joint_ref[i]
         squares = squares + joint * joint
     row = lax.broadcasted_iota(jnp.int32, sums_ref.shape, 0)
@@ -303,39 +305,39 @@
             name="partial",
         )(*nears, slots, lh, ll)
 
-    summed = shape((nsec, blk // LANES * half + PAD, LANES), F32)
-    send, full, norm, joints, *inner = pl.pallas_call(
+    summed = [shape((blk // LANES * half + PAD, LANES), F32)] * nsec
+    full, norm, joints, ih, il, *sends = pl.pallas_call(
         functools.partial(image_kernel, coupling, ncell, nsec),
         out_shape=[
-            summed,
             shape((nsec, blk, blk), F32),
             shape((8, 128), F32),
             shape(operator, F32),
             shape(operator, BF16),
             shape(operator, BF16),
+            *summed,
         ],
         in_specs=[vmem] * (len(halves) + 10),
-        out_specs=[vmem] * 6,
+        out_specs=[vmem] * (5 + nsec),
         compiler_params=PARAMS,
         name="image",
     )(*halves, own, partial([own, *masked]), slots, stat, lh, ll, th, tl, rh, rl)
 
-    keep = pl.pallas_call(
+    keeps = pl.pallas_call(
         functools.partial(keep_kernel, coupling),
         out_shape=summed,
         in_specs=[vmem] * 7,
-        out_specs=vmem,
+        out_specs=[vmem] * nsec,
         compiler_params=PARAMS,
         name="keep",
-    )(slots, norm, joints, th, tl, *inner)
-    chip = keep + across(send, "rep", 1)
+    )(slots, norm, joints, th, tl, ih, il)
+    chip = [keep + across(send, "rep", 1) for keep, send in zip(keeps, sends)]
     ntile = blk // LANES
     bounds = [tile * half for tile in range(ntile)] + [ntile * half + PAD]
     parts = []
     for tile, (low, high) in enumerate(zip(bounds[:-1], bounds[1:])):
-        part = chip[0, low:high]
+        part = chip[0][low:high]
         for step in range(1, nsec):
-            part = part + across(chip[step, low:high], "sector", step)
+            part = part + across(chip[step][low:high], "sector", step)
         steps = [1 << bit for bit in range(nz.bit_length() - 1)]
         if tile % 2:
             steps.reverse()

time: 49.9 us -> 49.8 us (level)
  waiting for transfers between devices: 16.7 us -> 16.1 us
    ppermute x13 -> x14, waiting for transfers between devices: 12.8 us -> 12.2 us  [across(): return lax.ppermute(x, axis, [(i, i ^ step) for i in range(size)])]
    ppermute x13 -> x14, starting transfers between devices: 17.2 us -> 17.6 us  [across(): return lax.ppermute(x, axis, [(i, i ^ step) for i in range(size)])]
  transfers between devices with their start and end apart: 17 -> 18, of which waited for: 13 -> 13; matrix products, arithmetic and copies ran while one was open for 0% -> 0% of each run, Pallas kernels for 7% -> 8%
where the time goes in v5:
time: 49.8 us; the launch traced here: 49.6 us
  starting transfers between devices  22.8 us (46%)
  waiting for transfers between devices  16.1 us (32%)
  Pallas kernels  7.8 us (16%)
  local copies, waits for them, and re-layouts  1.95 us (4%)
  between operations  0.78 us (2%)
    ppermute x14, starting transfers between devices, across(): return lax.ppermute(x, axis, [(i, i ^ step) for i in range(size)])  17.6 us
    ppermute x14, waiting for transfers between devices, across(): return lax.ppermute(x, axis, [(i, i ^ step) for i in range(size)])  12.2 us
    ppermute x4, starting transfers between devices, diagonally(): lax.ppermute(x, (axis, 'rep'), [(2 * i + c, 2 * (i ^ step) + 1 - c) for i...  5.22 us
    ppermute x4, waiting for transfers between devices, diagonally(): lax.ppermute(x, (axis, 'rep'), [(2 * i + c, 2 * (i ^ step) + 1 - c) for i...  3.89 us
    pallas_call x1, Pallas kernels, body(): pl.pallas_call(functools.partial(prepare_kernel, weight), out_shape=[shap...  2.4 us
    pallas_call x1, Pallas kernels, body(): pl.pallas_call(functools.partial(image_kernel, coupling, ncell, nsec), ou...  1.78 us
    pallas_call x1, Pallas kernels, body(): pl.pallas_call(functools.partial(corner_kernel, coupling, weight, ncell,...  1.2 us
  transfers between devices with their start and end apart: 18, of which 13 were waited for; matrix products, arithmetic and copies ran while one was open for 0% of the time, Pallas kernels for 8%

profile of v5, /device:TPU:0, one launch (start us, length us, event | category | flops | bytes accessed | tf_op | source)
XLA Modules:
  0.0 49.6 jit_solution(5614713382347820276)
XLA Ops:
  0.6 1.0 %dynamic-slice_bitcast_fusion = f32[128,256]{1,0:T(8,128)S(1)} fusion(f32[1,256,256]{2,1,0:T(8,128)} %psi_hbm.1, s32[]{:T(128)S(6)} %select_n.3), kind=kLoop, calls=%fused_computation.1 | loop fusion | bytes 262148 | tf_op jit(solution)/shard_map/dynamic_slice | solution.py:269
  1.6 0.0 copy-start.2
  1.6 0.0 copy-start.3
  1.6 3.0 %collective-permute-start = (f32[128,256]{1,0:T(8,128)S(1)}, f32[128,256]{1,0:T(8,128)S(1)}, u32[]{:S(2)}, u32[]{:S(2)}) collective-permute-start(f32[128,256]{1,0:T(8,128)S(1)} %dynamic-slice_bitcast_fusion), channel_id=1, source_target_pairs={{0,2},{2,0},{1,3},{3,1},{4,6},{6,4},{5,7},{7,5},{8,10},{10,8},{9,1... | collective-permute-start | bytes 393224 | tf_op jit(solution)/shard_map/ppermute | solution.py:248
  4.7 0.9 %copy-done.1 = f32[1,256,256]{2,1,0:T(8,128)S(1)} copy-done((f32[1,256,256]{2,1,0:T(8,128)S(1)}, f32[1,256,256]{2,1,0:T(8,128)}, u32[]{:S(2)}) %copy-start.1) | copy-done | bytes 262168
  5.6 2.4 %prepare.1 = (bf16[4,256,256]{2,1,0:T(8,128)(2,1)S(1)}, bf16[4,256,256]{2,1,0:T(8,128)(2,1)S(1)}, bf16[4,256,256]{2,1,0:T(8,128)(2,1)S(1)}, bf16[4,256,256]{2,1,...) custom-call(s32[2,2]{1,0:T(2,128)S(1)} %copy-done.2, ...), custom_call_target="tpu_custom_call" | custom-call | tf_op jit(solution)/shard_map/prepare/pallas_call | solution.py:276
  8.0 0.1 collective-permute-done
  8.2 0.1 collective-permute-start.1
  8.2 0.5 partial.2.refs_3_
  8.7 0.9 %collective-permute-done.1.refs_1_ = f32[128,256]{1,0:T(8,128)S(1)} collective-permute-done((f32[128,256]{1,0:T(8,128)S(1)}, f32[128,256]{1,0:T(8,128)S(1)}, u32[]{:S(2)}, u32[]{:S(2)}) %collective-permute-start.1) | collective-permute-done | bytes 131104 | tf_op jit(solution)/shard_map/ppermute | solution.py:248
  9.6 1.8 %image.1 = (f32[2,256,256]{2,1,0:T(8,128)S(1)}, f32[8,128]{1,0:T(8,128)S(1)}, f32[4,256,256]{2,1,0:T(8,128)S(1)}, bf16[4,256,256]{2,1,0:T(8,128)(2,1)S(1)}, bf16...) custom-call(f32[128,256]{1,0:T(8,128)S(1)} %bitcast_multiply_fusion.refs_1_.refs_0_, ...), custom_call_target="tpu_custom_call" | custom-call | tf_op jit(solution)/shard_map/image/pallas_call | solution.py:309
  11.4 0.2 collective-permute-start.3
  11.6 0.4 collective-permute-start.2
  11.9 0.4 keep.1
  12.3 0.4 collective-permute-done.3
  12.8 1.8 %collective-permute-start.7 = (f32[136,128]{1,0:T(8,128)S(1)}, f32[136,128]{1,0:T(8,128)S(1)}, u32[]{:S(2)}, u32[]{:S(2)}) collective-permute-start(f32[136,128]{1,0:T(8,128)S(1)} %slice.23), channel_id=1, source_target_pairs={{0,2},{2,0},{1,3},{3,1},{4,6},{6,4},{5,7},{7,5},{8,10},{10,8},{9,1... | collective-permute-start | bytes 208904 | tf_op jit(solution)/shard_map/ppermute | solution.py:248
  14.6 0.3 collective-permute-start.4
  14.9 0.0 collective-permute-done.2
  14.9 2.4 %collective-permute-done.7 = f32[136,128]{1,0:T(8,128)S(1)} collective-permute-done((f32[136,128]{1,0:T(8,128)S(1)}, f32[136,128]{1,0:T(8,128)S(1)}, u32[]{:S(2)}, u32[]{:S(2)}) %collective-permute-start.7) | collective-permute-done | bytes 69664 | tf_op jit(solution)/shard_map/ppermute | solution.py:248
  17.4 3.2 %collective-permute-start.8 = (f32[136,128]{1,0:T(8,128)S(1)}, f32[136,128]{1,0:T(8,128)S(1)}, u32[]{:S(2)}, u32[]{:S(2)}) collective-permute-start(f32[136,128]{1,0:T(8,128)S(1)} %slice_add_fusion), channel_id=1, source_target_pairs={{0,8},{4,12},{8,0},{12,4},{1,9},{5,13},{9,1},{13,5},{2,10},{6,14},... | collective-permute-start | bytes 208904 | tf_op jit(solution)/shard_map/ppermute | solution.py:248
  20.6 0.0 collective-permute-done.4
  20.6 1.6 %collective-permute-start.5 = (f32[128,128]{1,0:T(8,128)S(1)}, f32[128,128]{1,0:T(8,128)S(1)}, u32[]{:S(2)}, u32[]{:S(2)}) collective-permute-start(f32[128,128]{1,0:T(8,128)S(1)} %slice_add_fusion.1), channel_id=1, source_target_pairs={{0,4},{4,0},{8,12},{12,8},{1,5},{5,1},{9,13},{13,9},{2,6},{6,2},{1... | collective-permute-start | bytes 196616 | tf_op jit(solution)/shard_map/ppermute | solution.py:248
  22.2 0.7 %collective-permute-done.8 = f32[136,128]{1,0:T(8,128)S(1)} collective-permute-done((f32[136,128]{1,0:T(8,128)S(1)}, f32[136,128]{1,0:T(8,128)S(1)}, u32[]{:S(2)}, u32[]{:S(2)}) %collective-permute-start.8) | collective-permute-done | bytes 69664 | tf_op jit(solution)/shard_map/ppermute | solution.py:248
  23.0 1.9 %collective-permute-start.9 = (f32[136,128]{1,0:T(8,128)S(1)}, f32[136,128]{1,0:T(8,128)S(1)}, u32[]{:S(2)}, u32[]{:S(2)}) collective-permute-start(f32[136,128]{1,0:T(8,128)S(1)} %add.42.refs_2_), channel_id=1, source_target_pairs={{0,4},{4,0},{8,12},{12,8},{1,5},{5,1},{9,13},{13,9},{2,6},{6,2},{1... | collective-permute-start | bytes 208904 | tf_op jit(solution)/shard_map/ppermute | solution.py:248
  24.8 0.1 collective-permute-done.5
  24.9 3.3 %collective-permute-start.6 = (f32[128,128]{1,0:T(8,128)S(1)}, f32[128,128]{1,0:T(8,128)S(1)}, u32[]{:S(2)}, u32[]{:S(2)}) collective-permute-start(f32[128,128]{1,0:T(8,128)S(1)} %add.40.refs_0_), channel_id=1, source_target_pairs={{0,8},{4,12},{8,0},{12,4},{1,9},{5,13},{9,1},{13,5},{2,10},{6,14},... | collective-permute-start | bytes 196616 | tf_op jit(solution)/shard_map/ppermute | solution.py:248
  28.2 2.3 %collective-permute-done.6.refs_1_ = f32[128,128]{1,0:T(8,128)S(1)} collective-permute-done((f32[128,128]{1,0:T(8,128)S(1)}, f32[128,128]{1,0:T(8,128)S(1)}, u32[]{:S(2)}, u32[]{:S(2)}) %collective-permute-start.6) | collective-permute-done | bytes 65568 | tf_op jit(solution)/shard_map/ppermute | solution.py:248
  30.5 0.0 collective-permute-done.9.refs_3_
  30.5 0.3 fresh.1
  30.8 1.6 %collective-permute-start.10 = (f32[128,256]{1,0:T(8,128)S(1)}, f32[128,256]{1,0:T(8,128)S(1)}, u32[]{:S(2)}, u32[]{:S(2)}) collective-permute-start(f32[128,256]{1,0:T(8,128)S(1)} %get-tuple-element.47.refs_0_), channel_id=1, source_target_pairs={{0,2},{2,0},{1,3},{3,1},{4,6},{6,4},{5,7},{7,5},{8,10},{10,8},{9,1... | collective-permute-start | bytes 393224 | tf_op jit(solution)/shard_map/ppermute | solution.py:248
  32.4 0.0 collective-permute-start.11
  32.4 3.4 %collective-permute-done.10.refs_1_ = f32[128,256]{1,0:T(8,128)S(1)} collective-permute-done((f32[128,256]{1,0:T(8,128)S(1)}, f32[128,256]{1,0:T(8,128)S(1)}, u32[]{:S(2)}, u32[]{:S(2)}) %collective-permute-start.10) | collective-permute-done | bytes 131104 | tf_op jit(solution)/shard_map/ppermute | solution.py:248
  35.8 0.0 collective-permute-start.12
  35.8 0.5 partial.3.refs_4_
  36.3 0.0 collective-permute-done.11.refs_2_
  36.3 0.9 %collective-permute-done.12.refs_3_ = f32[128,256]{1,0:T(8,128)S(1)} collective-permute-done((f32[128,256]{1,0:T(8,128)S(1)}, f32[128,256]{1,0:T(8,128)S(1)}, u32[]{:S(2)}, u32[]{:S(2)}) %collective-permute-start.12) | collective-permute-done | bytes 131104 | tf_op jit(solution)/shard_map/ppermute | solution.py:248
  37.1 1.2 %corner.1 = (f32[8,128]{1,0:T(8,128)S(1)}, f32[256,256]{1,0:T(8,128)S(1)}, f32[8,128]{1,0:T(8,128)S(1)}) custom-call(f32[128,256]{1,0:T(8,128)S(1)} %get-tuple-element.47.refs_0_, f32[128,256]{1,0:T(8,128)S(1)} %collective-permute-done.10.refs_1_, f32[128,256]{1,0:T(8,128)S(1)} %collective-permute-done.11.refs_2_, ...), custom_call_target="tpu_custom_call" | custom-call | tf_op jit(solution)/shard_map/corner/pallas_call | solution.py:358
  38.4 0.2 collective-permute-start.13
  38.6 1.0 %collective-permute-done.13 = f32[8,128]{1,0:T(8,128)S(1)} collective-permute-done((f32[8,128]{1,0:T(8,128)S(1)}, f32[8,128]{1,0:T(8,128)S(1)}, u32[]{:S(2)}, u32[]{:S(2)}) %collective-permute-start.13) | collective-permute-done | bytes 4128 | tf_op jit(solution)/shard_map/ppermute | solution.py:248
  39.6 1.3 %collective-permute-start.14 = (f32[8,128]{1,0:T(8,128)S(1)}, f32[8,128]{1,0:T(8,128)S(1)}, u32[]{:S(2)}, u32[]{:S(2)}) collective-permute-start(f32[8,128]{1,0:T(8,128)S(1)} %add.43), channel_id=1, source_target_pairs={{0,3},{1,2},{2,1},{3,0},{4,7},{5,6},{6,5},{7,4},{8,11},{9,10},{10,... | collective-permute-start | bytes 12296 | tf_op jit(solution)/shard_map/ppermute | solution.py:253
  40.9 1.7 %collective-permute-done.14 = f32[8,128]{1,0:T(8,128)S(1)} collective-permute-done((f32[8,128]{1,0:T(8,128)S(1)}, f32[8,128]{1,0:T(8,128)S(1)}, u32[]{:S(2)}, u32[]{:S(2)}) %collective-permute-start.14) | collective-permute-done | bytes 4128 | tf_op jit(solution)/shard_map/ppermute | solution.py:253
  42.6 2.1 %collective-permute-start.17 = (f32[8,128]{1,0:T(8,128)S(1)}, f32[8,128]{1,0:T(8,128)S(1)}, u32[]{:S(2)}, u32[]{:S(2)}) collective-permute-start(f32[8,128]{1,0:T(8,128)S(1)} %add.44), channel_id=1, source_target_pairs={{0,13},{1,12},{4,9},{5,8},{8,5},{9,4},{12,1},{13,0},{2,15},{3,14},... | collective-permute-start | bytes 12296 | tf_op jit(solution)/shard_map/ppermute | solution.py:253
  44.8 0.5 %collective-permute-start.16 = (f32[8,128]{1,0:T(8,128)S(1)}, f32[8,128]{1,0:T(8,128)S(1)}, u32[]{:S(2)}, u32[]{:S(2)}) collective-permute-start(f32[8,128]{1,0:T(8,128)S(1)} %add.44), channel_id=1, source_target_pairs={{0,9},{1,8},{4,13},{5,12},{8,1},{9,0},{12,5},{13,4},{2,11},{3,10},... | collective-permute-start | bytes 12296 | tf_op jit(solution)/shard_map/ppermute | solution.py:253
  45.3 1.2 %collective-permute-start.15 = (f32[8,128]{1,0:T(8,128)S(1)}, f32[8,128]{1,0:T(8,128)S(1)}, u32[]{:S(2)}, u32[]{:S(2)}) collective-permute-start(f32[8,128]{1,0:T(8,128)S(1)} %add.44), channel_id=1, source_target_pairs={{0,5},{1,4},{4,1},{5,0},{8,13},{9,12},{12,9},{13,8},{2,7},{3,6},{6... | collective-permute-start | bytes 12296 | tf_op jit(solution)/shard_map/ppermute | solution.py:253
  46.5 0.9 %collective-permute-done.17 = f32[8,128]{1,0:T(8,128)S(1)} collective-permute-done((f32[8,128]{1,0:T(8,128)S(1)}, f32[8,128]{1,0:T(8,128)S(1)}, u32[]{:S(2)}, u32[]{:S(2)}) %collective-permute-start.17) | collective-permute-done | bytes 4128 | tf_op jit(solution)/shard_map/ppermute | solution.py:253
  47.5 1.2 %collective-permute-done.16 = f32[8,128]{1,0:T(8,128)S(1)} collective-permute-done((f32[8,128]{1,0:T(8,128)S(1)}, f32[8,128]{1,0:T(8,128)S(1)}, u32[]{:S(2)}, u32[]{:S(2)}) %collective-permute-start.16) | collective-permute-done | bytes 4128 | tf_op jit(solution)/shard_map/ppermute | solution.py:253
  48.7 0.0 collective-permute-done.15
  48.7 0.8 %result.1 = (f32[1,256,256]{2,1,0:T(8,128)}, f32[1]{0:T(128)}) custom-call(f32[8,128]{1,0:T(8,128)S(1)} %add_add_fusion.sums_ref, f32[8,128]{1,0:T(8,128)S(1)} %get-tuple-element.50.info_ref, f32[2,256,256]{2,1,0:T(8,128)S(1)} %get-tuple-element.45.refs_4_.refs_6_.full_ref, f32[256,256]{1,0:T(8,128)S(1)} %get-tuple-element.51.fresh_ref), custom_call_target="tpu_custom_call" | custom-call | tf_op jit(solution)/shard_map/result/pallas_call | solution.py:371
  (17 shorter events, 0.1 us)
Async XLA Ops:
  0.6 4.0 %copy-start = (f32[1,256,256]{2,1,0:T(8,128)S(1)}, f32[1,256,256]{2,1,0:T(8,128)}, u32[]{:S(2)}) copy-start(f32[1,256,256]{2,1,0:T(8,128)} %psi_hbm.1) | copy-start | bytes 786436
  1.6 3.0 %copy-start.2 = (s32[2,2]{1,0:T(2,128)S(1)}, s32[2,2]{1,0:T(2,128)}, u32[]{:S(2)}) copy-start(s32[2,2]{1,0:T(2,128)} %sizes_ref.1) | copy-start | bytes 52
  1.6 3.0 %copy-start.3 = (s32[4,1]{0,1:T(1,128)S(1)}, s32[4,1]{0,1:T(1,128)}, u32[]{:S(2)}) copy-start(s32[4,1]{0,1:T(1,128)} %param.9) | copy-start | bytes 52
  1.6 6.5 %collective-permute-start = (f32[128,256]{1,0:T(8,128)S(1)}, f32[128,256]{1,0:T(8,128)S(1)}, u32[]{:S(2)}, u32[]{:S(2)}) collective-permute-start(f32[128,256]{1,0:T(8,128)S(1)} %dynamic-slice_bitcast_fusion), channel_id=1, source_target_pairs={{0,2},{2,0},{1,3},{3,1},{4,6},{6,4},{5,7},{7,5},{8,10},{10,8},{9,1... | collective-permute-start | bytes 393224 | tf_op jit(solution)/shard_map/ppermute | solution.py:248
  4.7 1.0 %copy-start.1 = (f32[1,256,256]{2,1,0:T(8,128)S(1)}, f32[1,256,256]{2,1,0:T(8,128)}, u32[]{:S(2)}) copy-start(f32[1,256,256]{2,1,0:T(8,128)} %diag_hbm.1) | copy-start | bytes 786436
  8.2 1.4 %collective-permute-start.1 = (f32[128,256]{1,0:T(8,128)S(1)}, f32[128,256]{1,0:T(8,128)S(1)}, u32[]{:S(2)}, u32[]{:S(2)}) collective-permute-start(f32[128,256]{1,0:T(8,128)S(1)} %bitcast_multiply_fusion.refs_1_.refs_0_), channel_id=1, source_target_pairs={{0,1},{1,0},{2,3},{3,2},{4,5},{5,4},{6,7},{7,6},{8,9},{9,8},{10,11... | collective-permute-start | bytes 393224 | tf_op jit(solution)/shard_map/ppermute | solution.py:248
  11.4 1.4 %collective-permute-start.3 = (f32[264,128]{1,0:T(8,128)S(1)}, f32[264,128]{1,0:T(8,128)S(1)}, u32[]{:S(2)}, u32[]{:S(2)}) collective-permute-start(f32[264,128]{1,0:T(8,128)S(1)} %get-tuple-element.44), channel_id=1, source_target_pairs={{0,1},{1,0},{2,3},{3,2},{4,5},{5,4},{6,7},{7,6},{8,9},{9,8},{10,11... | collective-permute-start | bytes 405512 | tf_op jit(solution)/shard_map/ppermute | solution.py:248
  11.6 3.3 %collective-permute-start.2 = (f32[264,128]{1,0:T(8,128)S(1)}, f32[264,128]{1,0:T(8,128)S(1)}, u32[]{:S(2)}, u32[]{:S(2)}) collective-permute-start(f32[264,128]{1,0:T(8,128)S(1)} %get-tuple-element.42), channel_id=1, source_target_pairs={{0,1},{1,0},{2,3},{3,2},{4,5},{5,4},{6,7},{7,6},{8,9},{9,8},{10,11... | collective-permute-start | bytes 405512 | tf_op jit(solution)/shard_map/ppermute | solution.py:248
  12.8 4.5 %collective-permute-start.7 = (f32[136,128]{1,0:T(8,128)S(1)}, f32[136,128]{1,0:T(8,128)S(1)}, u32[]{:S(2)}, u32[]{:S(2)}) collective-permute-start(f32[136,128]{1,0:T(8,128)S(1)} %slice.23), channel_id=1, source_target_pairs={{0,2},{2,0},{1,3},{3,1},{4,6},{6,4},{5,7},{7,5},{8,10},{10,8},{9,1... | collective-permute-start | bytes 208904 | tf_op jit(solution)/shard_map/ppermute | solution.py:248
  14.6 5.9 %collective-permute-start.4 = (f32[128,128]{1,0:T(8,128)S(1)}, f32[128,128]{1,0:T(8,128)S(1)}, u32[]{:S(2)}, u32[]{:S(2)}) collective-permute-start(f32[128,128]{1,0:T(8,128)S(1)} %slice.21), channel_id=1, source_target_pairs={{0,2},{2,0},{1,3},{3,1},{4,6},{6,4},{5,7},{7,5},{8,10},{10,8},{9,1... | collective-permute-start | bytes 196616 | tf_op jit(solution)/shard_map/ppermute | solution.py:248
  17.4 5.6 %collective-permute-start.8 = (f32[136,128]{1,0:T(8,128)S(1)}, f32[136,128]{1,0:T(8,128)S(1)}, u32[]{:S(2)}, u32[]{:S(2)}) collective-permute-start(f32[136,128]{1,0:T(8,128)S(1)} %slice_add_fusion), channel_id=1, source_target_pairs={{0,8},{4,12},{8,0},{12,4},{1,9},{5,13},{9,1},{13,5},{2,10},{6,14},... | collective-permute-start | bytes 208904 | tf_op jit(solution)/shard_map/ppermute | solution.py:248
  20.6 4.3 %collective-permute-start.5 = (f32[128,128]{1,0:T(8,128)S(1)}, f32[128,128]{1,0:T(8,128)S(1)}, u32[]{:S(2)}, u32[]{:S(2)}) collective-permute-start(f32[128,128]{1,0:T(8,128)S(1)} %slice_add_fusion.1), channel_id=1, source_target_pairs={{0,4},{4,0},{8,12},{12,8},{1,5},{5,1},{9,13},{13,9},{2,6},{6,2},{1... | collective-permute-start | bytes 196616 | tf_op jit(solution)/shard_map/ppermute | solution.py:248
  23.0 7.5 %collective-permute-start.9 = (f32[136,128]{1,0:T(8,128)S(1)}, f32[136,128]{1,0:T(8,128)S(1)}, u32[]{:S(2)}, u32[]{:S(2)}) collective-permute-start(f32[136,128]{1,0:T(8,128)S(1)} %add.42.refs_2_), channel_id=1, source_target_pairs={{0,4},{4,0},{8,12},{12,8},{1,5},{5,1},{9,13},{13,9},{2,6},{6,2},{1... | collective-permute-start | bytes 208904 | tf_op jit(solution)/shard_map/ppermute | solution.py:248
  24.9 5.6 %collective-permute-start.6 = (f32[128,128]{1,0:T(8,128)S(1)}, f32[128,128]{1,0:T(8,128)S(1)}, u32[]{:S(2)}, u32[]{:S(2)}) collective-permute-start(f32[128,128]{1,0:T(8,128)S(1)} %add.40.refs_0_), channel_id=1, source_target_pairs={{0,8},{4,12},{8,0},{12,4},{1,9},{5,13},{9,1},{13,5},{2,10},{6,14},... | collective-permute-start | bytes 196616 | tf_op jit(solution)/shard_map/ppermute | solution.py:248
  30.8 5.0 %collective-permute-start.10 = (f32[128,256]{1,0:T(8,128)S(1)}, f32[128,256]{1,0:T(8,128)S(1)}, u32[]{:S(2)}, u32[]{:S(2)}) collective-permute-start(f32[128,256]{1,0:T(8,128)S(1)} %get-tuple-element.47.refs_0_), channel_id=1, source_target_pairs={{0,2},{2,0},{1,3},{3,1},{4,6},{6,4},{5,7},{7,5},{8,10},{10,8},{9,1... | collective-permute-start | bytes 393224 | tf_op jit(solution)/shard_map/ppermute | solution.py:248
  32.4 3.9 %collective-permute-start.11 = (f32[128,256]{1,0:T(8,128)S(1)}, f32[128,256]{1,0:T(8,128)S(1)}, u32[]{:S(2)}, u32[]{:S(2)}) collective-permute-start(f32[128,256]{1,0:T(8,128)S(1)} %get-tuple-element.47.refs_0_), channel_id=1, source_target_pairs={{0,1},{1,0},{2,3},{3,2},{4,5},{5,4},{6,7},{7,6},{8,9},{9,8},{10,11... | collective-permute-start | bytes 393224 | tf_op jit(solution)/shard_map/ppermute | solution.py:248
  35.8 1.3 %collective-permute-start.12 = (f32[128,256]{1,0:T(8,128)S(1)}, f32[128,256]{1,0:T(8,128)S(1)}, u32[]{:S(2)}, u32[]{:S(2)}) collective-permute-start(f32[128,256]{1,0:T(8,128)S(1)} %collective-permute-done.10.refs_1_), channel_id=1, source_target_pairs={{0,1},{1,0},{2,3},{3,2},{4,5},{5,4},{6,7},{7,6},{8,9},{9,8},{10,11... | collective-permute-start | bytes 393224 | tf_op jit(solution)/shard_map/ppermute | solution.py:248
  38.4 1.2 %collective-permute-start.13 = (f32[8,128]{1,0:T(8,128)S(1)}, f32[8,128]{1,0:T(8,128)S(1)}, u32[]{:S(2)}, u32[]{:S(2)}) collective-permute-start(f32[8,128]{1,0:T(8,128)S(1)} %get-tuple-element.49), channel_id=1, source_target_pairs={{0,1},{1,0},{2,3},{3,2},{4,5},{5,4},{6,7},{7,6},{8,9},{9,8},{10,11... | collective-permute-start | bytes 12296 | tf_op jit(solution)/shard_map/ppermute | solution.py:248
  39.6 3.0 %collective-permute-start.14 = (f32[8,128]{1,0:T(8,128)S(1)}, f32[8,128]{1,0:T(8,128)S(1)}, u32[]{:S(2)}, u32[]{:S(2)}) collective-permute-start(f32[8,128]{1,0:T(8,128)S(1)} %add.43), channel_id=1, source_target_pairs={{0,3},{1,2},{2,1},{3,0},{4,7},{5,6},{6,5},{7,4},{8,11},{9,10},{10,... | collective-permute-start | bytes 12296 | tf_op jit(solution)/shard_map/ppermute | solution.py:253
  42.6 4.8 %collective-permute-start.17 = (f32[8,128]{1,0:T(8,128)S(1)}, f32[8,128]{1,0:T(8,128)S(1)}, u32[]{:S(2)}, u32[]{:S(2)}) collective-permute-start(f32[8,128]{1,0:T(8,128)S(1)} %add.44), channel_id=1, source_target_pairs={{0,13},{1,12},{4,9},{5,8},{8,5},{9,4},{12,1},{13,0},{2,15},{3,14},... | collective-permute-start | bytes 12296 | tf_op jit(solution)/shard_map/ppermute | solution.py:253
  44.8 3.9 %collective-permute-start.16 = (f32[8,128]{1,0:T(8,128)S(1)}, f32[8,128]{1,0:T(8,128)S(1)}, u32[]{:S(2)}, u32[]{:S(2)}) collective-permute-start(f32[8,128]{1,0:T(8,128)S(1)} %add.44), channel_id=1, source_target_pairs={{0,9},{1,8},{4,13},{5,12},{8,1},{9,0},{12,5},{13,4},{2,11},{3,10},... | collective-permute-start | bytes 12296 | tf_op jit(solution)/shard_map/ppermute | solution.py:253
  45.3 3.4 %collective-permute-start.15 = (f32[8,128]{1,0:T(8,128)S(1)}, f32[8,128]{1,0:T(8,128)S(1)}, u32[]{:S(2)}, u32[]{:S(2)}) collective-permute-start(f32[8,128]{1,0:T(8,128)S(1)} %add.44), channel_id=1, source_target_pairs={{0,5},{1,4},{4,1},{5,0},{8,13},{9,12},{12,9},{13,8},{2,7},{3,6},{6... | collective-permute-start | bytes 12296 | tf_op jit(solution)/shard_map/ppermute | solution.py:253

commit v6 on v5

--- a/solution.py
+++ b/solution.py
@@ -33,7 +33,9 @@
 
 def product(a, b, dims):
     one = functools.partial(lax.dot_general, dimension_numbers=dims, preferred_element_type=F32)
-    return one(a[0], b[0]) + (one(a[0], b[1]) + one(a[1], b[0]))
+    rows = a[0].shape[0]
+    both = one(jnp.concatenate(a, axis=0), b[0])
+    return both[:rows] + (both[rows:] + one(a[0], b[1]))
 
 
 def live_mask(sizes_ref, sector, first, rows, cols):

time: 49.8 us -> 49.6 us (level)
  no operation moved by 1% of the time
where the time goes in v6:
time: 49.6 us; the launch traced here: 49.4 us
  starting transfers between devices  22.8 us (46%)
  waiting for transfers between devices  16.1 us (32%)
  Pallas kernels  7.69 us (16%)
  local copies, waits for them, and re-layouts  1.95 us (4%)
  between operations  0.78 us (2%)
    ppermute x14, starting transfers between devices, across(): return lax.ppermute(x, axis, [(i, i ^ step) for i in range(size)])  17.6 us
    ppermute x14, waiting for transfers between devices, across(): return lax.ppermute(x, axis, [(i, i ^ step) for i in range(size)])  12.2 us
    ppermute x4, starting transfers between devices, diagonally(): lax.ppermute(x, (axis, 'rep'), [(2 * i + c, 2 * (i ^ step) + 1 - c) for i...  5.23 us
    ppermute x4, waiting for transfers between devices, diagonally(): lax.ppermute(x, (axis, 'rep'), [(2 * i + c, 2 * (i ^ step) + 1 - c) for i...  3.87 us
    pallas_call x1, Pallas kernels, body(): pl.pallas_call(functools.partial(prepare_kernel, weight), out_shape=[shap...  2.4 us
    pallas_call x1, Pallas kernels, body(): pl.pallas_call(functools.partial(image_kernel, coupling, ncell, nsec), ou...  1.71 us
    pallas_call x1, Pallas kernels, body(): pl.pallas_call(functools.partial(corner_kernel, coupling, weight, ncell,...  1.17 us
  transfers between devices with their start and end apart: 18, of which 13 were waited for; matrix products, arithmetic and copies ran while one was open for 0% of the time, Pallas kernels for 8%

profile of v6, /device:TPU:0, one launch (start us, length us, event | category | flops | bytes accessed | tf_op | source)
XLA Modules:
  0.0 49.4 jit_solution(3366321277990763274)
XLA Ops:
  0.6 1.0 %dynamic-slice_bitcast_fusion = f32[128,256]{1,0:T(8,128)S(1)} fusion(f32[1,256,256]{2,1,0:T(8,128)} %psi_hbm.1, s32[]{:T(128)S(6)} %select_n.3), kind=kLoop, calls=%fused_computation.1 | loop fusion | bytes 262148 | tf_op jit(solution)/shard_map/dynamic_slice | solution.py:271
  1.6 0.0 copy-start.2
  1.6 0.0 copy-start.3
  1.6 3.0 %collective-permute-start = (f32[128,256]{1,0:T(8,128)S(1)}, f32[128,256]{1,0:T(8,128)S(1)}, u32[]{:S(2)}, u32[]{:S(2)}) collective-permute-start(f32[128,256]{1,0:T(8,128)S(1)} %dynamic-slice_bitcast_fusion), channel_id=1, source_target_pairs={{0,2},{2,0},{1,3},{3,1},{4,6},{6,4},{5,7},{7,5},{8,10},{10,8},{9,1... | collective-permute-start | bytes 393224 | tf_op jit(solution)/shard_map/ppermute | solution.py:250
  4.7 0.9 %copy-done.1 = f32[1,256,256]{2,1,0:T(8,128)S(1)} copy-done((f32[1,256,256]{2,1,0:T(8,128)S(1)}, f32[1,256,256]{2,1,0:T(8,128)}, u32[]{:S(2)}) %copy-start.1) | copy-done | bytes 262168
  5.6 2.4 %prepare.1 = (bf16[4,256,256]{2,1,0:T(8,128)(2,1)S(1)}, bf16[4,256,256]{2,1,0:T(8,128)(2,1)S(1)}, bf16[4,256,256]{2,1,0:T(8,128)(2,1)S(1)}, bf16[4,256,256]{2,1,...) custom-call(s32[2,2]{1,0:T(2,128)S(1)} %copy-done.2, ...), custom_call_target="tpu_custom_call" | custom-call | tf_op jit(solution)/shard_map/prepare/pallas_call | solution.py:278
  8.0 0.1 collective-permute-done
  8.2 0.1 collective-permute-start.1
  8.2 0.5 partial.2.refs_3_
  8.7 0.9 %collective-permute-done.1.refs_1_ = f32[128,256]{1,0:T(8,128)S(1)} collective-permute-done((f32[128,256]{1,0:T(8,128)S(1)}, f32[128,256]{1,0:T(8,128)S(1)}, u32[]{:S(2)}, u32[]{:S(2)}) %collective-permute-start.1) | collective-permute-done | bytes 131104 | tf_op jit(solution)/shard_map/ppermute | solution.py:250
  9.6 1.7 %image.1 = (f32[2,256,256]{2,1,0:T(8,128)S(1)}, f32[8,128]{1,0:T(8,128)S(1)}, f32[4,256,256]{2,1,0:T(8,128)S(1)}, bf16[4,256,256]{2,1,0:T(8,128)(2,1)S(1)}, bf16...) custom-call(f32[128,256]{1,0:T(8,128)S(1)} %bitcast_multiply_fusion.refs_1_.refs_0_, ...), custom_call_target="tpu_custom_call" | custom-call | tf_op jit(solution)/shard_map/image/pallas_call | solution.py:311
  11.3 0.2 collective-permute-start.3
  11.5 0.4 collective-permute-start.2
  11.9 0.4 keep.1
  12.3 0.5 collective-permute-done.3
  12.7 1.8 %collective-permute-start.7 = (f32[136,128]{1,0:T(8,128)S(1)}, f32[136,128]{1,0:T(8,128)S(1)}, u32[]{:S(2)}, u32[]{:S(2)}) collective-permute-start(f32[136,128]{1,0:T(8,128)S(1)} %slice.23), channel_id=1, source_target_pairs={{0,2},{2,0},{1,3},{3,1},{4,6},{6,4},{5,7},{7,5},{8,10},{10,8},{9,1... | collective-permute-start | bytes 208904 | tf_op jit(solution)/shard_map/ppermute | solution.py:250
  14.6 0.3 collective-permute-start.4
  14.8 0.0 collective-permute-done.2
  14.9 2.4 %collective-permute-done.7 = f32[136,128]{1,0:T(8,128)S(1)} collective-permute-done((f32[136,128]{1,0:T(8,128)S(1)}, f32[136,128]{1,0:T(8,128)S(1)}, u32[]{:S(2)}, u32[]{:S(2)}) %collective-permute-start.7) | collective-permute-done | bytes 69664 | tf_op jit(solution)/shard_map/ppermute | solution.py:250
  17.3 3.2 %collective-permute-start.8 = (f32[136,128]{1,0:T(8,128)S(1)}, f32[136,128]{1,0:T(8,128)S(1)}, u32[]{:S(2)}, u32[]{:S(2)}) collective-permute-start(f32[136,128]{1,0:T(8,128)S(1)} %slice_add_fusion), channel_id=1, source_target_pairs={{0,8},{4,12},{8,0},{12,4},{1,9},{5,13},{9,1},{13,5},{2,10},{6,14},... | collective-permute-start | bytes 208904 | tf_op jit(solution)/shard_map/ppermute | solution.py:250
  20.5 0.0 collective-permute-done.4
  20.5 1.6 %collective-permute-start.5 = (f32[128,128]{1,0:T(8,128)S(1)}, f32[128,128]{1,0:T(8,128)S(1)}, u32[]{:S(2)}, u32[]{:S(2)}) collective-permute-start(f32[128,128]{1,0:T(8,128)S(1)} %slice_add_fusion.1), channel_id=1, source_target_pairs={{0,4},{4,0},{8,12},{12,8},{1,5},{5,1},{9,13},{13,9},{2,6},{6,2},{1... | collective-permute-start | bytes 196616 | tf_op jit(solution)/shard_map/ppermute | solution.py:250
  22.1 0.7 %collective-permute-done.8 = f32[136,128]{1,0:T(8,128)S(1)} collective-permute-done((f32[136,128]{1,0:T(8,128)S(1)}, f32[136,128]{1,0:T(8,128)S(1)}, u32[]{:S(2)}, u32[]{:S(2)}) %collective-permute-start.8) | collective-permute-done | bytes 69664 | tf_op jit(solution)/shard_map/ppermute | solution.py:250
  22.9 1.9 %collective-permute-start.9 = (f32[136,128]{1,0:T(8,128)S(1)}, f32[136,128]{1,0:T(8,128)S(1)}, u32[]{:S(2)}, u32[]{:S(2)}) collective-permute-start(f32[136,128]{1,0:T(8,128)S(1)} %add.42.refs_2_), channel_id=1, source_target_pairs={{0,4},{4,0},{8,12},{12,8},{1,5},{5,1},{9,13},{13,9},{2,6},{6,2},{1... | collective-permute-start | bytes 208904 | tf_op jit(solution)/shard_map/ppermute | solution.py:250
  24.7 0.1 collective-permute-done.5
  24.8 3.3 %collective-permute-start.6 = (f32[128,128]{1,0:T(8,128)S(1)}, f32[128,128]{1,0:T(8,128)S(1)}, u32[]{:S(2)}, u32[]{:S(2)}) collective-permute-start(f32[128,128]{1,0:T(8,128)S(1)} %add.40.refs_0_), channel_id=1, source_target_pairs={{0,8},{4,12},{8,0},{12,4},{1,9},{5,13},{9,1},{13,5},{2,10},{6,14},... | collective-permute-start | bytes 196616 | tf_op jit(solution)/shard_map/ppermute | solution.py:250
  28.2 2.3 %collective-permute-done.6.refs_1_ = f32[128,128]{1,0:T(8,128)S(1)} collective-permute-done((f32[128,128]{1,0:T(8,128)S(1)}, f32[128,128]{1,0:T(8,128)S(1)}, u32[]{:S(2)}, u32[]{:S(2)}) %collective-permute-start.6) | collective-permute-done | bytes 65568 | tf_op jit(solution)/shard_map/ppermute | solution.py:250
  30.4 0.0 collective-permute-done.9.refs_3_
  30.4 0.3 fresh.1
  30.7 1.6 %collective-permute-start.10 = (f32[128,256]{1,0:T(8,128)S(1)}, f32[128,256]{1,0:T(8,128)S(1)}, u32[]{:S(2)}, u32[]{:S(2)}) collective-permute-start(f32[128,256]{1,0:T(8,128)S(1)} %get-tuple-element.47.refs_0_), channel_id=1, source_target_pairs={{0,2},{2,0},{1,3},{3,1},{4,6},{6,4},{5,7},{7,5},{8,10},{10,8},{9,1... | collective-permute-start | bytes 393224 | tf_op jit(solution)/shard_map/ppermute | solution.py:250
  32.3 0.0 collective-permute-start.11
  32.3 3.4 %collective-permute-done.10.refs_1_ = f32[128,256]{1,0:T(8,128)S(1)} collective-permute-done((f32[128,256]{1,0:T(8,128)S(1)}, f32[128,256]{1,0:T(8,128)S(1)}, u32[]{:S(2)}, u32[]{:S(2)}) %collective-permute-start.10) | collective-permute-done | bytes 131104 | tf_op jit(solution)/shard_map/ppermute | solution.py:250
  35.7 0.0 collective-permute-start.12
  35.7 0.5 partial.3.refs_4_
  36.2 0.0 collective-permute-done.11.refs_2_
  36.2 0.9 %collective-permute-done.12.refs_3_ = f32[128,256]{1,0:T(8,128)S(1)} collective-permute-done((f32[128,256]{1,0:T(8,128)S(1)}, f32[128,256]{1,0:T(8,128)S(1)}, u32[]{:S(2)}, u32[]{:S(2)}) %collective-permute-start.12) | collective-permute-done | bytes 131104 | tf_op jit(solution)/shard_map/ppermute | solution.py:250
  37.1 1.2 %corner.1 = (f32[8,128]{1,0:T(8,128)S(1)}, f32[256,256]{1,0:T(8,128)S(1)}, f32[8,128]{1,0:T(8,128)S(1)}) custom-call(f32[128,256]{1,0:T(8,128)S(1)} %get-tuple-element.47.refs_0_, f32[128,256]{1,0:T(8,128)S(1)} %collective-permute-done.10.refs_1_, f32[128,256]{1,0:T(8,128)S(1)} %collective-permute-done.11.refs_2_, ...), custom_call_target="tpu_custom_call" | custom-call | tf_op jit(solution)/shard_map/corner/pallas_call | solution.py:360
  38.2 0.2 collective-permute-start.13
  38.5 1.0 %collective-permute-done.13 = f32[8,128]{1,0:T(8,128)S(1)} collective-permute-done((f32[8,128]{1,0:T(8,128)S(1)}, f32[8,128]{1,0:T(8,128)S(1)}, u32[]{:S(2)}, u32[]{:S(2)}) %collective-permute-start.13) | collective-permute-done | bytes 4128 | tf_op jit(solution)/shard_map/ppermute | solution.py:250
  39.5 1.3 %collective-permute-start.14 = (f32[8,128]{1,0:T(8,128)S(1)}, f32[8,128]{1,0:T(8,128)S(1)}, u32[]{:S(2)}, u32[]{:S(2)}) collective-permute-start(f32[8,128]{1,0:T(8,128)S(1)} %add.43), channel_id=1, source_target_pairs={{0,3},{1,2},{2,1},{3,0},{4,7},{5,6},{6,5},{7,4},{8,11},{9,10},{10,... | collective-permute-start | bytes 12296 | tf_op jit(solution)/shard_map/ppermute | solution.py:255
  40.8 1.7 %collective-permute-done.14 = f32[8,128]{1,0:T(8,128)S(1)} collective-permute-done((f32[8,128]{1,0:T(8,128)S(1)}, f32[8,128]{1,0:T(8,128)S(1)}, u32[]{:S(2)}, u32[]{:S(2)}) %collective-permute-start.14) | collective-permute-done | bytes 4128 | tf_op jit(solution)/shard_map/ppermute | solution.py:255
  42.5 2.1 %collective-permute-start.17 = (f32[8,128]{1,0:T(8,128)S(1)}, f32[8,128]{1,0:T(8,128)S(1)}, u32[]{:S(2)}, u32[]{:S(2)}) collective-permute-start(f32[8,128]{1,0:T(8,128)S(1)} %add.44), channel_id=1, source_target_pairs={{0,13},{1,12},{4,9},{5,8},{8,5},{9,4},{12,1},{13,0},{2,15},{3,14},... | collective-permute-start | bytes 12296 | tf_op jit(solution)/shard_map/ppermute | solution.py:255
  44.7 0.6 %collective-permute-start.16 = (f32[8,128]{1,0:T(8,128)S(1)}, f32[8,128]{1,0:T(8,128)S(1)}, u32[]{:S(2)}, u32[]{:S(2)}) collective-permute-start(f32[8,128]{1,0:T(8,128)S(1)} %add.44), channel_id=1, source_target_pairs={{0,9},{1,8},{4,13},{5,12},{8,1},{9,0},{12,5},{13,4},{2,11},{3,10},... | collective-permute-start | bytes 12296 | tf_op jit(solution)/shard_map/ppermute | solution.py:255
  45.2 1.2 %collective-permute-start.15 = (f32[8,128]{1,0:T(8,128)S(1)}, f32[8,128]{1,0:T(8,128)S(1)}, u32[]{:S(2)}, u32[]{:S(2)}) collective-permute-start(f32[8,128]{1,0:T(8,128)S(1)} %add.44), channel_id=1, source_target_pairs={{0,5},{1,4},{4,1},{5,0},{8,13},{9,12},{12,9},{13,8},{2,7},{3,6},{6... | collective-permute-start | bytes 12296 | tf_op jit(solution)/shard_map/ppermute | solution.py:255
  46.4 0.9 %collective-permute-done.17 = f32[8,128]{1,0:T(8,128)S(1)} collective-permute-done((f32[8,128]{1,0:T(8,128)S(1)}, f32[8,128]{1,0:T(8,128)S(1)}, u32[]{:S(2)}, u32[]{:S(2)}) %collective-permute-start.17) | collective-permute-done | bytes 4128 | tf_op jit(solution)/shard_map/ppermute | solution.py:255
  47.3 1.2 %collective-permute-done.16 = f32[8,128]{1,0:T(8,128)S(1)} collective-permute-done((f32[8,128]{1,0:T(8,128)S(1)}, f32[8,128]{1,0:T(8,128)S(1)}, u32[]{:S(2)}, u32[]{:S(2)}) %collective-permute-start.16) | collective-permute-done | bytes 4128 | tf_op jit(solution)/shard_map/ppermute | solution.py:255
  48.6 0.0 collective-permute-done.15
  48.6 0.8 %result.1 = (f32[1,256,256]{2,1,0:T(8,128)}, f32[1]{0:T(128)}) custom-call(f32[8,128]{1,0:T(8,128)S(1)} %add_add_fusion.sums_ref, f32[8,128]{1,0:T(8,128)S(1)} %get-tuple-element.50.info_ref, f32[2,256,256]{2,1,0:T(8,128)S(1)} %get-tuple-element.45.refs_4_.refs_6_.full_ref, f32[256,256]{1,0:T(8,128)S(1)} %get-tuple-element.51.fresh_ref), custom_call_target="tpu_custom_call" | custom-call | tf_op jit(solution)/shard_map/result/pallas_call | solution.py:373
  (17 shorter events, 0.1 us)
Async XLA Ops:
  0.6 4.0 %copy-start = (f32[1,256,256]{2,1,0:T(8,128)S(1)}, f32[1,256,256]{2,1,0:T(8,128)}, u32[]{:S(2)}) copy-start(f32[1,256,256]{2,1,0:T(8,128)} %psi_hbm.1) | copy-start | bytes 786436
  1.6 3.0 %copy-start.2 = (s32[2,2]{1,0:T(2,128)S(1)}, s32[2,2]{1,0:T(2,128)}, u32[]{:S(2)}) copy-start(s32[2,2]{1,0:T(2,128)} %sizes_ref.1) | copy-start | bytes 52
  1.6 3.0 %copy-start.3 = (s32[4,1]{0,1:T(1,128)S(1)}, s32[4,1]{0,1:T(1,128)}, u32[]{:S(2)}) copy-start(s32[4,1]{0,1:T(1,128)} %param.9) | copy-start | bytes 52
  1.6 6.5 %collective-permute-start = (f32[128,256]{1,0:T(8,128)S(1)}, f32[128,256]{1,0:T(8,128)S(1)}, u32[]{:S(2)}, u32[]{:S(2)}) collective-permute-start(f32[128,256]{1,0:T(8,128)S(1)} %dynamic-slice_bitcast_fusion), channel_id=1, source_target_pairs={{0,2},{2,0},{1,3},{3,1},{4,6},{6,4},{5,7},{7,5},{8,10},{10,8},{9,1... | collective-permute-start | bytes 393224 | tf_op jit(solution)/shard_map/ppermute | solution.py:250
  4.7 1.0 %copy-start.1 = (f32[1,256,256]{2,1,0:T(8,128)S(1)}, f32[1,256,256]{2,1,0:T(8,128)}, u32[]{:S(2)}) copy-start(f32[1,256,256]{2,1,0:T(8,128)} %diag_hbm.1) | copy-start | bytes 786436
  8.2 1.4 %collective-permute-start.1 = (f32[128,256]{1,0:T(8,128)S(1)}, f32[128,256]{1,0:T(8,128)S(1)}, u32[]{:S(2)}, u32[]{:S(2)}) collective-permute-start(f32[128,256]{1,0:T(8,128)S(1)} %bitcast_multiply_fusion.refs_1_.refs_0_), channel_id=1, source_target_pairs={{0,1},{1,0},{2,3},{3,2},{4,5},{5,4},{6,7},{7,6},{8,9},{9,8},{10,11... | collective-permute-start | bytes 393224 | tf_op jit(solution)/shard_map/ppermute | solution.py:250
  11.3 1.4 %collective-permute-start.3 = (f32[264,128]{1,0:T(8,128)S(1)}, f32[264,128]{1,0:T(8,128)S(1)}, u32[]{:S(2)}, u32[]{:S(2)}) collective-permute-start(f32[264,128]{1,0:T(8,128)S(1)} %get-tuple-element.44), channel_id=1, source_target_pairs={{0,1},{1,0},{2,3},{3,2},{4,5},{5,4},{6,7},{7,6},{8,9},{9,8},{10,11... | collective-permute-start | bytes 405512 | tf_op jit(solution)/shard_map/ppermute | solution.py:250
  11.5 3.3 %collective-permute-start.2 = (f32[264,128]{1,0:T(8,128)S(1)}, f32[264,128]{1,0:T(8,128)S(1)}, u32[]{:S(2)}, u32[]{:S(2)}) collective-permute-start(f32[264,128]{1,0:T(8,128)S(1)} %get-tuple-element.42), channel_id=1, source_target_pairs={{0,1},{1,0},{2,3},{3,2},{4,5},{5,4},{6,7},{7,6},{8,9},{9,8},{10,11... | collective-permute-start | bytes 405512 | tf_op jit(solution)/shard_map/ppermute | solution.py:250
  12.7 4.5 %collective-permute-start.7 = (f32[136,128]{1,0:T(8,128)S(1)}, f32[136,128]{1,0:T(8,128)S(1)}, u32[]{:S(2)}, u32[]{:S(2)}) collective-permute-start(f32[136,128]{1,0:T(8,128)S(1)} %slice.23), channel_id=1, source_target_pairs={{0,2},{2,0},{1,3},{3,1},{4,6},{6,4},{5,7},{7,5},{8,10},{10,8},{9,1... | collective-permute-start | bytes 208904 | tf_op jit(solution)/shard_map/ppermute | solution.py:250
  14.6 5.9 %collective-permute-start.4 = (f32[128,128]{1,0:T(8,128)S(1)}, f32[128,128]{1,0:T(8,128)S(1)}, u32[]{:S(2)}, u32[]{:S(2)}) collective-permute-start(f32[128,128]{1,0:T(8,128)S(1)} %slice.21), channel_id=1, source_target_pairs={{0,2},{2,0},{1,3},{3,1},{4,6},{6,4},{5,7},{7,5},{8,10},{10,8},{9,1... | collective-permute-start | bytes 196616 | tf_op jit(solution)/shard_map/ppermute | solution.py:250
  17.3 5.6 %collective-permute-start.8 = (f32[136,128]{1,0:T(8,128)S(1)}, f32[136,128]{1,0:T(8,128)S(1)}, u32[]{:S(2)}, u32[]{:S(2)}) collective-permute-start(f32[136,128]{1,0:T(8,128)S(1)} %slice_add_fusion), channel_id=1, source_target_pairs={{0,8},{4,12},{8,0},{12,4},{1,9},{5,13},{9,1},{13,5},{2,10},{6,14},... | collective-permute-start | bytes 208904 | tf_op jit(solution)/shard_map/ppermute | solution.py:250
  20.5 4.3 %collective-permute-start.5 = (f32[128,128]{1,0:T(8,128)S(1)}, f32[128,128]{1,0:T(8,128)S(1)}, u32[]{:S(2)}, u32[]{:S(2)}) collective-permute-start(f32[128,128]{1,0:T(8,128)S(1)} %slice_add_fusion.1), channel_id=1, source_target_pairs={{0,4},{4,0},{8,12},{12,8},{1,5},{5,1},{9,13},{13,9},{2,6},{6,2},{1... | collective-permute-start | bytes 196616 | tf_op jit(solution)/shard_map/ppermute | solution.py:250
  22.9 7.5 %collective-permute-start.9 = (f32[136,128]{1,0:T(8,128)S(1)}, f32[136,128]{1,0:T(8,128)S(1)}, u32[]{:S(2)}, u32[]{:S(2)}) collective-permute-start(f32[136,128]{1,0:T(8,128)S(1)} %add.42.refs_2_), channel_id=1, source_target_pairs={{0,4},{4,0},{8,12},{12,8},{1,5},{5,1},{9,13},{13,9},{2,6},{6,2},{1... | collective-permute-start | bytes 208904 | tf_op jit(solution)/shard_map/ppermute | solution.py:250
  24.8 5.6 %collective-permute-start.6 = (f32[128,128]{1,0:T(8,128)S(1)}, f32[128,128]{1,0:T(8,128)S(1)}, u32[]{:S(2)}, u32[]{:S(2)}) collective-permute-start(f32[128,128]{1,0:T(8,128)S(1)} %add.40.refs_0_), channel_id=1, source_target_pairs={{0,8},{4,12},{8,0},{12,4},{1,9},{5,13},{9,1},{13,5},{2,10},{6,14},... | collective-permute-start | bytes 196616 | tf_op jit(solution)/shard_map/ppermute | solution.py:250
  30.7 5.0 %collective-permute-start.10 = (f32[128,256]{1,0:T(8,128)S(1)}, f32[128,256]{1,0:T(8,128)S(1)}, u32[]{:S(2)}, u32[]{:S(2)}) collective-permute-start(f32[128,256]{1,0:T(8,128)S(1)} %get-tuple-element.47.refs_0_), channel_id=1, source_target_pairs={{0,2},{2,0},{1,3},{3,1},{4,6},{6,4},{5,7},{7,5},{8,10},{10,8},{9,1... | collective-permute-start | bytes 393224 | tf_op jit(solution)/shard_map/ppermute | solution.py:250
  32.3 3.9 %collective-permute-start.11 = (f32[128,256]{1,0:T(8,128)S(1)}, f32[128,256]{1,0:T(8,128)S(1)}, u32[]{:S(2)}, u32[]{:S(2)}) collective-permute-start(f32[128,256]{1,0:T(8,128)S(1)} %get-tuple-element.47.refs_0_), channel_id=1, source_target_pairs={{0,1},{1,0},{2,3},{3,2},{4,5},{5,4},{6,7},{7,6},{8,9},{9,8},{10,11... | collective-permute-start | bytes 393224 | tf_op jit(solution)/shard_map/ppermute | solution.py:250
  35.7 1.3 %collective-permute-start.12 = (f32[128,256]{1,0:T(8,128)S(1)}, f32[128,256]{1,0:T(8,128)S(1)}, u32[]{:S(2)}, u32[]{:S(2)}) collective-permute-start(f32[128,256]{1,0:T(8,128)S(1)} %collective-permute-done.10.refs_1_), channel_id=1, source_target_pairs={{0,1},{1,0},{2,3},{3,2},{4,5},{5,4},{6,7},{7,6},{8,9},{9,8},{10,11... | collective-permute-start | bytes 393224 | tf_op jit(solution)/shard_map/ppermute | solution.py:250
  38.2 1.2 %collective-permute-start.13 = (f32[8,128]{1,0:T(8,128)S(1)}, f32[8,128]{1,0:T(8,128)S(1)}, u32[]{:S(2)}, u32[]{:S(2)}) collective-permute-start(f32[8,128]{1,0:T(8,128)S(1)} %get-tuple-element.49), channel_id=1, source_target_pairs={{0,1},{1,0},{2,3},{3,2},{4,5},{5,4},{6,7},{7,6},{8,9},{9,8},{10,11... | collective-permute-start | bytes 12296 | tf_op jit(solution)/shard_map/ppermute | solution.py:250
  39.5 3.0 %collective-permute-start.14 = (f32[8,128]{1,0:T(8,128)S(1)}, f32[8,128]{1,0:T(8,128)S(1)}, u32[]{:S(2)}, u32[]{:S(2)}) collective-permute-start(f32[8,128]{1,0:T(8,128)S(1)} %add.43), channel_id=1, source_target_pairs={{0,3},{1,2},{2,1},{3,0},{4,7},{5,6},{6,5},{7,4},{8,11},{9,10},{10,... | collective-permute-start | bytes 12296 | tf_op jit(solution)/shard_map/ppermute | solution.py:255
  42.5 4.8 %collective-permute-start.17 = (f32[8,128]{1,0:T(8,128)S(1)}, f32[8,128]{1,0:T(8,128)S(1)}, u32[]{:S(2)}, u32[]{:S(2)}) collective-permute-start(f32[8,128]{1,0:T(8,128)S(1)} %add.44), channel_id=1, source_target_pairs={{0,13},{1,12},{4,9},{5,8},{8,5},{9,4},{12,1},{13,0},{2,15},{3,14},... | collective-permute-start | bytes 12296 | tf_op jit(solution)/shard_map/ppermute | solution.py:255
  44.7 3.9 %collective-permute-start.16 = (f32[8,128]{1,0:T(8,128)S(1)}, f32[8,128]{1,0:T(8,128)S(1)}, u32[]{:S(2)}, u32[]{:S(2)}) collective-permute-start(f32[8,128]{1,0:T(8,128)S(1)} %add.44), channel_id=1, source_target_pairs={{0,9},{1,8},{4,13},{5,12},{8,1},{9,0},{12,5},{13,4},{2,11},{3,10},... | collective-permute-start | bytes 12296 | tf_op jit(solution)/shard_map/ppermute | solution.py:255
  45.2 3.4 %collective-permute-start.15 = (f32[8,128]{1,0:T(8,128)S(1)}, f32[8,128]{1,0:T(8,128)S(1)}, u32[]{:S(2)}, u32[]{:S(2)}) collective-permute-start(f32[8,128]{1,0:T(8,128)S(1)} %add.44), channel_id=1, source_target_pairs={{0,5},{1,4},{4,1},{5,0},{8,13},{9,12},{12,9},{13,8},{2,7},{3,6},{6... | collective-permute-start | bytes 12296 | tf_op jit(solution)/shard_map/ppermute | solution.py:255

commit v7 on v6

--- a/solution.py
+++ b/solution.py
@@ -225,8 +225,10 @@
     info_ref[...] = jnp.where(row == 0, norm, jnp.where(row == 1, length, cross_ref[1:2, :1]))
 
 
-def result_kernel(ncell, sums_ref, info_ref, full_ref, fresh_ref, vector_ref, energy_ref):
-    sums, info = sums_ref[...], info_ref[...]
+def result_kernel(ncell, *refs):
+    info_ref, full_ref, fresh_ref, vector_ref, energy_ref = refs[-5:]
+    info = info_ref[...]
+    sums = functools.reduce(lambda x, y: x + y, [ref[...] for ref in refs[:-5]])
     norm, length, theta = info[0:1, :1], info[1:2, :1], info[2:3, :1]
     corner = sums[0:1, :1] / (ncell * length)
     cross = sums[1:2, :1] / (ncell * jnp.sqrt(length))
@@ -369,15 +371,16 @@
     sums = sums + across(sums, "rep", 1)
     for axis in ("sector", "terms"):
         parts = [diagonally(sums, axis, step) for step in range(1, lax.axis_size(axis))]
-        sums = functools.reduce(lambda x, y: x + y, parts, sums)
+        if axis == "sector":
+            sums = functools.reduce(lambda x, y: x + y, parts, sums)
     vector, energy = pl.pallas_call(
         functools.partial(result_kernel, ncell),
         out_shape=[shape((1, blk, blk), F32), shape((1,), F32)],
-        in_specs=[vmem] * 4,
+        in_specs=[vmem] * (len(parts) + 4),
         out_specs=[vmem, smem],
         compiler_params=PARAMS,
         name="result",
-    )(sums, info, full, direction)
+    )(sums, *parts, info, full, direction)
     return vector, energy
 
 

time: 49.6 us -> 49.6 us (level)
  no operation moved by 1% of the time
where the time goes in v7:
time: 49.6 us; the launch traced here: 49.4 us
  starting transfers between devices  22.8 us (46%)
  waiting for transfers between devices  16.1 us (32%)
  Pallas kernels  7.69 us (16%)
  local copies, waits for them, and re-layouts  1.95 us (4%)
  between operations  0.78 us (2%)
    ppermute x14, starting transfers between devices, across(): return lax.ppermute(x, axis, [(i, i ^ step) for i in range(size)])  17.6 us
    ppermute x14, waiting for transfers between devices, across(): return lax.ppermute(x, axis, [(i, i ^ step) for i in range(size)])  12.2 us
    ppermute x4, starting transfers between devices, diagonally(): lax.ppermute(x, (axis, 'rep'), [(2 * i + c, 2 * (i ^ step) + 1 - c) for i...  5.23 us
    ppermute x4, waiting for transfers between devices, diagonally(): lax.ppermute(x, (axis, 'rep'), [(2 * i + c, 2 * (i ^ step) + 1 - c) for i...  3.87 us
    pallas_call x1, Pallas kernels, body(): pl.pallas_call(functools.partial(prepare_kernel, weight), out_shape=[shap...  2.4 us
    pallas_call x1, Pallas kernels, body(): pl.pallas_call(functools.partial(image_kernel, coupling, ncell, nsec), ou...  1.71 us
    pallas_call x1, Pallas kernels, body(): pl.pallas_call(functools.partial(corner_kernel, coupling, weight, ncell,...  1.17 us
  transfers between devices with their start and end apart: 18, of which 13 were waited for; matrix products, arithmetic and copies ran while one was open for 0% of the time, Pallas kernels for 8%

profile of v7, /device:TPU:0, one launch (start us, length us, event | category | flops | bytes accessed | tf_op | source)
XLA Modules:
  0.0 49.4 jit_solution(4142746746824524741)
XLA Ops:
  0.6 1.0 %dynamic-slice_bitcast_fusion = f32[128,256]{1,0:T(8,128)S(1)} fusion(f32[1,256,256]{2,1,0:T(8,128)} %psi_hbm.1, s32[]{:T(128)S(6)} %select_n.3), kind=kLoop, calls=%fused_computation.1 | loop fusion | bytes 262148 | tf_op jit(solution)/shard_map/dynamic_slice | solution.py:273
  1.6 0.0 copy-start.2
  1.6 0.0 copy-start.3
  1.6 3.0 %collective-permute-start = (f32[128,256]{1,0:T(8,128)S(1)}, f32[128,256]{1,0:T(8,128)S(1)}, u32[]{:S(2)}, u32[]{:S(2)}) collective-permute-start(f32[128,256]{1,0:T(8,128)S(1)} %dynamic-slice_bitcast_fusion), channel_id=1, source_target_pairs={{0,2},{2,0},{1,3},{3,1},{4,6},{6,4},{5,7},{7,5},{8,10},{10,8},{9,1... | collective-permute-start | bytes 393224 | tf_op jit(solution)/shard_map/ppermute | solution.py:252
  4.7 0.9 %copy-done.1 = f32[1,256,256]{2,1,0:T(8,128)S(1)} copy-done((f32[1,256,256]{2,1,0:T(8,128)S(1)}, f32[1,256,256]{2,1,0:T(8,128)}, u32[]{:S(2)}) %copy-start.1) | copy-done | bytes 262168
  5.6 2.4 %prepare.1 = (bf16[4,256,256]{2,1,0:T(8,128)(2,1)S(1)}, bf16[4,256,256]{2,1,0:T(8,128)(2,1)S(1)}, bf16[4,256,256]{2,1,0:T(8,128)(2,1)S(1)}, bf16[4,256,256]{2,1,...) custom-call(s32[2,2]{1,0:T(2,128)S(1)} %copy-done.2, ...), custom_call_target="tpu_custom_call" | custom-call | tf_op jit(solution)/shard_map/prepare/pallas_call | solution.py:280
  8.0 0.1 collective-permute-done
  8.2 0.1 collective-permute-start.1
  8.2 0.5 partial.2.refs_3_
  8.7 0.9 %collective-permute-done.1.refs_1_ = f32[128,256]{1,0:T(8,128)S(1)} collective-permute-done((f32[128,256]{1,0:T(8,128)S(1)}, f32[128,256]{1,0:T(8,128)S(1)}, u32[]{:S(2)}, u32[]{:S(2)}) %collective-permute-start.1) | collective-permute-done | bytes 131104 | tf_op jit(solution)/shard_map/ppermute | solution.py:252
  9.6 1.7 %image.1 = (f32[2,256,256]{2,1,0:T(8,128)S(1)}, f32[8,128]{1,0:T(8,128)S(1)}, f32[4,256,256]{2,1,0:T(8,128)S(1)}, bf16[4,256,256]{2,1,0:T(8,128)(2,1)S(1)}, bf16...) custom-call(f32[128,256]{1,0:T(8,128)S(1)} %bitcast_multiply_fusion.refs_1_.refs_0_, ...), custom_call_target="tpu_custom_call" | custom-call | tf_op jit(solution)/shard_map/image/pallas_call | solution.py:313
  11.3 0.2 collective-permute-start.3
  11.5 0.4 collective-permute-start.2
  11.9 0.4 keep.1
  12.3 0.5 collective-permute-done.3
  12.7 1.8 %collective-permute-start.7 = (f32[136,128]{1,0:T(8,128)S(1)}, f32[136,128]{1,0:T(8,128)S(1)}, u32[]{:S(2)}, u32[]{:S(2)}) collective-permute-start(f32[136,128]{1,0:T(8,128)S(1)} %slice.23), channel_id=1, source_target_pairs={{0,2},{2,0},{1,3},{3,1},{4,6},{6,4},{5,7},{7,5},{8,10},{10,8},{9,1... | collective-permute-start | bytes 208904 | tf_op jit(solution)/shard_map/ppermute | solution.py:252
  14.6 0.3 collective-permute-start.4
  14.8 0.0 collective-permute-done.2
  14.9 2.4 %collective-permute-done.7 = f32[136,128]{1,0:T(8,128)S(1)} collective-permute-done((f32[136,128]{1,0:T(8,128)S(1)}, f32[136,128]{1,0:T(8,128)S(1)}, u32[]{:S(2)}, u32[]{:S(2)}) %collective-permute-start.7) | collective-permute-done | bytes 69664 | tf_op jit(solution)/shard_map/ppermute | solution.py:252
  17.3 3.2 %collective-permute-start.8 = (f32[136,128]{1,0:T(8,128)S(1)}, f32[136,128]{1,0:T(8,128)S(1)}, u32[]{:S(2)}, u32[]{:S(2)}) collective-permute-start(f32[136,128]{1,0:T(8,128)S(1)} %slice_add_fusion), channel_id=1, source_target_pairs={{0,8},{4,12},{8,0},{12,4},{1,9},{5,13},{9,1},{13,5},{2,10},{6,14},... | collective-permute-start | bytes 208904 | tf_op jit(solution)/shard_map/ppermute | solution.py:252
  20.5 0.0 collective-permute-done.4
  20.5 1.6 %collective-permute-start.5 = (f32[128,128]{1,0:T(8,128)S(1)}, f32[128,128]{1,0:T(8,128)S(1)}, u32[]{:S(2)}, u32[]{:S(2)}) collective-permute-start(f32[128,128]{1,0:T(8,128)S(1)} %slice_add_fusion.1), channel_id=1, source_target_pairs={{0,4},{4,0},{8,12},{12,8},{1,5},{5,1},{9,13},{13,9},{2,6},{6,2},{1... | collective-permute-start | bytes 196616 | tf_op jit(solution)/shard_map/ppermute | solution.py:252
  22.1 0.7 %collective-permute-done.8 = f32[136,128]{1,0:T(8,128)S(1)} collective-permute-done((f32[136,128]{1,0:T(8,128)S(1)}, f32[136,128]{1,0:T(8,128)S(1)}, u32[]{:S(2)}, u32[]{:S(2)}) %collective-permute-start.8) | collective-permute-done | bytes 69664 | tf_op jit(solution)/shard_map/ppermute | solution.py:252
  22.9 1.9 %collective-permute-start.9 = (f32[136,128]{1,0:T(8,128)S(1)}, f32[136,128]{1,0:T(8,128)S(1)}, u32[]{:S(2)}, u32[]{:S(2)}) collective-permute-start(f32[136,128]{1,0:T(8,128)S(1)} %add.33.refs_2_), channel_id=1, source_target_pairs={{0,4},{4,0},{8,12},{12,8},{1,5},{5,1},{9,13},{13,9},{2,6},{6,2},{1... | collective-permute-start | bytes 208904 | tf_op jit(solution)/shard_map/ppermute | solution.py:252
  24.7 0.1 collective-permute-done.5
  24.8 3.3 %collective-permute-start.6 = (f32[128,128]{1,0:T(8,128)S(1)}, f32[128,128]{1,0:T(8,128)S(1)}, u32[]{:S(2)}, u32[]{:S(2)}) collective-permute-start(f32[128,128]{1,0:T(8,128)S(1)} %add.31.refs_0_), channel_id=1, source_target_pairs={{0,8},{4,12},{8,0},{12,4},{1,9},{5,13},{9,1},{13,5},{2,10},{6,14},... | collective-permute-start | bytes 196616 | tf_op jit(solution)/shard_map/ppermute | solution.py:252
  28.2 2.3 %collective-permute-done.6.refs_1_ = f32[128,128]{1,0:T(8,128)S(1)} collective-permute-done((f32[128,128]{1,0:T(8,128)S(1)}, f32[128,128]{1,0:T(8,128)S(1)}, u32[]{:S(2)}, u32[]{:S(2)}) %collective-permute-start.6) | collective-permute-done | bytes 65568 | tf_op jit(solution)/shard_map/ppermute | solution.py:252
  30.4 0.0 collective-permute-done.9.refs_3_
  30.4 0.3 fresh.1
  30.7 1.6 %collective-permute-start.10 = (f32[128,256]{1,0:T(8,128)S(1)}, f32[128,256]{1,0:T(8,128)S(1)}, u32[]{:S(2)}, u32[]{:S(2)}) collective-permute-start(f32[128,256]{1,0:T(8,128)S(1)} %get-tuple-element.47.refs_0_), channel_id=1, source_target_pairs={{0,2},{2,0},{1,3},{3,1},{4,6},{6,4},{5,7},{7,5},{8,10},{10,8},{9,1... | collective-permute-start | bytes 393224 | tf_op jit(solution)/shard_map/ppermute | solution.py:252
  32.3 0.0 collective-permute-start.11
  32.3 3.4 %collective-permute-done.10.refs_1_ = f32[128,256]{1,0:T(8,128)S(1)} collective-permute-done((f32[128,256]{1,0:T(8,128)S(1)}, f32[128,256]{1,0:T(8,128)S(1)}, u32[]{:S(2)}, u32[]{:S(2)}) %collective-permute-start.10) | collective-permute-done | bytes 131104 | tf_op jit(solution)/shard_map/ppermute | solution.py:252
  35.7 0.0 collective-permute-start.12
  35.7 0.5 partial.3.refs_4_
  36.2 0.0 collective-permute-done.11.refs_2_
  36.2 0.9 %collective-permute-done.12.refs_3_ = f32[128,256]{1,0:T(8,128)S(1)} collective-permute-done((f32[128,256]{1,0:T(8,128)S(1)}, f32[128,256]{1,0:T(8,128)S(1)}, u32[]{:S(2)}, u32[]{:S(2)}) %collective-permute-start.12) | collective-permute-done | bytes 131104 | tf_op jit(solution)/shard_map/ppermute | solution.py:252
  37.1 1.2 %corner.1 = (f32[8,128]{1,0:T(8,128)S(1)}, f32[256,256]{1,0:T(8,128)S(1)}, f32[8,128]{1,0:T(8,128)S(1)}) custom-call(f32[128,256]{1,0:T(8,128)S(1)} %get-tuple-element.47.refs_0_, f32[128,256]{1,0:T(8,128)S(1)} %collective-permute-done.10.refs_1_, f32[128,256]{1,0:T(8,128)S(1)} %collective-permute-done.11.refs_2_, ...), custom_call_target="tpu_custom_call" | custom-call | tf_op jit(solution)/shard_map/corner/pallas_call | solution.py:362
  38.2 0.2 collective-permute-start.13
  38.5 1.0 %collective-permute-done.13 = f32[8,128]{1,0:T(8,128)S(1)} collective-permute-done((f32[8,128]{1,0:T(8,128)S(1)}, f32[8,128]{1,0:T(8,128)S(1)}, u32[]{:S(2)}, u32[]{:S(2)}) %collective-permute-start.13) | collective-permute-done | bytes 4128 | tf_op jit(solution)/shard_map/ppermute | solution.py:252
  39.5 1.3 %collective-permute-start.14 = (f32[8,128]{1,0:T(8,128)S(1)}, f32[8,128]{1,0:T(8,128)S(1)}, u32[]{:S(2)}, u32[]{:S(2)}) collective-permute-start(f32[8,128]{1,0:T(8,128)S(1)} %add.34), channel_id=1, source_target_pairs={{0,3},{1,2},{2,1},{3,0},{4,7},{5,6},{6,5},{7,4},{8,11},{9,10},{10,... | collective-permute-start | bytes 12296 | tf_op jit(solution)/shard_map/ppermute | solution.py:257
  40.8 1.7 %collective-permute-done.14 = f32[8,128]{1,0:T(8,128)S(1)} collective-permute-done((f32[8,128]{1,0:T(8,128)S(1)}, f32[8,128]{1,0:T(8,128)S(1)}, u32[]{:S(2)}, u32[]{:S(2)}) %collective-permute-start.14) | collective-permute-done | bytes 4128 | tf_op jit(solution)/shard_map/ppermute | solution.py:257
  42.5 2.1 %collective-permute-start.17 = (f32[8,128]{1,0:T(8,128)S(1)}, f32[8,128]{1,0:T(8,128)S(1)}, u32[]{:S(2)}, u32[]{:S(2)}) collective-permute-start(f32[8,128]{1,0:T(8,128)S(1)} %add.35.refs_0_), channel_id=1, source_target_pairs={{0,13},{1,12},{4,9},{5,8},{8,5},{9,4},{12,1},{13,0},{2,15},{3,14},... | collective-permute-start | bytes 12296 | tf_op jit(solution)/shard_map/ppermute | solution.py:257
  44.7 0.6 %collective-permute-start.16 = (f32[8,128]{1,0:T(8,128)S(1)}, f32[8,128]{1,0:T(8,128)S(1)}, u32[]{:S(2)}, u32[]{:S(2)}) collective-permute-start(f32[8,128]{1,0:T(8,128)S(1)} %add.35.refs_0_), channel_id=1, source_target_pairs={{0,9},{1,8},{4,13},{5,12},{8,1},{9,0},{12,5},{13,4},{2,11},{3,10},... | collective-permute-start | bytes 12296 | tf_op jit(solution)/shard_map/ppermute | solution.py:257
  45.2 1.2 %collective-permute-start.15 = (f32[8,128]{1,0:T(8,128)S(1)}, f32[8,128]{1,0:T(8,128)S(1)}, u32[]{:S(2)}, u32[]{:S(2)}) collective-permute-start(f32[8,128]{1,0:T(8,128)S(1)} %add.35.refs_0_), channel_id=1, source_target_pairs={{0,5},{1,4},{4,1},{5,0},{8,13},{9,12},{12,9},{13,8},{2,7},{3,6},{6... | collective-permute-start | bytes 12296 | tf_op jit(solution)/shard_map/ppermute | solution.py:257
  46.4 0.9 %collective-permute-done.17.refs_3_ = f32[8,128]{1,0:T(8,128)S(1)} collective-permute-done((f32[8,128]{1,0:T(8,128)S(1)}, f32[8,128]{1,0:T(8,128)S(1)}, u32[]{:S(2)}, u32[]{:S(2)}) %collective-permute-start.17) | collective-permute-done | bytes 4128 | tf_op jit(solution)/shard_map/ppermute | solution.py:257
  47.3 1.2 %collective-permute-done.16.refs_2_ = f32[8,128]{1,0:T(8,128)S(1)} collective-permute-done((f32[8,128]{1,0:T(8,128)S(1)}, f32[8,128]{1,0:T(8,128)S(1)}, u32[]{:S(2)}, u32[]{:S(2)}) %collective-permute-start.16) | collective-permute-done | bytes 4128 | tf_op jit(solution)/shard_map/ppermute | solution.py:257
  48.6 0.0 collective-permute-done.15.refs_1_
  48.6 0.8 %result.1 = (f32[1,256,256]{2,1,0:T(8,128)}, f32[1]{0:T(128)}) custom-call(f32[8,128]{1,0:T(8,128)S(1)} %add.35.refs_0_, f32[8,128]{1,0:T(8,128)S(1)} %collective-permute-done.15.refs_1_, f32[8,128]{1,0:T(8,128)S(1)} %collective-permute-done.16.refs_2_, f32[8,128]{1,0:T(8,128)S(1)} %collective-permute-done.17.refs_3_, ...), custom_call_target="tpu_custom_call" | custom-call | tf_op jit(solution)/shard_map/result/pallas_call | solution.py:376
  (16 shorter events, 0.1 us)
Async XLA Ops:
  0.6 4.0 %copy-start = (f32[1,256,256]{2,1,0:T(8,128)S(1)}, f32[1,256,256]{2,1,0:T(8,128)}, u32[]{:S(2)}) copy-start(f32[1,256,256]{2,1,0:T(8,128)} %psi_hbm.1) | copy-start | bytes 786436
  1.6 3.0 %copy-start.2 = (s32[2,2]{1,0:T(2,128)S(1)}, s32[2,2]{1,0:T(2,128)}, u32[]{:S(2)}) copy-start(s32[2,2]{1,0:T(2,128)} %sizes_ref.1) | copy-start | bytes 52
  1.6 3.0 %copy-start.3 = (s32[4,1]{0,1:T(1,128)S(1)}, s32[4,1]{0,1:T(1,128)}, u32[]{:S(2)}) copy-start(s32[4,1]{0,1:T(1,128)} %param.9) | copy-start | bytes 52
  1.6 6.5 %collective-permute-start = (f32[128,256]{1,0:T(8,128)S(1)}, f32[128,256]{1,0:T(8,128)S(1)}, u32[]{:S(2)}, u32[]{:S(2)}) collective-permute-start(f32[128,256]{1,0:T(8,128)S(1)} %dynamic-slice_bitcast_fusion), channel_id=1, source_target_pairs={{0,2},{2,0},{1,3},{3,1},{4,6},{6,4},{5,7},{7,5},{8,10},{10,8},{9,1... | collective-permute-start | bytes 393224 | tf_op jit(solution)/shard_map/ppermute | solution.py:252
  4.7 1.0 %copy-start.1 = (f32[1,256,256]{2,1,0:T(8,128)S(1)}, f32[1,256,256]{2,1,0:T(8,128)}, u32[]{:S(2)}) copy-start(f32[1,256,256]{2,1,0:T(8,128)} %diag_hbm.1) | copy-start | bytes 786436
  8.2 1.4 %collective-permute-start.1 = (f32[128,256]{1,0:T(8,128)S(1)}, f32[128,256]{1,0:T(8,128)S(1)}, u32[]{:S(2)}, u32[]{:S(2)}) collective-permute-start(f32[128,256]{1,0:T(8,128)S(1)} %bitcast_multiply_fusion.refs_1_.refs_0_), channel_id=1, source_target_pairs={{0,1},{1,0},{2,3},{3,2},{4,5},{5,4},{6,7},{7,6},{8,9},{9,8},{10,11... | collective-permute-start | bytes 393224 | tf_op jit(solution)/shard_map/ppermute | solution.py:252
  11.3 1.4 %collective-permute-start.3 = (f32[264,128]{1,0:T(8,128)S(1)}, f32[264,128]{1,0:T(8,128)S(1)}, u32[]{:S(2)}, u32[]{:S(2)}) collective-permute-start(f32[264,128]{1,0:T(8,128)S(1)} %get-tuple-element.44), channel_id=1, source_target_pairs={{0,1},{1,0},{2,3},{3,2},{4,5},{5,4},{6,7},{7,6},{8,9},{9,8},{10,11... | collective-permute-start | bytes 405512 | tf_op jit(solution)/shard_map/ppermute | solution.py:252
  11.5 3.3 %collective-permute-start.2 = (f32[264,128]{1,0:T(8,128)S(1)}, f32[264,128]{1,0:T(8,128)S(1)}, u32[]{:S(2)}, u32[]{:S(2)}) collective-permute-start(f32[264,128]{1,0:T(8,128)S(1)} %get-tuple-element.42), channel_id=1, source_target_pairs={{0,1},{1,0},{2,3},{3,2},{4,5},{5,4},{6,7},{7,6},{8,9},{9,8},{10,11... | collective-permute-start | bytes 405512 | tf_op jit(solution)/shard_map/ppermute | solution.py:252
  12.7 4.5 %collective-permute-start.7 = (f32[136,128]{1,0:T(8,128)S(1)}, f32[136,128]{1,0:T(8,128)S(1)}, u32[]{:S(2)}, u32[]{:S(2)}) collective-permute-start(f32[136,128]{1,0:T(8,128)S(1)} %slice.23), channel_id=1, source_target_pairs={{0,2},{2,0},{1,3},{3,1},{4,6},{6,4},{5,7},{7,5},{8,10},{10,8},{9,1... | collective-permute-start | bytes 208904 | tf_op jit(solution)/shard_map/ppermute | solution.py:252
  14.6 5.9 %collective-permute-start.4 = (f32[128,128]{1,0:T(8,128)S(1)}, f32[128,128]{1,0:T(8,128)S(1)}, u32[]{:S(2)}, u32[]{:S(2)}) collective-permute-start(f32[128,128]{1,0:T(8,128)S(1)} %slice.21), channel_id=1, source_target_pairs={{0,2},{2,0},{1,3},{3,1},{4,6},{6,4},{5,7},{7,5},{8,10},{10,8},{9,1... | collective-permute-start | bytes 196616 | tf_op jit(solution)/shard_map/ppermute | solution.py:252
  17.3 5.6 %collective-permute-start.8 = (f32[136,128]{1,0:T(8,128)S(1)}, f32[136,128]{1,0:T(8,128)S(1)}, u32[]{:S(2)}, u32[]{:S(2)}) collective-permute-start(f32[136,128]{1,0:T(8,128)S(1)} %slice_add_fusion), channel_id=1, source_target_pairs={{0,8},{4,12},{8,0},{12,4},{1,9},{5,13},{9,1},{13,5},{2,10},{6,14},... | collective-permute-start | bytes 208904 | tf_op jit(solution)/shard_map/ppermute | solution.py:252
  20.5 4.3 %collective-permute-start.5 = (f32[128,128]{1,0:T(8,128)S(1)}, f32[128,128]{1,0:T(8,128)S(1)}, u32[]{:S(2)}, u32[]{:S(2)}) collective-permute-start(f32[128,128]{1,0:T(8,128)S(1)} %slice_add_fusion.1), channel_id=1, source_target_pairs={{0,4},{4,0},{8,12},{12,8},{1,5},{5,1},{9,13},{13,9},{2,6},{6,2},{1... | collective-permute-start | bytes 196616 | tf_op jit(solution)/shard_map/ppermute | solution.py:252
  22.9 7.5 %collective-permute-start.9 = (f32[136,128]{1,0:T(8,128)S(1)}, f32[136,128]{1,0:T(8,128)S(1)}, u32[]{:S(2)}, u32[]{:S(2)}) collective-permute-start(f32[136,128]{1,0:T(8,128)S(1)} %add.33.refs_2_), channel_id=1, source_target_pairs={{0,4},{4,0},{8,12},{12,8},{1,5},{5,1},{9,13},{13,9},{2,6},{6,2},{1... | collective-permute-start | bytes 208904 | tf_op jit(solution)/shard_map/ppermute | solution.py:252
  24.8 5.6 %collective-permute-start.6 = (f32[128,128]{1,0:T(8,128)S(1)}, f32[128,128]{1,0:T(8,128)S(1)}, u32[]{:S(2)}, u32[]{:S(2)}) collective-permute-start(f32[128,128]{1,0:T(8,128)S(1)} %add.31.refs_0_), channel_id=1, source_target_pairs={{0,8},{4,12},{8,0},{12,4},{1,9},{5,13},{9,1},{13,5},{2,10},{6,14},... | collective-permute-start | bytes 196616 | tf_op jit(solution)/shard_map/ppermute | solution.py:252
  30.7 5.0 %collective-permute-start.10 = (f32[128,256]{1,0:T(8,128)S(1)}, f32[128,256]{1,0:T(8,128)S(1)}, u32[]{:S(2)}, u32[]{:S(2)}) collective-permute-start(f32[128,256]{1,0:T(8,128)S(1)} %get-tuple-element.47.refs_0_), channel_id=1, source_target_pairs={{0,2},{2,0},{1,3},{3,1},{4,6},{6,4},{5,7},{7,5},{8,10},{10,8},{9,1... | collective-permute-start | bytes 393224 | tf_op jit(solution)/shard_map/ppermute | solution.py:252
  32.3 3.9 %collective-permute-start.11 = (f32[128,256]{1,0:T(8,128)S(1)}, f32[128,256]{1,0:T(8,128)S(1)}, u32[]{:S(2)}, u32[]{:S(2)}) collective-permute-start(f32[128,256]{1,0:T(8,128)S(1)} %get-tuple-element.47.refs_0_), channel_id=1, source_target_pairs={{0,1},{1,0},{2,3},{3,2},{4,5},{5,4},{6,7},{7,6},{8,9},{9,8},{10,11... | collective-permute-start | bytes 393224 | tf_op jit(solution)/shard_map/ppermute | solution.py:252
  35.7 1.3 %collective-permute-start.12 = (f32[128,256]{1,0:T(8,128)S(1)}, f32[128,256]{1,0:T(8,128)S(1)}, u32[]{:S(2)}, u32[]{:S(2)}) collective-permute-start(f32[128,256]{1,0:T(8,128)S(1)} %collective-permute-done.10.refs_1_), channel_id=1, source_target_pairs={{0,1},{1,0},{2,3},{3,2},{4,5},{5,4},{6,7},{7,6},{8,9},{9,8},{10,11... | collective-permute-start | bytes 393224 | tf_op jit(solution)/shard_map/ppermute | solution.py:252
  38.2 1.2 %collective-permute-start.13 = (f32[8,128]{1,0:T(8,128)S(1)}, f32[8,128]{1,0:T(8,128)S(1)}, u32[]{:S(2)}, u32[]{:S(2)}) collective-permute-start(f32[8,128]{1,0:T(8,128)S(1)} %get-tuple-element.49), channel_id=1, source_target_pairs={{0,1},{1,0},{2,3},{3,2},{4,5},{5,4},{6,7},{7,6},{8,9},{9,8},{10,11... | collective-permute-start | bytes 12296 | tf_op jit(solution)/shard_map/ppermute | solution.py:252
  39.5 3.0 %collective-permute-start.14 = (f32[8,128]{1,0:T(8,128)S(1)}, f32[8,128]{1,0:T(8,128)S(1)}, u32[]{:S(2)}, u32[]{:S(2)}) collective-permute-start(f32[8,128]{1,0:T(8,128)S(1)} %add.34), channel_id=1, source_target_pairs={{0,3},{1,2},{2,1},{3,0},{4,7},{5,6},{6,5},{7,4},{8,11},{9,10},{10,... | collective-permute-start | bytes 12296 | tf_op jit(solution)/shard_map/ppermute | solution.py:257
  42.5 4.8 %collective-permute-start.17 = (f32[8,128]{1,0:T(8,128)S(1)}, f32[8,128]{1,0:T(8,128)S(1)}, u32[]{:S(2)}, u32[]{:S(2)}) collective-permute-start(f32[8,128]{1,0:T(8,128)S(1)} %add.35.refs_0_), channel_id=1, source_target_pairs={{0,13},{1,12},{4,9},{5,8},{8,5},{9,4},{12,1},{13,0},{2,15},{3,14},... | collective-permute-start | bytes 12296 | tf_op jit(solution)/shard_map/ppermute | solution.py:257
  44.7 3.9 %collective-permute-start.16 = (f32[8,128]{1,0:T(8,128)S(1)}, f32[8,128]{1,0:T(8,128)S(1)}, u32[]{:S(2)}, u32[]{:S(2)}) collective-permute-start(f32[8,128]{1,0:T(8,128)S(1)} %add.35.refs_0_), channel_id=1, source_target_pairs={{0,9},{1,8},{4,13},{5,12},{8,1},{9,0},{12,5},{13,4},{2,11},{3,10},... | collective-permute-start | bytes 12296 | tf_op jit(solution)/shard_map/ppermute | solution.py:257
  45.2 3.4 %collective-permute-start.15 = (f32[8,128]{1,0:T(8,128)S(1)}, f32[8,128]{1,0:T(8,128)S(1)}, u32[]{:S(2)}, u32[]{:S(2)}) collective-permute-start(f32[8,128]{1,0:T(8,128)S(1)} %add.35.refs_0_), channel_id=1, source_target_pairs={{0,5},{1,4},{4,1},{5,0},{8,13},{9,12},{12,9},{13,8},{2,7},{3,6},{6... | collective-permute-start | bytes 12296 | tf_op jit(solution)/shard_map/ppermute | solution.py:257

commit v8 on v7

--- a/solution.py
+++ b/solution.py
@@ -129,30 +129,33 @@
         out_ref[blk // LANES * half :, :] = jnp.broadcast_to(scalar, (PAD, LANES))
 
 
-def keep_kernel(coupling, slot_ref, norm_ref, joint_ref, th, tl, ih, il, *keep_refs):
+def keep_kernel(coupling, ncell, nsec, *refs):
+    halves = refs[: 2 * (nsec - 1)]
+    own_ref, stat_ref, slot_ref, scalar_ref, joint_ref, th, tl, ih, il, full_ref, norm_ref, *keep_refs = refs[2 * (nsec - 1) :]
+    half = own_ref.shape[0] // 2
     terms = range(th.shape[0])
+    norm = stat_ref[:1, :1]
+    full_ref[0] = own_ref[...]
+    for slot in range(1, nsec):
+        for index, part in enumerate(halves[2 * slot - 2 : 2 * slot]):
+            value = part[...]
+            full_ref[slot, index * half : (index + 1) * half, :] = value
+            norm = norm + total(value * value)
+    norm_ref[...] = jnp.broadcast_to(norm / ncell, norm_ref.shape)
     inner = [(ih[i], il[i]) for i in terms]
-    sum_rows(coupling, 0, slot_ref, th, tl, inner, [joint_ref.at[i] for i in terms], norm_ref[1:2, :1], keep_refs)
-
-
-def image_kernel(coupling, ncell, nsec, *refs):
+    sum_rows(coupling, 0, slot_ref, th, tl, inner, [joint_ref.at[i] for i in terms], scalar_ref[:1, :1], keep_refs)
+
+
+def image_kernel(coupling, nsec, *refs):
     halves = refs[: 2 * (nsec - 1)]
     own_ref, part_ref, slot_ref, stat_ref = refs[2 * (nsec - 1) : 2 * (nsec - 1) + 4]
-    lh, ll, th, tl, rh, rl, full_ref, norm_ref, joint_ref, ih, il, *send_refs = refs[2 * (nsec - 1) + 4 :]
+    lh, ll, th, tl, rh, rl, scalar_ref, joint_ref, ih, il, *send_refs = refs[2 * (nsec - 1) + 4 :]
     blk = own_ref.shape[0]
     half = blk // 2
     nterm = lh.shape[0]
     own = own_ref[...]
-    blocks = [own] + [
-        jnp.concatenate([halves[2 * slot - 2][...], halves[2 * slot - 1][...]], axis=0) for slot in range(1, nsec)
-    ]
-    for slot in range(nsec):
-        full_ref[slot] = blocks[slot]
-    norm = stat_ref[:1, :1]
-    for block in blocks[1:]:
-        norm = norm + total(block * block)
+    fars = [own[half:]] + [halves[2 * slot - 1][...] for slot in range(1, nsec)]
     terms = range(nterm)
-    fars = [block[half:] for block in blocks]
     middles = [
         part_ref[i] + half_product((lh[i, :, half:], ll[i, :, half:]), split(pick(slot_ref, i, fars))) for i in terms
     ]
@@ -164,8 +167,7 @@
     for i in terms:
         joint_ref[i] = joints[i]
     scalar = stat_ref[1:2, :1] + total(squares)
-    row = lax.broadcasted_iota(jnp.int32, norm_ref.shape, 0)
-    norm_ref[...] = jnp.where(row == 0, norm / ncell, scalar)
+    scalar_ref[...] = jnp.broadcast_to(scalar, scalar_ref.shape)
     inner = [split(product(split(joints[i]), (rh[i], rl[i]), NN)) for i in terms]
     for i in terms:
         ih[i], il[i] = inner[i]
@@ -195,7 +197,7 @@
 def corner_kernel(coupling, weight, ncell, share, nsec, *refs):
     nears, fars = refs[:nsec], refs[nsec : 2 * nsec]
     part_ref, joint_ref, full_ref, diag_ref, norm_ref, cross_ref, slot_ref, lh, ll, rh, rl = refs[2 * nsec : 2 * nsec + 11]
-    sums_ref, fresh_ref, info_ref = refs[2 * nsec + 11 :]
+    sums_ref, overlap_ref = refs[2 * nsec + 11 :]
     half = nears[0].shape[0]
     terms = range(lh.shape[0])
     blocks = [far[...] for far in fars]
@@ -208,13 +210,8 @@
     for slot in range(1, nsec):
         overlap = overlap + full_ref[slot] * raw[slot]
     overlap = total(overlap) / (ncell * norm)
-    fresh = [raw[slot] - overlap * full_ref[slot] for slot in range(nsec)]
-    length = fresh[0] * fresh[0]
-    for slot in range(1, nsec):
-        length = length + fresh[slot] * fresh[slot]
-    length = total(length) / ncell
-    fresh_ref[...] = fresh[0]
-    squares = weight * fresh[0] * fresh[0] * diag_ref[...]
+    own = raw[0] - overlap * full_ref[0]
+    squares = weight * own * own * diag_ref[...]
     base = coupling * raw[0]
     for i in terms:
         joint = base + product(split(middles[i]), (rh[i], rl[i]), NT)
@@ -222,7 +219,23 @@
         squares = squares + joint * joint
     row = lax.broadcasted_iota(jnp.int32, sums_ref.shape, 0)
     sums_ref[...] = jnp.where(row == 0, total(squares), cross_ref[:1, :1] * share)
-    info_ref[...] = jnp.where(row == 0, norm, jnp.where(row == 1, length, cross_ref[1:2, :1]))
+    overlap_ref[...] = jnp.broadcast_to(overlap, overlap_ref.shape)
+
+
+def length_kernel(ncell, nsec, *refs):
+    overlap_ref, full_ref, norm_ref, cross_ref, fresh_ref, info_ref = refs[-6:]
+    half = fresh_ref.shape[0] // 2
+    nears, fars = ([ref[...] for ref in part] for part in (refs[:nsec], refs[nsec : 2 * nsec]))
+    overlap = overlap_ref[:1, :1]
+    length = jnp.zeros((1, 1), F32)
+    for slot in range(nsec):
+        value = jnp.concatenate([nears[slot], fars[slot]], axis=0) - overlap * full_ref[slot]
+        length = length + total(value * value)
+        if slot == 0:
+            fresh_ref[...] = value
+    row = lax.broadcasted_iota(jnp.int32, info_ref.shape, 0)
+    length = length / ncell
+    info_ref[...] = jnp.where(row == 0, norm_ref[:1, :1], jnp.where(row == 1, length, cross_ref[1:2, :1]))
 
 
 def result_kernel(ncell, *refs):
@@ -310,10 +323,9 @@
         )(*nears, slots, lh, ll)
 
     summed = [shape((blk // LANES * half + PAD, LANES), F32)] * nsec
-    full, norm, joints, ih, il, *sends = pl.pallas_call(
-        functools.partial(image_kernel, coupling, ncell, nsec),
+    scalar, joints, ih, il, *sends = pl.pallas_call(
+        functools.partial(image_kernel, coupling, nsec),
         out_shape=[
-            shape((nsec, blk, blk), F32),
             shape((8, 128), F32),
             shape(operator, F32),
             shape(operator, BF16),
@@ -321,19 +333,19 @@
             *summed,
         ],
         in_specs=[vmem] * (len(halves) + 10),
-        out_specs=[vmem] * (5 + nsec),
+        out_specs=[vmem] * (4 + nsec),
         compiler_params=PARAMS,
         name="image",
     )(*halves, own, partial([own, *masked]), slots, stat, lh, ll, th, tl, rh, rl)
 
-    keeps = pl.pallas_call(
-        functools.partial(keep_kernel, coupling),
-        out_shape=summed,
-        in_specs=[vmem] * 7,
-        out_specs=[vmem] * nsec,
+    full, norm, *keeps = pl.pallas_call(
+        functools.partial(keep_kernel, coupling, ncell, nsec),
+        out_shape=[shape((nsec, blk, blk), F32), shape((8, 128), F32), *summed],
+        in_specs=[vmem] * (len(halves) + 9),
+        out_specs=[vmem] * (2 + nsec),
         compiler_params=PARAMS,
         name="keep",
-    )(slots, norm, joints, th, tl, ih, il)
+    )(*halves, own, stat, slots, scalar, joints, th, tl, ih, il)
     chip = [keep + across(send, "rep", 1) for keep, send in zip(keeps, sends)]
     ntile = blk // LANES
     bounds = [tile * half for tile in range(ntile)] + [ntile * half + PAD]
@@ -359,15 +371,23 @@
 
     nears = [across(fresh, "sector", step) if step else fresh for step in range(nsec)]
     fars = [across(near, "rep", 1) for near in nears]
-    sums, direction, info = pl.pallas_call(
+    sums, overlap = pl.pallas_call(
         functools.partial(corner_kernel, coupling, weight, ncell, 1.0 / nz, nsec),
-        out_shape=[shape((8, 128), F32), shape((blk, blk), F32), shape((8, 128), F32)],
+        out_shape=[shape((8, 128), F32)] * 2,
         in_specs=[vmem] * (2 * nsec + 11),
-        out_specs=[vmem] * 3,
+        out_specs=[vmem] * 2,
         compiler_params=PARAMS,
         name="corner",
     )(*nears, *fars, partial(nears), joints, full, diag, norm, cross, slots, lh, ll, rh, rl)
 
+    direction, info = pl.pallas_call(
+        functools.partial(length_kernel, ncell, nsec),
+        out_shape=[shape((blk, blk), F32), shape((8, 128), F32)],
+        in_specs=[vmem] * (2 * nsec + 4),
+        out_specs=[vmem] * 2,
+        compiler_params=PARAMS,
+        name="length",
+    )(*nears, *fars, overlap, full, norm, cross)
     sums = sums + across(sums, "rep", 1)
     for axis in ("sector", "terms"):
         parts = [diagonally(sums, axis, step) for step in range(1, lax.axis_size(axis))]

time: 49.6 us -> 49.6 us (level)
    pallas_call x2 -> x3, Pallas kernels: 2.09 us -> 2.38 us  [the longest x1 1.67 us: body(): pl.pallas_call(functools.partial(image_kernel, coupling, nsec), out_shape...]
where the time goes in v8:
time: 49.6 us; the launch traced here: 49.4 us
  starting transfers between devices  22.8 us (46%)
  waiting for transfers between devices  15.8 us (32%)
  Pallas kernels  8 us (16%)
  local copies, waits for them, and re-layouts  1.95 us (4%)
  between operations  0.79 us (2%)
    ppermute x14, starting transfers between devices, across(): return lax.ppermute(x, axis, [(i, i ^ step) for i in range(size)])  17.6 us
    ppermute x14, waiting for transfers between devices, across(): return lax.ppermute(x, axis, [(i, i ^ step) for i in range(size)])  12.2 us
    ppermute x4, starting transfers between devices, diagonally(): lax.ppermute(x, (axis, 'rep'), [(2 * i + c, 2 * (i ^ step) + 1 - c) for i...  5.22 us
    ppermute x4, waiting for transfers between devices, diagonally(): lax.ppermute(x, (axis, 'rep'), [(2 * i + c, 2 * (i ^ step) + 1 - c) for i...  3.6 us
    pallas_call x1, Pallas kernels, body(): pl.pallas_call(functools.partial(prepare_kernel, weight), out_shape=[shap...  2.4 us
    pallas_call x1, Pallas kernels, body(): pl.pallas_call(functools.partial(image_kernel, coupling, nsec), out_shape...  1.67 us
    pallas_call x1, Pallas kernels, body(): pl.pallas_call(functools.partial(corner_kernel, coupling, weight, ncell,...  1.19 us
  transfers between devices with their start and end apart: 18, of which 13 were waited for; matrix products, arithmetic and copies ran while one was open for 0% of the time, Pallas kernels for 8%

profile of v8, /device:TPU:0, one launch (start us, length us, event | category | flops | bytes accessed | tf_op | source)
XLA Modules:
  0.0 49.4 jit_solution(11985546977790433468)
XLA Ops:
  0.6 1.0 %dynamic-slice_bitcast_fusion = f32[128,256]{1,0:T(8,128)S(1)} fusion(f32[1,256,256]{2,1,0:T(8,128)} %psi_hbm.1, s32[]{:T(128)S(6)} %select_n.3), kind=kLoop, calls=%fused_computation.1 | loop fusion | bytes 262148 | tf_op jit(solution)/shard_map/dynamic_slice | solution.py:286
  1.6 0.0 copy-start.2
  1.6 0.0 copy-start.3
  1.6 3.0 %collective-permute-start = (f32[128,256]{1,0:T(8,128)S(1)}, f32[128,256]{1,0:T(8,128)S(1)}, u32[]{:S(2)}, u32[]{:S(2)}) collective-permute-start(f32[128,256]{1,0:T(8,128)S(1)} %dynamic-slice_bitcast_fusion), channel_id=1, source_target_pairs={{0,2},{2,0},{1,3},{3,1},{4,6},{6,4},{5,7},{7,5},{8,10},{10,8},{9,1... | collective-permute-start | bytes 393224 | tf_op jit(solution)/shard_map/ppermute | solution.py:265
  4.7 0.9 %copy-done.1 = f32[1,256,256]{2,1,0:T(8,128)S(1)} copy-done((f32[1,256,256]{2,1,0:T(8,128)S(1)}, f32[1,256,256]{2,1,0:T(8,128)}, u32[]{:S(2)}) %copy-start.1) | copy-done | bytes 262168
  5.6 2.4 %prepare.1 = (bf16[4,256,256]{2,1,0:T(8,128)(2,1)S(1)}, bf16[4,256,256]{2,1,0:T(8,128)(2,1)S(1)}, bf16[4,256,256]{2,1,0:T(8,128)(2,1)S(1)}, bf16[4,256,256]{2,1,...) custom-call(s32[2,2]{1,0:T(2,128)S(1)} %copy-done.2, ...), custom_call_target="tpu_custom_call" | custom-call | tf_op jit(solution)/shard_map/prepare/pallas_call | solution.py:293
  8.0 0.1 collective-permute-done
  8.2 0.1 collective-permute-start.1
  8.2 0.5 partial.2.refs_3_
  8.7 0.9 %collective-permute-done.1.refs_1_ = f32[128,256]{1,0:T(8,128)S(1)} collective-permute-done((f32[128,256]{1,0:T(8,128)S(1)}, f32[128,256]{1,0:T(8,128)S(1)}, u32[]{:S(2)}, u32[]{:S(2)}) %collective-permute-start.1) | collective-permute-done | bytes 131104 | tf_op jit(solution)/shard_map/ppermute | solution.py:265
  9.6 1.7 %image.1 = (f32[8,128]{1,0:T(8,128)S(1)}, f32[4,256,256]{2,1,0:T(8,128)S(1)}, bf16[4,256,256]{2,1,0:T(8,128)(2,1)S(1)}, bf16[4,256,256]{2,1,0:T(8,128)(2,1)S(1)}...) custom-call(f32[128,256]{1,0:T(8,128)S(1)} %bitcast_multiply_fusion.refs_1_.refs_0_, ...), custom_call_target="tpu_custom_call" | custom-call | tf_op jit(solution)/shard_map/image/pallas_call | solution.py:326
  11.3 0.2 collective-permute-start.3
  11.5 0.4 collective-permute-start.2
  11.8 0.4 keep.1
  12.3 0.4 collective-permute-done.3
  12.7 1.8 %collective-permute-start.7 = (f32[136,128]{1,0:T(8,128)S(1)}, f32[136,128]{1,0:T(8,128)S(1)}, u32[]{:S(2)}, u32[]{:S(2)}) collective-permute-start(f32[136,128]{1,0:T(8,128)S(1)} %slice.23), channel_id=1, source_target_pairs={{0,2},{2,0},{1,3},{3,1},{4,6},{6,4},{5,7},{7,5},{8,10},{10,8},{9,1... | collective-permute-start | bytes 208904 | tf_op jit(solution)/shard_map/ppermute | solution.py:265
  14.5 0.3 collective-permute-start.4
  14.8 0.0 collective-permute-done.2
  14.8 2.4 %collective-permute-done.7 = f32[136,128]{1,0:T(8,128)S(1)} collective-permute-done((f32[136,128]{1,0:T(8,128)S(1)}, f32[136,128]{1,0:T(8,128)S(1)}, u32[]{:S(2)}, u32[]{:S(2)}) %collective-permute-start.7) | collective-permute-done | bytes 69664 | tf_op jit(solution)/shard_map/ppermute | solution.py:265
  17.3 3.2 %collective-permute-start.8 = (f32[136,128]{1,0:T(8,128)S(1)}, f32[136,128]{1,0:T(8,128)S(1)}, u32[]{:S(2)}, u32[]{:S(2)}) collective-permute-start(f32[136,128]{1,0:T(8,128)S(1)} %slice_add_fusion), channel_id=1, source_target_pairs={{0,8},{4,12},{8,0},{12,4},{1,9},{5,13},{9,1},{13,5},{2,10},{6,14},... | collective-permute-start | bytes 208904 | tf_op jit(solution)/shard_map/ppermute | solution.py:265
  20.4 0.0 collective-permute-done.4
  20.5 1.6 %collective-permute-start.5 = (f32[128,128]{1,0:T(8,128)S(1)}, f32[128,128]{1,0:T(8,128)S(1)}, u32[]{:S(2)}, u32[]{:S(2)}) collective-permute-start(f32[128,128]{1,0:T(8,128)S(1)} %slice_add_fusion.1), channel_id=1, source_target_pairs={{0,4},{4,0},{8,12},{12,8},{1,5},{5,1},{9,13},{13,9},{2,6},{6,2},{1... | collective-permute-start | bytes 196616 | tf_op jit(solution)/shard_map/ppermute | solution.py:265
  22.1 0.7 %collective-permute-done.8 = f32[136,128]{1,0:T(8,128)S(1)} collective-permute-done((f32[136,128]{1,0:T(8,128)S(1)}, f32[136,128]{1,0:T(8,128)S(1)}, u32[]{:S(2)}, u32[]{:S(2)}) %collective-permute-start.8) | collective-permute-done | bytes 69664 | tf_op jit(solution)/shard_map/ppermute | solution.py:265
  22.9 1.9 %collective-permute-start.9 = (f32[136,128]{1,0:T(8,128)S(1)}, f32[136,128]{1,0:T(8,128)S(1)}, u32[]{:S(2)}, u32[]{:S(2)}) collective-permute-start(f32[136,128]{1,0:T(8,128)S(1)} %add.33.refs_2_), channel_id=1, source_target_pairs={{0,4},{4,0},{8,12},{12,8},{1,5},{5,1},{9,13},{13,9},{2,6},{6,2},{1... | collective-permute-start | bytes 208904 | tf_op jit(solution)/shard_map/ppermute | solution.py:265
  24.7 0.1 collective-permute-done.5
  24.8 3.3 %collective-permute-start.6 = (f32[128,128]{1,0:T(8,128)S(1)}, f32[128,128]{1,0:T(8,128)S(1)}, u32[]{:S(2)}, u32[]{:S(2)}) collective-permute-start(f32[128,128]{1,0:T(8,128)S(1)} %add.31.refs_0_), channel_id=1, source_target_pairs={{0,8},{4,12},{8,0},{12,4},{1,9},{5,13},{9,1},{13,5},{2,10},{6,14},... | collective-permute-start | bytes 196616 | tf_op jit(solution)/shard_map/ppermute | solution.py:265
  28.1 2.3 %collective-permute-done.6.refs_1_ = f32[128,128]{1,0:T(8,128)S(1)} collective-permute-done((f32[128,128]{1,0:T(8,128)S(1)}, f32[128,128]{1,0:T(8,128)S(1)}, u32[]{:S(2)}, u32[]{:S(2)}) %collective-permute-start.6) | collective-permute-done | bytes 65568 | tf_op jit(solution)/shard_map/ppermute | solution.py:265
  30.4 0.0 collective-permute-done.9.refs_3_
  30.4 0.3 fresh.1
  30.7 1.6 %collective-permute-start.10 = (f32[128,256]{1,0:T(8,128)S(1)}, f32[128,256]{1,0:T(8,128)S(1)}, u32[]{:S(2)}, u32[]{:S(2)}) collective-permute-start(f32[128,256]{1,0:T(8,128)S(1)} %get-tuple-element.50.refs_0_), channel_id=1, source_target_pairs={{0,2},{2,0},{1,3},{3,1},{4,6},{6,4},{5,7},{7,5},{8,10},{10,8},{9,1... | collective-permute-start | bytes 393224 | tf_op jit(solution)/shard_map/ppermute | solution.py:265
  32.3 3.4 %collective-permute-done.10.refs_1_ = f32[128,256]{1,0:T(8,128)S(1)} collective-permute-done((f32[128,256]{1,0:T(8,128)S(1)}, f32[128,256]{1,0:T(8,128)S(1)}, u32[]{:S(2)}, u32[]{:S(2)}) %collective-permute-start.10) | collective-permute-done | bytes 131104 | tf_op jit(solution)/shard_map/ppermute | solution.py:265
  35.7 0.0 collective-permute-start.12
  35.7 0.5 partial.3.refs_4_
  36.2 0.0 collective-permute-done.11.refs_2_
  36.2 0.9 %collective-permute-done.12.refs_3_ = f32[128,256]{1,0:T(8,128)S(1)} collective-permute-done((f32[128,256]{1,0:T(8,128)S(1)}, f32[128,256]{1,0:T(8,128)S(1)}, u32[]{:S(2)}, u32[]{:S(2)}) %collective-permute-start.12) | collective-permute-done | bytes 131104 | tf_op jit(solution)/shard_map/ppermute | solution.py:265
  37.0 1.2 %corner.1 = (f32[8,128]{1,0:T(8,128)S(1)}, f32[8,128]{1,0:T(8,128)S(1)}) custom-call(f32[128,256]{1,0:T(8,128)S(1)} %get-tuple-element.50.refs_0_, f32[128,256]{1,0:T(8,128)S(1)} %collective-permute-done.10.refs_1_, f32[128,256]{1,0:T(8,128)S(1)} %collective-permute-done.11.refs_2_, f32[128,256]{1,0:T(8,128)S(1)} %collective-permute-done.12.refs_3_, ...), custom_call_target="tpu_custom_call" | custom-call | tf_op jit(solution)/shard_map/corner/pallas_call | solution.py:374
  38.2 0.2 collective-permute-start.13
  38.4 1.0 %collective-permute-done.13 = f32[8,128]{1,0:T(8,128)S(1)} collective-permute-done((f32[8,128]{1,0:T(8,128)S(1)}, f32[8,128]{1,0:T(8,128)S(1)}, u32[]{:S(2)}, u32[]{:S(2)}) %collective-permute-start.13) | collective-permute-done | bytes 4128 | tf_op jit(solution)/shard_map/ppermute | solution.py:265
  39.5 1.3 %collective-permute-start.14 = (f32[8,128]{1,0:T(8,128)S(1)}, f32[8,128]{1,0:T(8,128)S(1)}, u32[]{:S(2)}, u32[]{:S(2)}) collective-permute-start(f32[8,128]{1,0:T(8,128)S(1)} %add.34), channel_id=1, source_target_pairs={{0,3},{1,2},{2,1},{3,0},{4,7},{5,6},{6,5},{7,4},{8,11},{9,10},{10,... | collective-permute-start | bytes 12296 | tf_op jit(solution)/shard_map/ppermute | solution.py:270
  40.8 1.7 %collective-permute-done.14 = f32[8,128]{1,0:T(8,128)S(1)} collective-permute-done((f32[8,128]{1,0:T(8,128)S(1)}, f32[8,128]{1,0:T(8,128)S(1)}, u32[]{:S(2)}, u32[]{:S(2)}) %collective-permute-start.14) | collective-permute-done | bytes 4128 | tf_op jit(solution)/shard_map/ppermute | solution.py:270
  42.5 2.1 %collective-permute-start.17 = (f32[8,128]{1,0:T(8,128)S(1)}, f32[8,128]{1,0:T(8,128)S(1)}, u32[]{:S(2)}, u32[]{:S(2)}) collective-permute-start(f32[8,128]{1,0:T(8,128)S(1)} %add.35.refs_0_), channel_id=1, source_target_pairs={{0,13},{1,12},{4,9},{5,8},{8,5},{9,4},{12,1},{13,0},{2,15},{3,14},... | collective-permute-start | bytes 12296 | tf_op jit(solution)/shard_map/ppermute | solution.py:270
  44.7 0.5 %collective-permute-start.16 = (f32[8,128]{1,0:T(8,128)S(1)}, f32[8,128]{1,0:T(8,128)S(1)}, u32[]{:S(2)}, u32[]{:S(2)}) collective-permute-start(f32[8,128]{1,0:T(8,128)S(1)} %add.35.refs_0_), channel_id=1, source_target_pairs={{0,9},{1,8},{4,13},{5,12},{8,1},{9,0},{12,5},{13,4},{2,11},{3,10},... | collective-permute-start | bytes 12296 | tf_op jit(solution)/shard_map/ppermute | solution.py:270
  45.2 1.2 %collective-permute-start.15 = (f32[8,128]{1,0:T(8,128)S(1)}, f32[8,128]{1,0:T(8,128)S(1)}, u32[]{:S(2)}, u32[]{:S(2)}) collective-permute-start(f32[8,128]{1,0:T(8,128)S(1)} %add.35.refs_0_), channel_id=1, source_target_pairs={{0,5},{1,4},{4,1},{5,0},{8,13},{9,12},{12,9},{13,8},{2,7},{3,6},{6... | collective-permute-start | bytes 12296 | tf_op jit(solution)/shard_map/ppermute | solution.py:270
  46.4 0.3 length.1
  46.7 0.7 %collective-permute-done.17.refs_3_ = f32[8,128]{1,0:T(8,128)S(1)} collective-permute-done((f32[8,128]{1,0:T(8,128)S(1)}, f32[8,128]{1,0:T(8,128)S(1)}, u32[]{:S(2)}, u32[]{:S(2)}) %collective-permute-start.17) | collective-permute-done | bytes 4128 | tf_op jit(solution)/shard_map/ppermute | solution.py:270
  47.3 1.2 %collective-permute-done.16.refs_2_ = f32[8,128]{1,0:T(8,128)S(1)} collective-permute-done((f32[8,128]{1,0:T(8,128)S(1)}, f32[8,128]{1,0:T(8,128)S(1)}, u32[]{:S(2)}, u32[]{:S(2)}) %collective-permute-start.16) | collective-permute-done | bytes 4128 | tf_op jit(solution)/shard_map/ppermute | solution.py:270
  48.6 0.0 collective-permute-done.15.refs_1_
  48.6 0.8 %result.1 = (f32[1,256,256]{2,1,0:T(8,128)}, f32[1]{0:T(128)}) custom-call(f32[8,128]{1,0:T(8,128)S(1)} %add.35.refs_0_, f32[8,128]{1,0:T(8,128)S(1)} %collective-permute-done.15.refs_1_, f32[8,128]{1,0:T(8,128)S(1)} %collective-permute-done.16.refs_2_, f32[8,128]{1,0:T(8,128)S(1)} %collective-permute-done.17.refs_3_, ...), custom_call_target="tpu_custom_call" | custom-call | tf_op jit(solution)/shard_map/result/pallas_call | solution.py:396
  (17 shorter events, 0.1 us)
Async XLA Ops:
  0.6 4.0 %copy-start = (f32[1,256,256]{2,1,0:T(8,128)S(1)}, f32[1,256,256]{2,1,0:T(8,128)}, u32[]{:S(2)}) copy-start(f32[1,256,256]{2,1,0:T(8,128)} %psi_hbm.1) | copy-start | bytes 786436
  1.6 3.0 %copy-start.2 = (s32[2,2]{1,0:T(2,128)S(1)}, s32[2,2]{1,0:T(2,128)}, u32[]{:S(2)}) copy-start(s32[2,2]{1,0:T(2,128)} %sizes_ref.1) | copy-start | bytes 52
  1.6 3.0 %copy-start.3 = (s32[4,1]{0,1:T(1,128)S(1)}, s32[4,1]{0,1:T(1,128)}, u32[]{:S(2)}) copy-start(s32[4,1]{0,1:T(1,128)} %param.9) | copy-start | bytes 52
  1.6 6.5 %collective-permute-start = (f32[128,256]{1,0:T(8,128)S(1)}, f32[128,256]{1,0:T(8,128)S(1)}, u32[]{:S(2)}, u32[]{:S(2)}) collective-permute-start(f32[128,256]{1,0:T(8,128)S(1)} %dynamic-slice_bitcast_fusion), channel_id=1, source_target_pairs={{0,2},{2,0},{1,3},{3,1},{4,6},{6,4},{5,7},{7,5},{8,10},{10,8},{9,1... | collective-permute-start | bytes 393224 | tf_op jit(solution)/shard_map/ppermute | solution.py:265
  4.7 1.0 %copy-start.1 = (f32[1,256,256]{2,1,0:T(8,128)S(1)}, f32[1,256,256]{2,1,0:T(8,128)}, u32[]{:S(2)}) copy-start(f32[1,256,256]{2,1,0:T(8,128)} %diag_hbm.1) | copy-start | bytes 786436
  8.2 1.4 %collective-permute-start.1 = (f32[128,256]{1,0:T(8,128)S(1)}, f32[128,256]{1,0:T(8,128)S(1)}, u32[]{:S(2)}, u32[]{:S(2)}) collective-permute-start(f32[128,256]{1,0:T(8,128)S(1)} %bitcast_multiply_fusion.refs_1_.refs_0_), channel_id=1, source_target_pairs={{0,1},{1,0},{2,3},{3,2},{4,5},{5,4},{6,7},{7,6},{8,9},{9,8},{10,11... | collective-permute-start | bytes 393224 | tf_op jit(solution)/shard_map/ppermute | solution.py:265
  11.3 1.4 %collective-permute-start.3 = (f32[264,128]{1,0:T(8,128)S(1)}, f32[264,128]{1,0:T(8,128)S(1)}, u32[]{:S(2)}, u32[]{:S(2)}) collective-permute-start(f32[264,128]{1,0:T(8,128)S(1)} %get-tuple-element.46), channel_id=1, source_target_pairs={{0,1},{1,0},{2,3},{3,2},{4,5},{5,4},{6,7},{7,6},{8,9},{9,8},{10,11... | collective-permute-start | bytes 405512 | tf_op jit(solution)/shard_map/ppermute | solution.py:265
  11.5 3.3 %collective-permute-start.2 = (f32[264,128]{1,0:T(8,128)S(1)}, f32[264,128]{1,0:T(8,128)S(1)}, u32[]{:S(2)}, u32[]{:S(2)}) collective-permute-start(f32[264,128]{1,0:T(8,128)S(1)} %get-tuple-element.44), channel_id=1, source_target_pairs={{0,1},{1,0},{2,3},{3,2},{4,5},{5,4},{6,7},{7,6},{8,9},{9,8},{10,11... | collective-permute-start | bytes 405512 | tf_op jit(solution)/shard_map/ppermute | solution.py:265
  12.7 4.5 %collective-permute-start.7 = (f32[136,128]{1,0:T(8,128)S(1)}, f32[136,128]{1,0:T(8,128)S(1)}, u32[]{:S(2)}, u32[]{:S(2)}) collective-permute-start(f32[136,128]{1,0:T(8,128)S(1)} %slice.23), channel_id=1, source_target_pairs={{0,2},{2,0},{1,3},{3,1},{4,6},{6,4},{5,7},{7,5},{8,10},{10,8},{9,1... | collective-permute-start | bytes 208904 | tf_op jit(solution)/shard_map/ppermute | solution.py:265
  14.5 5.9 %collective-permute-start.4 = (f32[128,128]{1,0:T(8,128)S(1)}, f32[128,128]{1,0:T(8,128)S(1)}, u32[]{:S(2)}, u32[]{:S(2)}) collective-permute-start(f32[128,128]{1,0:T(8,128)S(1)} %slice.21), channel_id=1, source_target_pairs={{0,2},{2,0},{1,3},{3,1},{4,6},{6,4},{5,7},{7,5},{8,10},{10,8},{9,1... | collective-permute-start | bytes 196616 | tf_op jit(solution)/shard_map/ppermute | solution.py:265
  17.3 5.6 %collective-permute-start.8 = (f32[136,128]{1,0:T(8,128)S(1)}, f32[136,128]{1,0:T(8,128)S(1)}, u32[]{:S(2)}, u32[]{:S(2)}) collective-permute-start(f32[136,128]{1,0:T(8,128)S(1)} %slice_add_fusion), channel_id=1, source_target_pairs={{0,8},{4,12},{8,0},{12,4},{1,9},{5,13},{9,1},{13,5},{2,10},{6,14},... | collective-permute-start | bytes 208904 | tf_op jit(solution)/shard_map/ppermute | solution.py:265
  20.5 4.3 %collective-permute-start.5 = (f32[128,128]{1,0:T(8,128)S(1)}, f32[128,128]{1,0:T(8,128)S(1)}, u32[]{:S(2)}, u32[]{:S(2)}) collective-permute-start(f32[128,128]{1,0:T(8,128)S(1)} %slice_add_fusion.1), channel_id=1, source_target_pairs={{0,4},{4,0},{8,12},{12,8},{1,5},{5,1},{9,13},{13,9},{2,6},{6,2},{1... | collective-permute-start | bytes 196616 | tf_op jit(solution)/shard_map/ppermute | solution.py:265
  22.9 7.5 %collective-permute-start.9 = (f32[136,128]{1,0:T(8,128)S(1)}, f32[136,128]{1,0:T(8,128)S(1)}, u32[]{:S(2)}, u32[]{:S(2)}) collective-permute-start(f32[136,128]{1,0:T(8,128)S(1)} %add.33.refs_2_), channel_id=1, source_target_pairs={{0,4},{4,0},{8,12},{12,8},{1,5},{5,1},{9,13},{13,9},{2,6},{6,2},{1... | collective-permute-start | bytes 208904 | tf_op jit(solution)/shard_map/ppermute | solution.py:265
  24.8 5.6 %collective-permute-start.6 = (f32[128,128]{1,0:T(8,128)S(1)}, f32[128,128]{1,0:T(8,128)S(1)}, u32[]{:S(2)}, u32[]{:S(2)}) collective-permute-start(f32[128,128]{1,0:T(8,128)S(1)} %add.31.refs_0_), channel_id=1, source_target_pairs={{0,8},{4,12},{8,0},{12,4},{1,9},{5,13},{9,1},{13,5},{2,10},{6,14},... | collective-permute-start | bytes 196616 | tf_op jit(solution)/shard_map/ppermute | solution.py:265
  30.7 5.0 %collective-permute-start.10 = (f32[128,256]{1,0:T(8,128)S(1)}, f32[128,256]{1,0:T(8,128)S(1)}, u32[]{:S(2)}, u32[]{:S(2)}) collective-permute-start(f32[128,256]{1,0:T(8,128)S(1)} %get-tuple-element.50.refs_0_), channel_id=1, source_target_pairs={{0,2},{2,0},{1,3},{3,1},{4,6},{6,4},{5,7},{7,5},{8,10},{10,8},{9,1... | collective-permute-start | bytes 393224 | tf_op jit(solution)/shard_map/ppermute | solution.py:265
  32.3 3.9 %collective-permute-start.11 = (f32[128,256]{1,0:T(8,128)S(1)}, f32[128,256]{1,0:T(8,128)S(1)}, u32[]{:S(2)}, u32[]{:S(2)}) collective-permute-start(f32[128,256]{1,0:T(8,128)S(1)} %get-tuple-element.50.refs_0_), channel_id=1, source_target_pairs={{0,1},{1,0},{2,3},{3,2},{4,5},{5,4},{6,7},{7,6},{8,9},{9,8},{10,11... | collective-permute-start | bytes 393224 | tf_op jit(solution)/shard_map/ppermute | solution.py:265
  35.7 1.3 %collective-permute-start.12 = (f32[128,256]{1,0:T(8,128)S(1)}, f32[128,256]{1,0:T(8,128)S(1)}, u32[]{:S(2)}, u32[]{:S(2)}) collective-permute-start(f32[128,256]{1,0:T(8,128)S(1)} %collective-permute-done.10.refs_1_), channel_id=1, source_target_pairs={{0,1},{1,0},{2,3},{3,2},{4,5},{5,4},{6,7},{7,6},{8,9},{9,8},{10,11... | collective-permute-start | bytes 393224 | tf_op jit(solution)/shard_map/ppermute | solution.py:265
  38.2 1.2 %collective-permute-start.13 = (f32[8,128]{1,0:T(8,128)S(1)}, f32[8,128]{1,0:T(8,128)S(1)}, u32[]{:S(2)}, u32[]{:S(2)}) collective-permute-start(f32[8,128]{1,0:T(8,128)S(1)} %get-tuple-element.52), channel_id=1, source_target_pairs={{0,1},{1,0},{2,3},{3,2},{4,5},{5,4},{6,7},{7,6},{8,9},{9,8},{10,11... | collective-permute-start | bytes 12296 | tf_op jit(solution)/shard_map/ppermute | solution.py:265
  39.5 3.0 %collective-permute-start.14 = (f32[8,128]{1,0:T(8,128)S(1)}, f32[8,128]{1,0:T(8,128)S(1)}, u32[]{:S(2)}, u32[]{:S(2)}) collective-permute-start(f32[8,128]{1,0:T(8,128)S(1)} %add.34), channel_id=1, source_target_pairs={{0,3},{1,2},{2,1},{3,0},{4,7},{5,6},{6,5},{7,4},{8,11},{9,10},{10,... | collective-permute-start | bytes 12296 | tf_op jit(solution)/shard_map/ppermute | solution.py:270
  42.5 4.8 %collective-permute-start.17 = (f32[8,128]{1,0:T(8,128)S(1)}, f32[8,128]{1,0:T(8,128)S(1)}, u32[]{:S(2)}, u32[]{:S(2)}) collective-permute-start(f32[8,128]{1,0:T(8,128)S(1)} %add.35.refs_0_), channel_id=1, source_target_pairs={{0,13},{1,12},{4,9},{5,8},{8,5},{9,4},{12,1},{13,0},{2,15},{3,14},... | collective-permute-start | bytes 12296 | tf_op jit(solution)/shard_map/ppermute | solution.py:270
  44.7 3.9 %collective-permute-start.16 = (f32[8,128]{1,0:T(8,128)S(1)}, f32[8,128]{1,0:T(8,128)S(1)}, u32[]{:S(2)}, u32[]{:S(2)}) collective-permute-start(f32[8,128]{1,0:T(8,128)S(1)} %add.35.refs_0_), channel_id=1, source_target_pairs={{0,9},{1,8},{4,13},{5,12},{8,1},{9,0},{12,5},{13,4},{2,11},{3,10},... | collective-permute-start | bytes 12296 | tf_op jit(solution)/shard_map/ppermute | solution.py:270
  45.2 3.4 %collective-permute-start.15 = (f32[8,128]{1,0:T(8,128)S(1)}, f32[8,128]{1,0:T(8,128)S(1)}, u32[]{:S(2)}, u32[]{:S(2)}) collective-permute-start(f32[8,128]{1,0:T(8,128)S(1)} %add.35.refs_0_), channel_id=1, source_target_pairs={{0,5},{1,4},{4,1},{5,0},{8,13},{9,12},{12,9},{13,8},{2,7},{3,6},{6... | collective-permute-start | bytes 12296 | tf_op jit(solution)/shard_map/ppermute | solution.py:270
